TPU v7x, 256 devices: a whole 4x4x8 slice. The times are simulated.
256 devices in a mesh: gx: 64 (over z, x, y_hi), gy: 4 (over y_lo, core).
Axes of the slice: x: 4, y: 4 (y_hi: 2, y_lo: 2; y = y_hi * 2 + y_lo), z: 8, core: 2. Of those that a mesh axis runs over, the one named last changes fastest.
Arguments:
- positions: float32 [3, 32768], P(None, ('gx', 'gy')), may hold values from 0 to 4
- velocities: float32 [3, 32768], P(None, ('gx', 'gy')), may hold values from -3 to 3
- species: int32 [32768], P(('gx', 'gy')), may hold values from 0 to 3
- counts: int32 [32768], P(('gx', 'gy')), may hold values from 3 to 12
- neighbours: int32 [12, 32768], P(None, ('gx', 'gy')), may hold values from 0 to 639
- send_lists: int32 [4, 16384], P(None, ('gx', 'gy')), may hold values from 0 to 127
- inv_mass: float32 [4], replicated, may hold values from 0.5 to 2
- w_rad_one: float32 [4, 8, 256], replicated, may hold values from -2 to 2
- emb_nbr: float32 [4, 4, 256], replicated, may hold values from -4 to 4
- emb_self: float32 [4, 4, 256], replicated, may hold values from -4 to 4
- w_one: float32 [4, 256, 256], replicated, may hold values from -0.375 to 0.375
- w_src: float32 [4, 256, 256], replicated, may hold values from -0.375 to 0.375
- w_dst: float32 [4, 256, 256], replicated, may hold values from -0.375 to 0.375
- w_rad_two: float32 [4, 8, 256], replicated, may hold values from -2 to 2
- w_edge: float32 [4, 256, 256], replicated, may hold values from -0.375 to 0.375
- w_out: float32 [4, 256], replicated, may hold values from -0.375 to 0.375
Outputs:
- new_positions: float32 [3, 32768], P(None, ('gx', 'gy'))
- new_velocities: float32 [3, 32768], P(None, ('gx', 'gy'))
Inputs may be any that keep to these rules, and one draw needn't show every extreme that they name: `neighbours`: entries index a sub-box's extended list: its owned atoms first, then the 8 ghost blocks in the stated order. `counts`: slots at or beyond an atom's count are padding. `send_lists`: an atom may stand in several lists or several times in one.
All inputs are finite; a program needn't handle non-finite values.
Results may differ from a plain program's by a relative error of at most 0.0003.
Values sent between devices are 32-bit elements; how exact they have to be, the bound alone decides.
No kernel may reach another device: no remote copies, remote signals or barrier semaphores. Data moves between devices by JAX's collectives and lax.ppermute only.
A program may use at most 128 MiB of HBM per device.

v0:
```python
import jax
import jax.numpy as jnp
from jax import lax
from jax.sharding import PartitionSpec as P

RADIAL = 8
SPECIES = 4


box_side = 4.0
soft_square = 0.25
centre_step = 0.75
basis_width = 0.75
pool_scale = 0.25
time_step = 0.25
highest = lax.Precision.HIGHEST


def with_halo(shard, sides, width):
    for axis, dim in sides:
        peers, length = (lax.axis_size(axis), shard.shape[dim])
        up = [(i, (i + 1) % peers) for i in range(peers)]
        down = [(j, i) for i, j in up]
        last = lax.slice_in_dim(shard, length - width, length, axis=dim)
        leading = lax.slice_in_dim(shard, 0, width, axis=dim)
        before = lax.ppermute(last, axis, up)
        after = lax.ppermute(leading, axis, down)
        shard = jnp.concatenate([before, shard, after], axis=dim)
    return shard


def shifted(shard, axis, by):
    peers = lax.axis_size(axis)
    return lax.ppermute(shard, axis, [(i, (i + by) % peers) for i in range(peers)])


def radial_basis(distance):
    centres = centre_step * jnp.arange(RADIAL, dtype=jnp.float32)
    scaled = (distance[None, :] - centres[:, None]) / basis_width
    return jnp.exp(-scaled * scaled)


def edge_terms(ext_pos, neighbours, counts):
    slot_count, own_count = neighbours.shape
    flat_index = neighbours.reshape(-1)
    centre_pos = jnp.tile(ext_pos[:, :own_count], (1, slot_count))
    separation = ext_pos[:, flat_index] - centre_pos
    distance = jnp.sqrt(jnp.sum(separation * separation, axis=0) + soft_square)
    live_mask = (
        (jnp.arange(slot_count, dtype=jnp.int32)[:, None] < counts[None, :])
        .astype(jnp.float32)
        .reshape(-1)
    )
    return (radial_basis(distance), live_mask, flat_index)


def first_layer(ext_pos, ext_onehot, neighbours, counts, w_rad_one, emb_nbr, emb_self, w_one):
    slot_count, own_count = neighbours.shape
    radial_terms, live_mask, flat_index = edge_terms(ext_pos, neighbours, counts)
    radial = jnp.einsum("mkl,ke->mle", w_rad_one, radial_terms, precision=highest)
    embedded = jnp.einsum("msl,se->mle", emb_nbr, ext_onehot[:, flat_index], precision=highest)
    members, latent = (radial.shape[0], radial.shape[1])
    pooled = (radial * embedded * live_mask).reshape(members, latent, slot_count, own_count).sum(
        axis=2
    ) * pool_scale
    before = jnp.einsum("mkl,mka->mla", w_one, pooled, precision=highest)
    before = before + jnp.einsum(
        "msl,sa->mla", emb_self, ext_onehot[:, :own_count], precision=highest
    )
    return jax.nn.silu(before)


def second_layer(
    hidden, ghost_feat, ext_pos, neighbours, counts, w_src, w_dst, w_rad_two, w_edge, w_out
):
    slot_count = neighbours.shape[0]
    radial_terms, live_mask, flat_index = edge_terms(ext_pos, neighbours, counts)
    own_feat = jnp.einsum("mkl,mka->mla", w_dst, hidden, precision=highest)
    ext_feat = jnp.concatenate([own_feat, ghost_feat], axis=2)
    centre_feat = jnp.einsum("mkl,mka->mla", w_src, hidden, precision=highest)
    pair = jnp.tile(centre_feat, (1, 1, slot_count)) + ext_feat[:, :, flat_index]
    pair = jax.nn.silu(pair + jnp.einsum("mkl,ke->mle", w_rad_two, radial_terms, precision=highest))
    update = jax.nn.silu(jnp.einsum("mkl,mke->mle", w_edge, pair, precision=highest))
    pair_energy = jnp.einsum("ml,mle->e", w_out, update, precision=highest)
    return jnp.sum(pair_energy * live_mask) / w_out.shape[0]


def share_ghosts(values, send_lists):
    columns = values.shape[0]
    ghosts = send_lists.shape[1]
    outgoing = values[:, send_lists.reshape(-1)].reshape(columns, 2, 2, ghosts)
    padded = with_halo(outgoing, (("gx", 1), ("gy", 2)), 1)
    pieces = [
        padded[:, 0, 1],
        padded[:, 0, 2],
        padded[:, 3, 1],
        padded[:, 3, 2],
        padded[:, 1, 0],
        padded[:, 2, 0],
        padded[:, 1, 3],
        padded[:, 2, 3],
    ]
    return jnp.concatenate(pieces, axis=1)


def return_ghosts(values, send_lists, own_count):
    columns = values.shape[0]
    ghosts = send_lists.shape[1]
    blocks = values.reshape(columns, 8, ghosts)
    gathered = jnp.zeros((columns, 4, ghosts), jnp.float32)
    for direction in (1, -1):
        outgoing = blocks[:, 2:4] if direction == 1 else blocks[:, 0:2]
        arrived = shifted(outgoing, "gx", direction)
        if direction == 1:
            gathered = gathered.at[:, 0:2].add(arrived)
        else:
            gathered = gathered.at[:, 2:4].add(arrived)
    for direction in (1, -1):
        outgoing = blocks[:, 6:8] if direction == 1 else blocks[:, 4:6]
        arrived = shifted(outgoing, "gy", direction)
        if direction == 1:
            gathered = gathered.at[:, 0::2].add(arrived)
        else:
            gathered = gathered.at[:, 1::2].add(arrived)
    onehot = (
        send_lists.reshape(-1)[:, None] == jnp.arange(own_count, dtype=jnp.int32)[None, :]
    ).astype(jnp.float32)
    return jnp.dot(gathered.reshape(columns, 4 * ghosts), onehot, precision=highest)


def shards(
    positions,
    velocities,
    species,
    counts,
    neighbours,
    send_lists,
    inv_mass,
    w_rad_one,
    emb_nbr,
    emb_self,
    w_one,
    w_src,
    w_dst,
    w_rad_two,
    w_edge,
    w_out,
):
    own_count = positions.shape[1]
    ghosts = send_lists.shape[1]
    members, latent = (w_one.shape[0], w_one.shape[1])
    species_row = species.astype(jnp.float32)
    ghost_rows = share_ghosts(
        jnp.concatenate([positions, species_row[None, :]], axis=0), send_lists
    )
    sign_x = jnp.array([-1.0, -1.0, 1.0, 1.0, 0.0, 0.0, 0.0, 0.0], dtype=jnp.float32)
    sign_y = jnp.array([0.0, 0.0, 0.0, 0.0, -1.0, -1.0, 1.0, 1.0], dtype=jnp.float32)
    offsets = box_side * jnp.stack(
        [jnp.repeat(sign_x, ghosts), jnp.repeat(sign_y, ghosts), jnp.zeros(8 * ghosts, jnp.float32)]
    )
    ext_pos = jnp.concatenate([positions, ghost_rows[:3] + offsets], axis=1)
    ext_species = jnp.concatenate([species_row, ghost_rows[3]])
    ext_onehot = (ext_species[None, :] == jnp.arange(SPECIES, dtype=jnp.float32)[:, None]).astype(
        jnp.float32
    )

    def layer_one(place):
        return first_layer(
            place, ext_onehot, neighbours, counts, w_rad_one, emb_nbr, emb_self, w_one
        )

    hidden, pull_one = jax.vjp(layer_one, ext_pos)
    ghost_pay = share_ghosts(hidden.reshape(members * latent, own_count), send_lists).reshape(
        members, latent, 8 * ghosts
    )

    def layer_two(hid, place, ghost_in):
        ghost_feat = jnp.einsum("mkl,mka->mla", w_dst, ghost_in, precision=highest)
        return second_layer(
            hid, ghost_feat, place, neighbours, counts, w_src, w_dst, w_rad_two, w_edge, w_out
        )

    energy, pull_two = jax.vjp(layer_two, hidden, ext_pos, ghost_pay)
    ct_hidden, ct_place, ct_ghost = pull_two(jnp.ones((), jnp.float32))
    returned = return_ghosts(
        ct_ghost.reshape(members * latent, 8 * ghosts), send_lists, own_count
    ).reshape(members, latent, own_count)
    ct_hidden = ct_hidden + returned
    ct_first = pull_one(ct_hidden)[0]
    ct_total = ct_place + ct_first
    back_terms = return_ghosts(ct_total[:, own_count:], send_lists, own_count)
    forces = -(ct_total[:, :own_count] + back_terms)
    own_onehot = (species[None, :] == jnp.arange(SPECIES, dtype=jnp.int32)[:, None]).astype(
        jnp.float32
    )
    inv_scale = jnp.sum(own_onehot * inv_mass[:, None], axis=0)
    new_velocities = velocities + time_step * inv_scale[None, :] * forces
    new_positions = positions + time_step * new_velocities
    return (new_positions, new_velocities)


def solution(mesh):
    placed = (
        P(None, ("gx", "gy")),
        P(None, ("gx", "gy")),
        P(("gx", "gy")),
        P(("gx", "gy")),
        P(None, ("gx", "gy")),
        P(None, ("gx", "gy")),
        P(),
        P(),
        P(),
        P(),
        P(),
        P(),
        P(),
        P(),
        P(),
        P(),
    )
    return jax.shard_map(
        shards,
        mesh=mesh,
        in_specs=placed,
        out_specs=(P(None, ("gx", "gy")), P(None, ("gx", "gy"))),
        check_vma=False,
    )
```

profile of v0, /device:TPU:0, one launch (start us, length us, event | category | flops | bytes accessed | tf_op | source)
XLA Modules:
  0.0 466.3 jit_solution(6567128750588078418)
XLA Ops:
  3.8 1.5 collective-permute-start
  5.4 7.6 %collective-permute-start.1 = (f32[4,1,2,64]{3,1,2,0:T(1,128)S(1)}, f32[4,1,2,64]{3,1,2,0:T(1,128)S(1)}, u32[]{:S(2)}, u32[]{:S(2)}) collective-permute-start(f32[4,1,2,64]{3,1,2,0:T(1,128)S(1)} %get-tuple-element.82), channel_id=1, source_target_pairs={{4,0},{8,4},{12,8},{16,12},{20,16},{24,20},{28,24},{32,28},{36,32}... | collective-permute-start | bytes 6152 | tf_op jit(solution)/shard_map/ppermute | solution.py:27
  14.1 1.3 select_bitcast_fusion
  16.7 1.3 select_reduce_fusion
  19.4 1.3 eq.26
  22.5 2.2 collective-permute-start.3
  28.6 2.6 gather_fusion.1
  31.2 2.9 gather_fusion.2
  34.4 3.4 fusion.42
  37.8 7.7 %fusion.10 = f32[4,256,1536]{1,2,0:T(8,128)} fusion(f32[1536,4,256]{2,0,1:T(8,128)S(1)} %fusion.42, f32[4,8,256]{2,1,0:T(8,128)S(1)} %copy-done.13, f32[1536]{0:T(1024)S(1)} %convert_bitcast_fusion, f32[8]{0:T(128)S(1)} %copy-done.23, f32[1536]{0:T(1024)S(1)} %add_sqrt_fusion), kind=kOutput, calls=%fused_computation.31 | convolution fusion | flops 154189824 | bytes 12628000 | tf_op jit(solution)/shard_map/jvp(mkl,ke->mle)/dot_general | solution.py:60
  45.5 4.1 reduce_sum.72
  49.6 3.0 fusion.51
  53.6 1.3 copy.122
  55.0 2.2 gather_fusion.3
  57.1 1.4 fusion.94
  58.6 7.9 %collective-permute-start.5 = (f32[1024,1,2,64]{0,3,2,1:T(8,128)S(1)}, f32[1024,1,2,64]{0,3,2,1:T(8,128)S(1)}, u32[]{:S(2)}, u32[]{:S(2)}) collective-permute-start(f32[1024,1,2,64]{0,3,2,1:T(8,128)S(1)} %get-tuple-element.62), channel_id=1, source_target_pairs={{4,0},{8,4},{12,8},{16,12},{20,16},{24,20},{28,24},{32,28},{36,32}... | collective-permute-start | bytes 1572872 | tf_op jit(solution)/shard_map/ppermute | solution.py:27
  66.5 2.7 convolution_bitcast_fusion.3
  69.2 3.0 convolution_bitcast_fusion.4
  72.2 9.1 %collective-permute-done.4 = f32[1024,1,2,64]{0,3,2,1:T(8,128)S(1)} collective-permute-done((f32[1024,1,2,64]{0,3,2,1:T(8,128)S(1)}, f32[1024,1,2,64]{0,3,2,1:T(8,128)S(1)}, u32[]{:S(2)}, u32[]{:S(2)}) %collective-permute-start.4) | collective-permute-done | bytes 524320 | tf_op jit(solution)/shard_map/ppermute | solution.py:26
  81.3 4.9 %collective-permute-done.5 = f32[1024,1,2,64]{0,3,2,1:T(8,128)S(1)} collective-permute-done((f32[1024,1,2,64]{0,3,2,1:T(8,128)S(1)}, f32[1024,1,2,64]{0,3,2,1:T(8,128)S(1)}, u32[]{:S(2)}, u32[]{:S(2)}) %collective-permute-start.5) | collective-permute-done | bytes 524320 | tf_op jit(solution)/shard_map/ppermute | solution.py:27
  86.4 1.4 fusion.91
  87.9 1.7 collective-permute-start.7
  94.3 1.8 concatenate.59
  97.5 1.7 copy_dynamic-update-slice_fusion.4
  99.3 13.6 %collective-permute-done.6 = f32[1024,4,1,64]{0,3,2,1:T(8,128)} collective-permute-done((f32[1024,4,1,64]{0,3,2,1:T(8,128)}, f32[1024,4,1,64]{0,3,2,1:T(8,128)}, u32[]{:S(2)}, u32[]{:S(2)}) %collective-permute-start.6) | collective-permute-done | bytes 1048608 | tf_op jit(solution)/shard_map/ppermute | solution.py:26
  112.9 1.8 fusion.93
  115.9 1.9 fusion.92
  117.7 1.8 concatenate.63
  119.5 1.8 concatenate.64
  122.8 1.7 copy_dynamic-update-slice_fusion.1
  124.6 1.7 copy_dynamic-update-slice_fusion
  126.3 3.6 convolution_bitcast_fusion.2
  130.1 3.2 copy.131
  133.3 10.7 %gather_fusion.4 = f32[1536,4,256]{2,1,0:T(4,128)} fusion(f32[4,256,640]{1,0,2:T(4,128)} %copy.131, s32[2048]{0:T(1024)S(1)} %pad_clamp_fusion), kind=kCustom, calls=%fused_computation.4 | custom fusion | bytes 12589056 | tf_op jit(solution)/shard_map/jvp()/gather | solution.py:81
  144.0 9.4 %bitcast_add_fusion = f32[4,256,1536]{1,2,0:T(8,128)S(1)} fusion(f32[1536,4,256]{2,1,0:T(4,128)} %gather_fusion.4, f32[4,8,256]{2,1,0:T(8,128)S(1)} %copy-done.12, f32[4,256,128]{1,2,0:T(8,128)S(1)} %copy-done.10, f32[8]{0:T(128)} %iota_multiply_fusion.1, f32[1536]{0:T(1024)S(1)} %add_sqrt_fusion), kind=kOutput, calls=%fused_computation.28 | convolution fusion | flops 154189824 | bytes 13146144 | tf_op jit(solution)/shard_map/jvp(mkl,ke->mle)/dot_general | solution.py:82
  153.4 7.4 %fusion.13 = f32[4,1536,256]{2,1,0:T(8,128)S(1)} fusion(f32[4,256,256]{2,1,0:T(8,128)S(1)} %copy-done, f32[4,256,1536]{1,2,0:T(8,128)S(1)} %bitcast_add_fusion), kind=kOutput, calls=%fused_computation.34 | convolution fusion | flops 4838129664 | bytes 13631488 | tf_op jit(solution)/shard_map/jvp(mkl,mke->mle)/dot_general | solution.py:83
  160.9 10.6 %fusion.5 = f32[4,256,1536]{1,2,0:T(8,128)S(1)} fusion(f32[4,256,1536]{1,2,0:T(8,128)S(1)} %bitcast_add_fusion, f32[4,256,256]{2,1,0:T(8,128)S(1)} %copy-done, f32[4,1536,256]{2,1,0:T(8,128)S(1)} %fusion.13, f32[4,256]{1,0:T(4,128)S(1)} %copy-done.32, f32[1536]{0:T(1024)S(1)} %copy-done.26), kind=kOutput, calls=%fused_computation.18 | convolution fusion | flops 4861722624 | bytes 19933184 | tf_op jit(solution)/shard_map/transpose(jvp(mkl,mke->mle))/dot_general | solution.py:83
  171.4 11.8 %copy.134 = f32[1536,4,256]{2,1,0:T(4,128)} copy(f32[1536,4,256]{2,0,1:T(8,128)S(1)} %bitcast.225) | data formatting | bytes 12582912 | tf_op jit(solution)/shard_map/transpose(jvp(jit(silu)))/add_any | solution.py:82
  183.2 1.9 broadcast_in_dim.29
  185.1 170.2 %scatter_fusion = f32[4,256,640]{1,0,2:T(4,128)} fusion(f32[4,256,640]{1,0,2:T(4,128)} %broadcast_in_dim.29, s32[1536]{0:T(1024)S(1)} %copy-done.17, f32[1536,4,256]{2,1,0:T(4,128)} %copy.134), kind=kCustom, calls=%fused_computation.6 | custom fusion | flops 1572864 | bytes 18880512 | tf_op jit(solution)/shard_map/transpose(jvp())/scatter-add | solution.py:81
  356.4 3.3 split.9
  359.6 3.3 reduce_sum.89
  362.9 2.4 fusion.105
  365.3 3.8 fusion.26
  369.1 2.7 copy.137
  371.7 3.3 reshape_reshape.3
  375.0 2.5 fusion.90
  377.6 2.1 collective-permute-start.9
  379.7 1.4 collective-permute-start.8
  381.1 1.7 collective-permute-start.11
  382.8 2.0 fusion.30
  384.9 8.7 %fusion.64 = f32[1536]{0:T(1024)} fusion(f32[4,256,1536]{1,2,0:T(8,128)} %copy-done.3, f32[4,8,256]{2,1,0:T(8,128)S(1)} %copy-done.12, f32[8]{0:T(128)S(1)} %copy-done.24, f32[1536]{0:T(1024)S(1)} %add_sqrt_fusion), kind=kOutput, calls=%fused_computation.113 | convolution fusion | flops 151128576 | bytes 6336544 | tf_op jit(solution)/shard_map/transpose(jvp(mkl,ke->mle))/dot_general | solution.py:82
  393.6 11.6 %collective-permute-done.9 = f32[1024,2,64]{0,2,1:T(8,128)S(1)} collective-permute-done((f32[1024,2,64]{0,2,1:T(8,128)S(1)}, f32[1024,2,64]{0,2,1:T(8,128)S(1)}, u32[]{:S(2)}, u32[]{:S(2)}) %collective-permute-start.9) | collective-permute-done | bytes 524320 | tf_op jit(solution)/shard_map/ppermute | solution.py:34
  405.3 5.2 %collective-permute-done.10 = f32[1024,2,64]{0,2,1:T(8,128)S(1)} collective-permute-done((f32[1024,2,64]{0,2,1:T(8,128)S(1)}, f32[1024,2,64]{0,2,1:T(8,128)S(1)}, u32[]{:S(2)}, u32[]{:S(2)}) %collective-permute-start.10) | collective-permute-done | bytes 524320 | tf_op jit(solution)/shard_map/ppermute | solution.py:34
  411.3 2.5 scatter_fusion.1
  413.8 1.8 scatter_fusion.2
  416.8 2.7 fusion.29
  419.5 3.9 fusion.6
  423.5 5.4 %fusion.67 = f32[1536]{0:T(1024)S(1)} fusion(f32[4,256,1536]{1,2,0:T(8,128)S(1)} %fusion.6, f32[4,8,256]{2,1,0:T(8,128)S(1)} %copy-done.13, f32[8]{0:T(128)S(1)} %copy-done.25, f32[1536]{0:T(1024)S(1)} %add_sqrt_fusion), kind=kOutput, calls=%fused_computation.116 | convolution fusion | flops 151128576 | bytes 6336544 | tf_op jit(solution)/shard_map/transpose(jvp(mkl,ke->mle))/dot_general | solution.py:60
  429.6 9.7 %scatter_custom_fusion = f32[3,640]{0,1:T(8,128)S(1)} fusion(f32[3,640]{0,1:T(8,128)S(1)} %pad.16, s32[1536]{0:T(1024)S(1)} %copy-done.17, f32[3,1536]{0,1:T(8,128)S(1)} %get-tuple-element.64, f32[1536]{0:T(1024)S(1)} %get-tuple-element.76), kind=kCustom, calls=%fused_computation.70 | custom fusion | flops 9216 | bytes 802304 | tf_op jit(solution)/shard_map/transpose(jvp())/scatter-add | solution.py:47
  439.4 9.8 %scatter_custom_fusion.4 = f32[3,640]{0,1:T(8,128)S(1)} fusion(f32[3,640]{0,1:T(8,128)S(1)} %pad.17, s32[1536]{0:T(1024)S(1)} %copy-done.17, f32[3,1536]{0,1:T(8,128)S(1)} %get-tuple-element.64, f32[1536]{0:T(1024)S(1)} %get-tuple-element.77), kind=kCustom, calls=%fused_computation.68 | custom fusion | flops 9216 | bytes 802304 | tf_op jit(solution)/shard_map/transpose(jvp())/scatter-add | solution.py:47
  449.5 5.0 %collective-permute-start.13 = (f32[3,2,64]{2,0,1:T(4,128)S(1)}, f32[3,2,64]{2,0,1:T(4,128)S(1)}, u32[]{:S(2)}, u32[]{:S(2)}) collective-permute-start(f32[3,2,64]{2,0,1:T(4,128)S(1)} %copy.156), channel_id=1, source_target_pairs={{0,252},{4,0},{8,4},{12,8},{16,12},{20,16},{24,20},{28,24},{32,28}... | collective-permute-start | bytes 4616 | tf_op jit(solution)/shard_map/ppermute | solution.py:34
  454.7 1.7 collective-permute-start.15
  456.4 7.5 %collective-permute-done.12 = f32[3,2,64]{2,0,1:T(4,128)S(1)} collective-permute-done((f32[3,2,64]{2,0,1:T(4,128)S(1)}, f32[3,2,64]{2,0,1:T(4,128)S(1)}, u32[]{:S(2)}, u32[]{:S(2)}) %collective-permute-start.12) | collective-permute-done | bytes 1568 | tf_op jit(solution)/shard_map/ppermute | solution.py:34
  (166 shorter events, 29.6 us)
Async XLA Ops:
  0.6 152.8 %copy-start = (f32[4,256,256]{2,1,0:T(8,128)S(1)}, f32[4,256,256]{2,1,0:T(8,128)}, u32[]{:S(2)}) copy-start(f32[4,256,256]{2,1,0:T(8,128)} %param.40) | copy-start | bytes 3145732
  0.6 37.1 %copy-start.13 = (f32[4,8,256]{2,1,0:T(8,128)S(1)}, f32[4,8,256]{2,1,0:T(8,128)}, u32[]{:S(2)}) copy-start(f32[4,8,256]{2,1,0:T(8,128)} %param.33) | copy-start | bytes 98308
  3.0 24.4 %copy-start.22 = (s32[1024]{0:T(1024)}, s32[1024]{0:T(1024)S(1)}, u32[]{:S(2)}) copy-start(s32[1024]{0:T(1024)S(1)} %pad_clamp_fusion.1) | copy-start | bytes 12292
  3.8 18.5 %collective-permute-start = (f32[4,1,2,64]{3,1,2,0:T(1,128)S(1)}, f32[4,1,2,64]{3,1,2,0:T(1,128)S(1)}, u32[]{:S(2)}, u32[]{:S(2)}) collective-permute-start(f32[4,1,2,64]{3,1,2,0:T(1,128)S(1)} %get-tuple-element.83), channel_id=1, source_target_pairs={{0,4},{4,8},{8,12},{12,16},{16,20},{20,24},{24,28},{28,32},{32,36}... | collective-permute-start | bytes 6152 | tf_op jit(solution)/shard_map/ppermute | solution.py:26
  5.4 17.0 %collective-permute-start.1 = (f32[4,1,2,64]{3,1,2,0:T(1,128)S(1)}, f32[4,1,2,64]{3,1,2,0:T(1,128)S(1)}, u32[]{:S(2)}, u32[]{:S(2)}) collective-permute-start(f32[4,1,2,64]{3,1,2,0:T(1,128)S(1)} %get-tuple-element.82), channel_id=1, source_target_pairs={{4,0},{8,4},{12,8},{16,12},{20,16},{24,20},{28,24},{32,28},{36,32}... | collective-permute-start | bytes 6152 | tf_op jit(solution)/shard_map/ppermute | solution.py:27
  14.1 31.4 %copy-start.18 = (f32[1536]{0:T(1024)}, f32[1536]{0:T(1024)S(1)}, u32[]{:S(2)}) copy-start(f32[1536]{0:T(1024)S(1)} %convert_bitcast_fusion) | copy-start | bytes 18436
  16.7 1.3 copy-start.16
  22.4 15.4 %copy-start.23 = (f32[8]{0:T(128)S(1)}, f32[8]{0:T(128)}, u32[]{:S(2)}) copy-start(f32[8]{0:T(128)} %iota_multiply_fusion.1) | copy-start | bytes 100
  22.4 3.2 collective-permute-start.2
  22.5 3.6 collective-permute-start.3
  31.2 14.3 %copy-start.6 = (f32[1536,3]{1,0:T(8,128)}, f32[1536,3]{1,0:T(8,128)S(1)}, u32[]{:S(2)}) copy-start(f32[1536,3]{1,0:T(8,128)S(1)} %gather_fusion.1) | copy-start | bytes 55300
  34.4 11.1 %copy-start.14 = (f32[1536]{0:T(1024)}, f32[1536]{0:T(1024)S(1)}, u32[]{:S(2)}) copy-start(f32[1536]{0:T(1024)S(1)} %get-tuple-element.65) | copy-start | bytes 18436
  37.8 7.7 %copy-start.2 = (f32[1536,4,256]{2,0,1:T(8,128)}, f32[1536,4,256]{2,0,1:T(8,128)S(1)}, u32[]{:S(2)}) copy-start(f32[1536,4,256]{2,0,1:T(8,128)S(1)} %fusion.42) | copy-start | bytes 18874372
  53.6 12.8 %copy-start.4 = (f32[4,256,256]{2,1,0:T(8,128)S(1)}, f32[4,256,256]{2,1,0:T(8,128)}, u32[]{:S(2)}) copy-start(f32[4,256,256]{2,1,0:T(8,128)} %param.38) | copy-start | bytes 3145732
  57.1 29.1 %copy-start.5 = (f32[256,1024]{1,0:T(8,128)S(1)}, f32[256,1024]{1,0:T(8,128)}, u32[]{:S(2)}) copy-start(f32[256,1024]{1,0:T(8,128)} %gather_fusion.3) | copy-start | bytes 3145732
  58.5 22.8 %collective-permute-start.4 = (f32[1024,1,2,64]{0,3,2,1:T(8,128)S(1)}, f32[1024,1,2,64]{0,3,2,1:T(8,128)S(1)}, u32[]{:S(2)}, u32[]{:S(2)}) collective-permute-start(f32[1024,1,2,64]{0,3,2,1:T(8,128)S(1)} %get-tuple-element.63), channel_id=1, source_target_pairs={{0,4},{4,8},{8,12},{12,16},{16,20},{20,24},{24,28},{28,32},{32,36}... | collective-permute-start | bytes 1572872 | tf_op jit(solution)/shard_map/ppermute | solution.py:26
  58.6 27.6 %collective-permute-start.5 = (f32[1024,1,2,64]{0,3,2,1:T(8,128)S(1)}, f32[1024,1,2,64]{0,3,2,1:T(8,128)S(1)}, u32[]{:S(2)}, u32[]{:S(2)}) collective-permute-start(f32[1024,1,2,64]{0,3,2,1:T(8,128)S(1)} %get-tuple-element.62), channel_id=1, source_target_pairs={{4,0},{8,4},{12,8},{16,12},{20,16},{24,20},{28,24},{32,28},{36,32}... | collective-permute-start | bytes 1572872 | tf_op jit(solution)/shard_map/ppermute | solution.py:27
  87.9 25.0 %collective-permute-start.6 = (f32[1024,4,1,64]{0,3,2,1:T(8,128)}, f32[1024,4,1,64]{0,3,2,1:T(8,128)}, u32[]{:S(2)}, u32[]{:S(2)}) collective-permute-start(f32[1024,4,1,64]{0,3,2,1:T(8,128)} %get-tuple-element.57), channel_id=1, source_target_pairs={{0,1},{1,2},{2,3},{3,0},{4,5},{5,6},{6,7},{7,4},{8,9},{9,10},{10,1... | collective-permute-start | bytes 3145736 | tf_op jit(solution)/shard_map/ppermute | solution.py:26
  87.9 28.0 %collective-permute-start.7 = (f32[1024,4,1,64]{0,3,2,1:T(8,128)}, f32[1024,4,1,64]{0,3,2,1:T(8,128)}, u32[]{:S(2)}, u32[]{:S(2)}) collective-permute-start(f32[1024,4,1,64]{0,3,2,1:T(8,128)} %get-tuple-element.56), channel_id=1, source_target_pairs={{1,0},{2,1},{3,2},{0,3},{5,4},{6,5},{7,6},{4,7},{9,8},{10,9},{11,1... | collective-permute-start | bytes 3145736 | tf_op jit(solution)/shard_map/ppermute | solution.py:27
  121.3 8.6 %copy-start.11 = (f32[4,256,128]{1,2,0:T(8,128)S(1)}, f32[4,256,128]{1,2,0:T(8,128)}, u32[]{:S(2)}) copy-start(f32[4,256,128]{1,2,0:T(8,128)} %convolution_bitcast_fusion.3) | copy-start | bytes 1572868
  133.3 10.7 %copy-start.10 = (f32[4,256,128]{1,2,0:T(8,128)S(1)}, f32[4,256,128]{1,2,0:T(8,128)}, u32[]{:S(2)}) copy-start(f32[4,256,128]{1,2,0:T(8,128)} %convolution_bitcast_fusion.4) | copy-start | bytes 1572868
  133.3 10.7 %copy-start.12 = (f32[4,8,256]{2,1,0:T(8,128)S(1)}, f32[4,8,256]{2,1,0:T(8,128)}, u32[]{:S(2)}) copy-start(f32[4,8,256]{2,1,0:T(8,128)} %param.39) | copy-start | bytes 98308
  153.4 7.4 %copy-start.26 = (f32[1536]{0:T(1024)S(1)}, f32[1536]{0:T(1024)}, u32[]{:S(2)}) copy-start(f32[1536]{0:T(1024)} %select_bitcast_fusion) | copy-start | bytes 18436
  153.4 7.4 %copy-start.32 = (f32[4,256]{1,0:T(4,128)S(1)}, f32[4,256]{1,0:T(4,128)}, u32[]{:S(2)}) copy-start(f32[4,256]{1,0:T(4,128)} %param.41) | copy-start | bytes 12292
  171.4 11.8 %copy-start.3 = (f32[4,256,1536]{1,2,0:T(8,128)}, f32[4,256,1536]{1,2,0:T(8,128)S(1)}, u32[]{:S(2)}) copy-start(f32[4,256,1536]{1,2,0:T(8,128)S(1)} %fusion.5) | copy-start | bytes 18874372
  171.4 13.7 %copy-start.17 = (s32[1536]{0:T(1024)S(1)}, s32[1536]{0:T(1024)}, u32[]{:S(2)}) copy-start(s32[1536]{0:T(1024)} %copy-done.16) | copy-start | bytes 18436
  375.0 9.8 %copy-start.24 = (f32[8]{0:T(128)S(1)}, f32[8]{0:T(128)}, u32[]{:S(2)}) copy-start(f32[8]{0:T(128)} %iota_multiply_fusion.1) | copy-start | bytes 100
  377.6 27.6 %collective-permute-start.9 = (f32[1024,2,64]{0,2,1:T(8,128)S(1)}, f32[1024,2,64]{0,2,1:T(8,128)S(1)}, u32[]{:S(2)}, u32[]{:S(2)}) collective-permute-start(f32[1024,2,64]{0,2,1:T(8,128)S(1)} %get-tuple-element.54), channel_id=1, source_target_pairs={{0,252},{4,0},{8,4},{12,8},{16,12},{20,16},{24,20},{28,24},{32,28}... | collective-permute-start | bytes 1572872 | tf_op jit(solution)/shard_map/ppermute | solution.py:34
  379.7 25.5 %collective-permute-start.8 = (f32[1024,2,64]{0,2,1:T(8,128)S(1)}, f32[1024,2,64]{0,2,1:T(8,128)S(1)}, u32[]{:S(2)}, u32[]{:S(2)}) collective-permute-start(f32[1024,2,64]{0,2,1:T(8,128)S(1)} %get-tuple-element.55), channel_id=1, source_target_pairs={{0,4},{4,8},{8,12},{12,16},{16,20},{20,24},{24,28},{28,32},{32,36}... | collective-permute-start | bytes 1572872 | tf_op jit(solution)/shard_map/ppermute | solution.py:34
  381.1 29.4 %collective-permute-start.10 = (f32[1024,2,64]{0,2,1:T(8,128)S(1)}, f32[1024,2,64]{0,2,1:T(8,128)S(1)}, u32[]{:S(2)}, u32[]{:S(2)}) collective-permute-start(f32[1024,2,64]{0,2,1:T(8,128)S(1)} %get-tuple-element.53), channel_id=1, source_target_pairs={{0,1},{1,2},{2,3},{3,0},{4,5},{5,6},{6,7},{7,4},{8,9},{9,10},{10,1... | collective-permute-start | bytes 1572872 | tf_op jit(solution)/shard_map/ppermute | solution.py:34
  381.1 32.7 %collective-permute-start.11 = (f32[1024,2,64]{0,2,1:T(8,128)}, f32[1024,2,64]{0,2,1:T(8,128)}, u32[]{:S(2)}, u32[]{:S(2)}) collective-permute-start(f32[1024,2,64]{0,2,1:T(8,128)} %get-tuple-element.52), channel_id=1, source_target_pairs={{0,3},{1,0},{2,1},{3,2},{4,7},{5,4},{6,5},{7,6},{8,11},{9,8},{10,9... | collective-permute-start | bytes 1572872 | tf_op jit(solution)/shard_map/ppermute | solution.py:34
  384.9 28.9 %copy-start.29 = (s32[2]{0:T(128)S(1)}, s32[2]{0:T(128)}, u32[]{:S(2)}) copy-start(s32[2]{0:T(128)} %add_bitcast_fusion) | copy-start | bytes 28
  393.6 22.5 %copy-start.8 = (f32[4,256,128]{1,2,0:T(8,128)S(1)}, f32[4,256,128]{1,2,0:T(8,128)}, u32[]{:S(2)}) copy-start(f32[4,256,128]{1,2,0:T(8,128)} %fusion.30) | copy-start | bytes 1572868
  393.6 22.5 %copy-start.27 = (s32[256]{0:T(256)S(1)}, s32[256]{0:T(256)}, u32[]{:S(2)}) copy-start(s32[256]{0:T(256)} %eq.26) | copy-start | bytes 3076
  410.5 0.8 copy-start.9
  411.3 8.2 %copy-start.19 = (f32[1536]{0:T(1024)S(1)}, f32[1536]{0:T(1024)}, u32[]{:S(2)}) copy-start(f32[1536]{0:T(1024)} %copy-done.18) | copy-start | bytes 18436
  419.5 4.0 copy-start.25
  419.5 46.6 %copy-start.1 = (f32[4,256,256]{2,1,0:T(8,128)S(1)}, f32[4,256,256]{2,1,0:T(8,128)}, u32[]{:S(2)}) copy-start(f32[4,256,256]{2,1,0:T(8,128)} %param.40) | copy-start | bytes 3145732
  423.5 5.5 %copy-start.15 = (f32[1536]{0:T(1024)S(1)}, f32[1536]{0:T(1024)}, u32[]{:S(2)}) copy-start(f32[1536]{0:T(1024)} %copy-done.14) | copy-start | bytes 18436
  423.5 5.5 %copy-start.20 = (f32[1536]{0:T(1024)S(1)}, f32[1536]{0:T(1024)}, u32[]{:S(2)}) copy-start(f32[1536]{0:T(1024)} %fusion.64) | copy-start | bytes 18436
  423.5 5.6 %copy-start.7 = (f32[1536,3]{1,0:T(8,128)S(1)}, f32[1536,3]{1,0:T(8,128)}, u32[]{:S(2)}) copy-start(f32[1536,3]{1,0:T(8,128)} %copy-done.6) | copy-start | bytes 55300
  423.5 31.1 %copy-start.34 = (f32[128]{0:T(128)S(1)}, f32[128]{0:T(128)}, u32[]{:S(2)}) copy-start(f32[128]{0:T(128)} %select_reduce_fusion) | copy-start | bytes 1540
  423.5 40.4 %copy-start.31 = (s32[2]{0:T(128)S(1)}, s32[2]{0:T(128)}, u32[]{:S(2)}) copy-start(s32[2]{0:T(128)} %fusion.81) | copy-start | bytes 28
  423.5 41.0 %copy-start.30 = (s32[2]{0:T(128)S(1)}, s32[2]{0:T(128)}, u32[]{:S(2)}) copy-start(s32[2]{0:T(128)} %add_bitcast_fusion) | copy-start | bytes 28
  423.5 41.7 %copy-start.21 = (f32[3,128]{1,0:T(4,128)S(1)}, f32[3,128]{1,0:T(4,128)}, u32[]{:S(2)}) copy-start(f32[3,128]{1,0:T(4,128)} %param.26) | copy-start | bytes 4612
  423.5 41.7 %copy-start.28 = (s32[256]{0:T(256)S(1)}, s32[256]{0:T(256)}, u32[]{:S(2)}) copy-start(s32[256]{0:T(256)} %eq.26) | copy-start | bytes 3076
  423.5 41.7 %copy-start.33 = (f32[3,128]{1,0:T(4,128)S(1)}, f32[3,128]{1,0:T(4,128)}, u32[]{:S(2)}) copy-start(f32[3,128]{1,0:T(4,128)} %param.27) | copy-start | bytes 4612
  449.5 6.9 %collective-permute-start.13 = (f32[3,2,64]{2,0,1:T(4,128)S(1)}, f32[3,2,64]{2,0,1:T(4,128)S(1)}, u32[]{:S(2)}, u32[]{:S(2)}) collective-permute-start(f32[3,2,64]{2,0,1:T(4,128)S(1)} %copy.156), channel_id=1, source_target_pairs={{0,252},{4,0},{8,4},{12,8},{16,12},{20,16},{24,20},{28,24},{32,28}... | collective-permute-start | bytes 4616 | tf_op jit(solution)/shard_map/ppermute | solution.py:34
  454.5 9.3 %collective-permute-start.12 = (f32[3,2,64]{2,0,1:T(4,128)S(1)}, f32[3,2,64]{2,0,1:T(4,128)S(1)}, u32[]{:S(2)}, u32[]{:S(2)}) collective-permute-start(f32[3,2,64]{2,0,1:T(4,128)S(1)} %copy.155), channel_id=1, source_target_pairs={{0,4},{4,8},{8,12},{12,16},{16,20},{20,24},{24,28},{28,32},{32,36}... | collective-permute-start | bytes 4616 | tf_op jit(solution)/shard_map/ppermute | solution.py:34
  454.6 9.3 %collective-permute-start.14 = (f32[3,2,64]{2,0,1:T(4,128)S(1)}, f32[3,2,64]{2,0,1:T(4,128)S(1)}, u32[]{:S(2)}, u32[]{:S(2)}) collective-permute-start(f32[3,2,64]{2,0,1:T(4,128)S(1)} %copy.157), channel_id=1, source_target_pairs={{0,1},{1,2},{2,3},{3,0},{4,5},{5,6},{6,7},{7,4},{8,9},{9,10},{10,1... | collective-permute-start | bytes 4616 | tf_op jit(solution)/shard_map/ppermute | solution.py:34
  454.7 9.8 %collective-permute-start.15 = (f32[3,2,64]{2,0,1:T(4,128)S(1)}, f32[3,2,64]{2,0,1:T(4,128)S(1)}, u32[]{:S(2)}, u32[]{:S(2)}) collective-permute-start(f32[3,2,64]{2,0,1:T(4,128)S(1)} %copy.158), channel_id=1, source_target_pairs={{0,3},{1,0},{2,1},{3,2},{4,7},{5,4},{6,5},{7,6},{8,11},{9,8},{10,9... | collective-permute-start | bytes 4616 | tf_op jit(solution)/shard_map/ppermute | solution.py:34
where the time goes:
time: 475 us; the launch traced here: 466 us
  other arithmetic  216 us (45%)
  local copies, waits for them, and re-layouts  84.2 us (18%)
  matrix products  78.5 us (17%)
  waiting for transfers between devices  53.2 us (11%)
  starting transfers between devices  33.2 us (7%)
    scatter-add x1, other arithmetic, second_layer(): ext_feat[:, :, flat_index]  170 us
    ppermute x8, waiting for transfers between devices, shifted(): lax.ppermute(shard, axis, [(i, (i + by) % peers) for i in range(peers)])  24.3 us
    ppermute x4, waiting for transfers between devices, with_halo(): before = lax.ppermute(last, axis, up)  23.5 us
    scatter-add x2, other arithmetic, edge_terms(): separation = ext_pos[:, flat_index] - centre_pos  19.5 us
    ppermute x4, starting transfers between devices, with_halo(): after = lax.ppermute(leading, axis, down)  19.4 us
    dot_general x2, matrix products, second_layer(): jnp.einsum('mkl,ke->mle', w_rad_two, radial_terms, precision=highest)  18.1 us
    dot_general x2, matrix products, second_layer(): jnp.einsum('mkl,mke->mle', w_edge, pair, precision=highest)  18 us
    dot_general x2, matrix products, first_layer(): jnp.einsum('mkl,ke->mle', w_rad_one, radial_terms, precision=highest)  13.1 us
  transfers between devices with their start and end apart: 16, of which 8 were waited for; matrix products, arithmetic and copies ran while one was open for 9% of the time, Pallas kernels for 0%

commit v1 on v0

v1 whole, which is shorter than its diff:
```python
import jax
import jax.numpy as jnp
from jax import lax
from jax.experimental import pallas as pl
from jax.experimental.pallas import tpu as pltpu
from jax.sharding import PartitionSpec as P

SPECIES = 4
RADIAL = 8
FEATS = 40
OWN = 128
SLOTS = 12
EXT = 640
EDGES = SLOTS * OWN
LATENT = 256
MEMBERS = 4
STEP = 512

box_side = 4.0
soft_square = 0.25
centre_step = 0.75
basis_width = 0.75
pool_scale = 0.25
time_step = 0.25

f32 = jnp.float32
bf16 = jnp.bfloat16
NT = (((1,), (1,)), ((), ()))


def vmem(count):
    return [pl.BlockSpec(memory_space=pltpu.VMEM)] * count


def params():
    return pltpu.CompilerParams(vmem_limit_bytes=56 * 1024 * 1024)


def mm(a, b):
    return jnp.dot(a, b, preferred_element_type=f32)


def mm_nt(a, b):
    return lax.dot_general(a, b, NT, preferred_element_type=f32)


def split2(x):
    hi = x.astype(bf16)
    lo = (x - hi.astype(f32)).astype(bf16)
    return hi, lo


def split3(x):
    one = x.astype(bf16).astype(f32)
    rest = x - one
    two = rest.astype(bf16).astype(f32)
    return one, two, rest - two


def stacked3(x, rows):
    parts = list(split3(x))
    left = rows - 3 * x.shape[0]
    if left:
        parts.append(jnp.zeros((left, x.shape[1]), f32))
    return jnp.concatenate(parts, axis=0).astype(bf16)


def unstacked3(x, rows):
    return x[0:rows] + x[rows : 2 * rows] + x[2 * rows : 3 * rows]


def one_hot(rows, index_row, first=0):
    ids = lax.broadcasted_iota(jnp.int32, (rows, index_row.shape[1]), 0) + first
    return (ids == index_row).astype(f32).astype(bf16)


def lists_of(send_ref):
    pairs = ((2, 3), (0, 1), (1, 3), (0, 2))
    return [
        jnp.concatenate([send_ref[a : a + 1, :], send_ref[b : b + 1, :]], axis=1) for a, b in pairs
    ]


def pack_kernel(pos_ref, spec_ref, send_ref, own_ref, o0, o1, o2, o3):
    own = jnp.concatenate(
        [pos_ref[...], spec_ref[...].astype(f32), jnp.zeros((4, OWN), f32)], axis=0
    )
    own_ref[...] = own
    stacked = stacked3(own, 32)
    for out, index in zip((o0, o1, o2, o3), lists_of(send_ref)):
        out[...] = unstacked3(mm(stacked, one_hot(OWN, index)), 8)


def prep_kernel(
    nbr_ref,
    counts_ref,
    wr1_ref,
    nbr_emb_ref,
    self_emb_ref,
    wone_ref,
    wsrc_ref,
    wdst_ref,
    wr2_ref,
    wedge_ref,
    wout_ref,
    a_ref,
    at_ref,
    live_ref,
    weff_ref,
    wback_ref,
    wr2s_ref,
    wr2b_ref,
    src_ref,
    dst_ref,
    edge_ref,
    eout_ref,
):
    slot_ids = lax.broadcasted_iota(jnp.int32, (SLOTS, OWN), 0)
    live = slot_ids < counts_ref[...]
    live_ref[...] = live.astype(f32)
    masked = jnp.where(live, nbr_ref[...], -1)
    padded = jnp.concatenate([masked, jnp.full((OWN - SLOTS, OWN), -1, jnp.int32)], axis=0)
    columns = jnp.transpose(padded)
    lanes = lax.broadcasted_iota(jnp.int32, (OWN, EXT), 1)
    centre = lax.broadcasted_iota(jnp.int32, (OWN, OWN), 0)
    atom = lax.broadcasted_iota(jnp.int32, (1, OWN), 1)
    for s in range(SLOTS):
        a_ref[s * OWN : (s + 1) * OWN, :] = (lanes == columns[:, s : s + 1]).astype(f32).astype(bf16)
        row = masked[s : s + 1, :]
        at_ref[0:EXT, s * OWN : (s + 1) * OWN] = one_hot(EXT, row)
        own_row = jnp.where(row >= 0, atom, -1)
        at_ref[EXT : EXT + OWN, s * OWN : (s + 1) * OWN] = (
            (centre == own_row).astype(f32).astype(bf16)
        )
    for m in range(MEMBERS):
        mixed = jnp.concatenate(
            [wr1_ref[m] * nbr_emb_ref[m, sp : sp + 1, :] for sp in range(SPECIES)], axis=0
        )
        eff = pool_scale * jnp.dot(
            mixed, wone_ref[m], precision=lax.Precision.HIGHEST, preferred_element_type=f32
        )
        full = jnp.concatenate([eff, self_emb_ref[m], jnp.zeros((4, LATENT), f32)], axis=0)
        hi = full.astype(bf16).astype(f32)
        lo = full - hi
        weff_ref[m] = jnp.concatenate([hi, hi, lo, jnp.zeros((8, LATENT), f32)], axis=0).astype(bf16)
        hi, lo = hi[0:32], lo[0:32]
        wback_ref[m, 0] = jnp.concatenate([hi, lo, jnp.zeros((64, LATENT), f32)], axis=0).astype(bf16)
        wback_ref[m, 1] = jnp.concatenate([hi, jnp.zeros((96, LATENT), f32)], axis=0).astype(bf16)
        full = wr2_ref[m]
        hi = full.astype(bf16).astype(f32)
        lo = full - hi
        wr2s_ref[m] = jnp.concatenate([hi, hi, lo, jnp.zeros((104, LATENT), f32)], axis=0).astype(
            bf16
        )
        wr2b_ref[m, 0] = jnp.concatenate([hi, lo, jnp.zeros((112, LATENT), f32)], axis=0).astype(bf16)
        wr2b_ref[m, 1] = jnp.concatenate([hi, jnp.zeros((120, LATENT), f32)], axis=0).astype(bf16)
        for given, kept in ((wsrc_ref, src_ref), (wdst_ref, dst_ref), (wedge_ref, edge_ref)):
            hi, lo = split2(given[m])
            kept[m, 0] = hi
            kept[m, 1] = lo
        hi, lo = split2(wedge_ref[m] * (wout_ref[m : m + 1, :] * (1.0 / MEMBERS)))
        eout_ref[m, 0] = hi
        eout_ref[m, 1] = lo


def geometry_kernel(own_ref, g0, g1, g2, g3, send_ref, at_ref, live_ref, b_ref, geo_ref, basis_ref, o0, o1, o2, o3):
    own = own_ref[...]
    rows = lax.broadcasted_iota(jnp.int32, (8, OWN), 0)
    pieces = [own]
    for ref, row, by in ((g0, 0, -box_side), (g1, 0, box_side), (g2, 1, -box_side), (g3, 1, box_side)):
        pieces.append(ref[...] + jnp.where(rows == row, by, 0.0))
    ext = jnp.concatenate(pieces, axis=1)
    there = unstacked3(mm(stacked3(ext, 32), at_ref[0:EXT, :]), 8)
    centres = centre_step * lax.broadcasted_iota(jnp.int32, (RADIAL, OWN), 0).astype(f32)
    sums = [jnp.zeros((RADIAL, OWN), f32) for _ in range(SPECIES)]
    for s in range(SLOTS):
        other = there[:, s * OWN : (s + 1) * OWN]
        sep = other - own
        square = sep[0:1] * sep[0:1] + sep[1:2] * sep[1:2] + sep[2:3] * sep[2:3]
        distance = jnp.sqrt(square + soft_square)
        scaled = (distance - centres) / basis_width
        basis = jnp.exp(-scaled * scaled)
        basis_ref[:, s * OWN : (s + 1) * OWN] = basis
        geo_ref[:, s * OWN : (s + 1) * OWN] = jnp.where(
            rows == 4, distance, jnp.where(rows < 3, sep, other)
        )
        kind = other[3:4]
        alive = live_ref[s : s + 1, :]
        for sp in range(SPECIES):
            sums[sp] = sums[sp] + basis * jnp.where(kind == float(sp), alive, 0.0)
    flags = jnp.where(rows.astype(f32) == own[3:4], 1.0, 0.0)
    b_own = jnp.concatenate(sums + [flags], axis=0)
    b_ref[...] = b_own
    stacked = stacked3(b_own, OWN)
    for out, index in zip((o0, o1, o2, o3), lists_of(send_ref)):
        out[...] = unstacked3(mm(stacked, one_hot(OWN, index)), FEATS)


def half_tanh(x):
    return 0.5 + 0.5 * jnp.tanh(0.5 * x)


def main_kernel(
    b0,
    b1,
    b2,
    b3,
    b4,
    basis_ref,
    a_ref,
    at_ref,
    weff_ref,
    wback_ref,
    wr2s_ref,
    wr2b_ref,
    src_ref,
    dst_ref,
    edge_ref,
    eout_ref,
    c0,
    c1,
    c2,
    c3,
    c4,
    ctb_out,
    xb,
    bs,
    slope,
    u_hi,
    u_lo,
    centre,
    cx_hi,
    cx_lo,
    ctb,
    acc,
):
    for n, ref in enumerate((b0, b1, b2, b3, b4)):
        full = ref[...]
        hi = full.astype(bf16).astype(f32)
        lo = full - hi
        tall = jnp.concatenate([hi, lo, hi, jnp.zeros((8, OWN), f32)], axis=0)
        xb[n * OWN : (n + 1) * OWN, :] = jnp.transpose(tall).astype(bf16)
    for s in range(SLOTS):
        full = basis_ref[:, s * OWN : (s + 1) * OWN]
        hi = full.astype(bf16).astype(f32)
        lo = full - hi
        tall = jnp.concatenate([hi, lo, hi, jnp.zeros((104, OWN), f32)], axis=0)
        bs[s * OWN : (s + 1) * OWN, :] = jnp.transpose(tall).astype(bf16)
    ctb[...] = jnp.zeros_like(ctb)
    acc[...] = jnp.zeros_like(acc)

    def three(dot, hi, lo, w_ref, m):
        return dot(hi, w_ref[m, 0]) + dot(lo, w_ref[m, 0]) + dot(hi, w_ref[m, 1])

    @pl.loop(0, MEMBERS)
    def _(m):
        pre = mm(xb[...], weff_ref[m])
        sig = half_tanh(pre)
        hid = pre * sig
        slope[...] = sig + hid * (1.0 - sig)
        hi, lo = split2(hid)
        hi2, lo2 = split2(three(mm, hi, lo, dst_ref, m))
        u_hi[...] = hi2
        u_lo[...] = lo2
        centre[...] = three(mm, hi[0:OWN], lo[0:OWN], src_ref, m)

        @pl.loop(0, EDGES // STEP)
        def _(t):
            at = pl.ds(pl.multiple_of(t * STEP, STEP), STEP)
            pick = a_ref[at, :]
            x = mm(pick, u_hi[...]) + mm(pick, u_lo[...]) + mm(bs[at, :], wr2s_ref[m])
            x = x + jnp.concatenate([centre[...]] * (STEP // OWN), axis=0)
            sig = half_tanh(x)
            pair = x * sig
            dx = sig + pair * (1.0 - sig)
            hi, lo = split2(pair)
            y = three(mm, hi, lo, edge_ref, m)
            sig = half_tanh(y)
            hi, lo = split2(sig + y * sig * (1.0 - sig))
            hi, lo = split2(three(mm_nt, hi, lo, eout_ref, m) * dx)
            cx_hi[at, :] = hi
            cx_lo[at, :] = lo
            ctb[at, :] += mm_nt(hi, wr2b_ref[m, 0]) + mm_nt(lo, wr2b_ref[m, 1])

        ct = mm(at_ref[...], cx_hi[...]) + mm(at_ref[...], cx_lo[...])
        hi, lo = split2(ct)
        ct_hid = three(mm_nt, hi[0:EXT], lo[0:EXT], dst_ref, m)
        ct_own = three(mm_nt, hi[EXT:], lo[EXT:], src_ref, m)
        ct_hid = jnp.concatenate([ct_hid[0:OWN] + ct_own, ct_hid[OWN:]], axis=0)
        hi, lo = split2(ct_hid * slope[...])
        acc[...] += mm_nt(hi, wback_ref[m, 0]) + mm_nt(lo, wback_ref[m, 1])

    for n, ref in enumerate((c0, c1, c2, c3, c4)):
        wide = jnp.transpose(acc[n * OWN : (n + 1) * OWN, :])
        ref[...] = wide[0:32] + wide[32:64]
    for s in range(SLOTS):
        wide = jnp.transpose(ctb[s * OWN : (s + 1) * OWN, :])
        ctb_out[:, s * OWN : (s + 1) * OWN] = wide[0:8] + wide[8:16]


def list_columns(send_ref):
    pairs = ((0, 1), (2, 3), (0, 2), (1, 3))
    return [
        jnp.concatenate([send_ref[a : a + 1, :], send_ref[b : b + 1, :]], axis=1) for a, b in pairs
    ]


def collected(pieces, send_ref, rows):
    total = None
    for piece, index in zip(pieces, list_columns(send_ref)):
        got = unstacked3(
            mm_nt(stacked3(piece[...], -(-3 * rows // 16) * 16), one_hot(OWN, index)), rows
        )
        total = got if total is None else total + got
    return total


def push_kernel(own_ct, r0, r1, r2, r3, send_ref, basis_ref, geo_ref, live_ref, ctb_ref, a_ref, own_out, o0, o1, o2, o3):
    ct = own_ct[...] + collected((r0, r1, r2, r3), send_ref, 32)
    rows = lax.broadcasted_iota(jnp.int32, (8, OWN), 0)
    centres = centre_step * lax.broadcasted_iota(jnp.int32, (RADIAL, OWN), 0).astype(f32)
    pulled = jnp.zeros((8, OWN), f32)
    seps = []
    for s in range(SLOTS):
        at = slice(s * OWN, (s + 1) * OWN)
        geo = geo_ref[:, at]
        kind = geo[3:4]
        picked = ctb_ref[:, at]
        for sp in range(SPECIES):
            picked = picked + jnp.where(kind == float(sp), ct[sp * 8 : sp * 8 + 8], 0.0)
        distance = geo[4:5]
        slope = picked * basis_ref[:, at] * (distance - centres)
        ct_d = jnp.sum(slope, axis=0, keepdims=True) * (-2.0 / (basis_width * basis_width))
        ct_sep = jnp.where(rows < 3, geo * (ct_d * live_ref[s : s + 1, :] / distance), 0.0)
        pulled = pulled - ct_sep
        seps.append(ct_sep)
    all_sep = jnp.concatenate(seps, axis=1)
    spread = unstacked3(mm(stacked3(all_sep, 32), a_ref[...]), 8)
    own_out[...] = spread[:, 0:OWN] + pulled
    for n, out in enumerate((o0, o1, o2, o3)):
        out[...] = spread[:, (n + 1) * OWN : (n + 2) * OWN]


def finish_kernel(own_ct, r0, r1, r2, r3, send_ref, pos_ref, vel_ref, spec_ref, mass_ref, pos_out, vel_out):
    ct = own_ct[...] + collected((r0, r1, r2, r3), send_ref, 8)
    spec = spec_ref[...]
    scale = jnp.zeros(spec.shape, f32)
    for sp in range(SPECIES):
        scale = scale + jnp.where(spec == sp, mass_ref[sp], 0.0)
    vel = vel_ref[...] - time_step * scale * ct[0:3]
    vel_out[...] = vel
    pos_out[...] = pos_ref[...] + time_step * vel


def shifted(shard, axis, by):
    peers = lax.axis_size(axis)
    return lax.ppermute(shard, axis, [(i, (i + by) % peers) for i in range(peers)])


def sent(four):
    return (
        shifted(four[0], "gx", 1),
        shifted(four[1], "gx", -1),
        shifted(four[2], "gy", 1),
        shifted(four[3], "gy", -1),
    )


def returned(four):
    return (
        shifted(four[1], "gx", 1),
        shifted(four[0], "gx", -1),
        shifted(four[3], "gy", 1),
        shifted(four[2], "gy", -1),
    )


def like(*shape):
    return jax.ShapeDtypeStruct(shape, f32)


def like16(*shape):
    return jax.ShapeDtypeStruct(shape, bf16)


def shards(
    positions,
    velocities,
    species,
    counts,
    neighbours,
    send_lists,
    inv_mass,
    w_rad_one,
    emb_nbr,
    emb_self,
    w_one,
    w_src,
    w_dst,
    w_rad_two,
    w_edge,
    w_out,
):
    spec = species[None, :]
    own, *packed = pl.pallas_call(
        pack_kernel,
        out_shape=[like(8, OWN)] * 5,
        in_specs=vmem(3),
        out_specs=vmem(5),
        name="pack",
    )(positions, spec, send_lists)
    ghosts = sent(packed)
    a, at, live, weff, wback, wr2s, wr2b, src, dst, edge, eout = pl.pallas_call(
        prep_kernel,
        out_shape=[
            like16(EDGES, EXT),
            like16(EXT + OWN, EDGES),
            like(SLOTS, OWN),
            like16(MEMBERS, 128, LATENT),
            like16(MEMBERS, 2, 128, LATENT),
            like16(MEMBERS, 128, LATENT),
            like16(MEMBERS, 2, 128, LATENT),
        ]
        + [like16(MEMBERS, 2, LATENT, LATENT)] * 4,
        in_specs=vmem(11),
        out_specs=vmem(11),
        compiler_params=params(),
        cost_estimate=pl.CostEstimate(flops=200_000_000, bytes_accessed=16_000_000, transcendentals=0),
        name="prep",
    )(
        neighbours,
        counts[None, :],
        w_rad_one,
        emb_nbr,
        emb_self,
        w_one,
        w_src,
        w_dst,
        w_rad_two,
        w_edge,
        w_out,
    )
    b_own, geo, basis, *b_packed = pl.pallas_call(
        geometry_kernel,
        out_shape=[like(FEATS, OWN), like(8, EDGES), like(8, EDGES)] + [like(FEATS, OWN)] * 4,
        in_specs=vmem(8),
        out_specs=vmem(7),
        compiler_params=params(),
        name="geometry",
    )(own, *ghosts, send_lists, at, live)
    b_ghosts = sent(b_packed)
    *cts, ctb = pl.pallas_call(
        main_kernel,
        out_shape=[like(32, OWN)] * 5 + [like(8, EDGES)],
        in_specs=vmem(16),
        out_specs=vmem(6),
        scratch_shapes=[
            pltpu.VMEM((EXT, 128), bf16),
            pltpu.VMEM((EDGES, 128), bf16),
            pltpu.VMEM((EXT, LATENT), f32),
            pltpu.VMEM((EXT, LATENT), bf16),
            pltpu.VMEM((EXT, LATENT), bf16),
            pltpu.VMEM((OWN, LATENT), f32),
            pltpu.VMEM((EDGES, LATENT), bf16),
            pltpu.VMEM((EDGES, LATENT), bf16),
            pltpu.VMEM((EDGES, 128), f32),
            pltpu.VMEM((EXT, 128), f32),
        ],
        compiler_params=params(),
        name="members",
    )(b_own, *b_ghosts, basis, a, at, weff, wback, wr2s, wr2b, src, dst, edge, eout)
    back = returned(cts[1:])
    own_ct, *outgoing = pl.pallas_call(
        push_kernel,
        out_shape=[like(8, OWN)] * 5,
        in_specs=vmem(11),
        out_specs=vmem(5),
        compiler_params=params(),
        name="push",
    )(cts[0], *back, send_lists, basis, geo, live, ctb, a)
    last = returned(outgoing)
    new_positions, new_velocities = pl.pallas_call(
        finish_kernel,
        out_shape=[like(3, OWN), like(3, OWN)],
        in_specs=vmem(9) + [pl.BlockSpec(memory_space=pltpu.SMEM)],
        out_specs=vmem(2),
        name="finish",
    )(own_ct, *last, send_lists, positions, velocities, spec, inv_mass)
    return (new_positions, new_velocities)


def solution(mesh):
    split = P(None, ("gx", "gy"))
    row = P(("gx", "gy"))
    placed = (split, split, row, row, split, split) + (P(),) * 10
    return jax.shard_map(
        shards, mesh=mesh, in_specs=placed, out_specs=(split, split), check_vma=False
    )
```

time: 475 us -> 113 us (0.24)
  the two profiles are of different devices: /device:TPU:0 before, /device:TPU:1 now
where the time goes in v1:
time: 113 us
  Pallas kernels  62.2 us (55%)
  starting transfers between devices  37.5 us (33%)
  waiting for transfers between devices  10 us (9%)
  local copies, waits for them, and re-layouts  2.36 us (2%)
    pallas_call x1, Pallas kernels, shards(): pl.pallas_call(main_kernel, out_shape=[like(32, OWN)] * 5 + [like(8, EDGE...  45 us
    ppermute x16, starting transfers between devices, shifted(): lax.ppermute(shard, axis, [(i, (i + by) % peers) for i in range(peers)])  37.5 us
    ppermute x16, waiting for transfers between devices, shifted(): lax.ppermute(shard, axis, [(i, (i + by) % peers) for i in range(peers)])  10 us
    pallas_call x1, Pallas kernels, shards(): pl.pallas_call(prep_kernel, out_shape=[like16(EDGES, EXT), like16(EXT + O...  7.89 us
    pallas_call x1, Pallas kernels, shards(): pl.pallas_call(push_kernel, out_shape=[like(8, OWN)] * 5, in_specs=vmem(1...  3.16 us
    pallas_call x1, Pallas kernels, shards(): pl.pallas_call(geometry_kernel, out_shape=[like(FEATS, OWN), like(8, EDGE...  2.98 us
    unnamed x32, local copies, waits for them, and re-layouts  2.36 us
  transfers between devices with their start and end apart: 16, of which 8 were waited for; matrix products, arithmetic and copies ran while one was open for 0% of the time, Pallas kernels for 7%

profile of v1, /device:TPU:1, one launch (start us, length us, event | category | flops | bytes accessed | tf_op | source)
XLA Modules:
  0.0 112.9 jit_solution(6550400669598958159)
XLA Ops:
  0.6 1.5 %pack.1 = (f32[8,128]{1,0:T(8,128)}, f32[8,128]{1,0:T(8,128)}, f32[8,128]{1,0:T(8,128)}, f32[8,128]{1,0:T(8,128)}, f32[8,128]{1,0:T(8,128)}) custom-call(f32[3,128]{1,0:T(4,128)} %pos_ref.3, s32[1,128]{1,0:T(1,128)} %bitcast.2, s32[4,64]{1,0:T(4,128)} %send_ref.7), custom_call_target="tpu_custom_call" | custom-call | tf_op jit(solution)/shard_map/pack/pallas_call | solution.py:405
  2.2 3.7 %collective-permute-start = (f32[8,128]{1,0:T(8,128)}, f32[8,128]{1,0:T(8,128)S(1)}, u32[]{:S(2)}, u32[]{:S(2)}) collective-permute-start(f32[8,128]{1,0:T(8,128)} %get-tuple-element.37), channel_id=1, source_target_pairs={{0,4},{4,8},{8,12},{12,16},{16,20},{20,24},{24,28},{28,32},{32,36}... | collective-permute-start | bytes 12296 | tf_op jit(solution)/shard_map/ppermute | solution.py:357
  5.9 7.5 %collective-permute-start.1 = (f32[8,128]{1,0:T(8,128)}, f32[8,128]{1,0:T(8,128)S(1)}, u32[]{:S(2)}, u32[]{:S(2)}) collective-permute-start(f32[8,128]{1,0:T(8,128)} %get-tuple-element.38), channel_id=1, source_target_pairs={{0,252},{4,0},{8,4},{12,8},{16,12},{20,16},{24,20},{28,24},{32,28}... | collective-permute-start | bytes 12296 | tf_op jit(solution)/shard_map/ppermute | solution.py:357
  13.4 1.2 %collective-permute-start.2 = (f32[8,128]{1,0:T(8,128)}, f32[8,128]{1,0:T(8,128)S(1)}, u32[]{:S(2)}, u32[]{:S(2)}) collective-permute-start(f32[8,128]{1,0:T(8,128)} %get-tuple-element.39), channel_id=1, source_target_pairs={{0,1},{1,2},{2,3},{3,0},{4,5},{5,6},{6,7},{7,4},{8,9},{9,10},{10,1... | collective-permute-start | bytes 12296 | tf_op jit(solution)/shard_map/ppermute | solution.py:357
  14.6 0.0 collective-permute-start.3
  14.7 7.9 %prep.1 = (bf16[1536,640]{1,0:T(8,128)(2,1)}, bf16[768,1536]{1,0:T(8,128)(2,1)}, f32[12,128]{1,0:T(8,128)}, bf16[4,128,256]{2,1,0:T(8,128)(2,1)}, bf16[4,2,128,2...) custom-call(s32[12,128]{1,0:T(8,128)} %nbr_ref.1, ...), custom_call_target="tpu_custom_call" | custom-call | flops 200000000 | bytes 16000000 | tf_op jit(solution)/shard_map/prep/pallas_call | solution.py:413
  22.5 0.0 collective-permute-done.g0
  22.5 0.0 copy-start.8
  22.6 0.0 collective-permute-done.1.g1
  22.6 0.0 copy-start.9
  22.6 0.0 collective-permute-done.2.g2
  22.6 0.0 copy-start.10
  22.6 0.0 collective-permute-done.3.g3
  22.6 0.0 copy-start.11
  22.6 0.5 copy-done.8
  23.1 0.0 copy-done.9
  23.2 0.0 copy-done.10
  23.2 0.0 copy-done.11
  23.2 3.0 %geometry.1 = (f32[40,128]{1,0:T(8,128)}, f32[8,1536]{1,0:T(8,128)}, f32[8,1536]{1,0:T(8,128)}, f32[40,128]{1,0:T(8,128)}, f32[40,128]{1,0:T(8,128)}, /*index=5*/f32[40,128]{1,0:T(8,128)}, f32[40,128]{1,0:T(8,128)}) custom-call(f32[8,128]{1,0:T(8,128)} %get-tuple-element.36.own_ref, f32[8,128]{1,0:T(8,128)} %copy-done.8, f32[8,128]{1,0:T(8,128)} %copy-done.9, ...), custom_call_target="tpu_custom_call" | custom-call | tf_op jit(solution)/shard_map/geometry/pallas_call | solution.py:443
  26.2 0.0 collective-permute-start.4
  26.2 7.2 %collective-permute-start.5 = (f32[40,128]{1,0:T(8,128)}, f32[40,128]{1,0:T(8,128)S(1)}, u32[]{:S(2)}, u32[]{:S(2)}) collective-permute-start(f32[40,128]{1,0:T(8,128)} %get-tuple-element.45), channel_id=1, source_target_pairs={{0,252},{4,0},{8,4},{12,8},{16,12},{20,16},{24,20},{28,24},{32,28}... | collective-permute-start | bytes 61448 | tf_op jit(solution)/shard_map/ppermute | solution.py:357
  33.4 2.3 %collective-permute-start.6 = (f32[40,128]{1,0:T(8,128)}, f32[40,128]{1,0:T(8,128)S(1)}, u32[]{:S(2)}, u32[]{:S(2)}) collective-permute-start(f32[40,128]{1,0:T(8,128)} %get-tuple-element.46), channel_id=1, source_target_pairs={{0,1},{1,2},{2,3},{3,0},{4,5},{5,6},{6,7},{7,4},{8,9},{9,10},{10,1... | collective-permute-start | bytes 61448 | tf_op jit(solution)/shard_map/ppermute | solution.py:357
  35.7 0.0 collective-permute-start.7
  35.7 0.0 collective-permute-done.4.b1
  35.7 0.0 copy-start
  35.7 0.0 collective-permute-done.5.b2
  35.7 0.0 copy-start.1
  35.7 1.1 collective-permute-done.6.b3
  36.8 0.0 copy-start.2
  36.8 2.3 %collective-permute-done.7.b4 = f32[40,128]{1,0:T(8,128)S(1)} collective-permute-done((f32[40,128]{1,0:T(8,128)}, f32[40,128]{1,0:T(8,128)S(1)}, u32[]{:S(2)}, u32[]{:S(2)}) %collective-permute-start.7) | collective-permute-done | bytes 20512 | tf_op jit(solution)/shard_map/ppermute | solution.py:357
  39.1 0.0 copy-start.3
  39.1 0.0 copy-done
  39.1 0.0 copy-done.1
  39.1 0.0 copy-done.2
  39.1 0.6 copy-done.3
  39.7 45.0 %members.1 = (f32[32,128]{1,0:T(8,128)}, f32[32,128]{1,0:T(8,128)}, f32[32,128]{1,0:T(8,128)}, f32[32,128]{1,0:T(8,128)}, f32[32,128]{1,0:T(8,128)}, /*index=5*/f32[8,1536]{1,0:T(8,128)}) custom-call(f32[40,128]{1,0:T(8,128)} %get-tuple-element.43.b0, f32[40,128]{1,0:T(8,128)} %copy-done, f32[40,128]{1,0:T(8,128)} %copy-done.1, f32[40,128]{1,0:T(8,128)} %copy-done.2, ...), custom_call_target="tpu_custom_call" | custom-call | tf_op jit(solution)/shard_map/members/pallas_call | solution.py:452
  84.7 0.0 collective-permute-start.8
  84.7 7.2 %collective-permute-start.9 = (f32[32,128]{1,0:T(8,128)}, f32[32,128]{1,0:T(8,128)S(1)}, u32[]{:S(2)}, u32[]{:S(2)}) collective-permute-start(f32[32,128]{1,0:T(8,128)} %get-tuple-element.60), channel_id=1, source_target_pairs={{0,252},{4,0},{8,4},{12,8},{16,12},{20,16},{24,20},{28,24},{32,28}... | collective-permute-start | bytes 49160 | tf_op jit(solution)/shard_map/ppermute | solution.py:357
  91.9 0.6 collective-permute-start.10
  92.5 0.0 collective-permute-start.11
  92.5 0.7 collective-permute-done.8.r0
  93.2 0.0 copy-start.4
  93.2 0.0 collective-permute-done.9.r1
  93.2 0.0 copy-start.5
  93.2 0.3 collective-permute-done.10.r2
  93.6 2.3 %collective-permute-done.11.r3 = f32[32,128]{1,0:T(8,128)S(1)} collective-permute-done((f32[32,128]{1,0:T(8,128)}, f32[32,128]{1,0:T(8,128)S(1)}, u32[]{:S(2)}, u32[]{:S(2)}) %collective-permute-start.11) | collective-permute-done | bytes 16416 | tf_op jit(solution)/shard_map/ppermute | solution.py:357
  95.9 0.0 copy-done.4
  95.9 0.0 copy-done.5
  95.9 0.0 copy-done.6
  95.9 0.6 copy-done.7
  96.5 3.2 %push.1 = (f32[8,128]{1,0:T(8,128)}, f32[8,128]{1,0:T(8,128)}, f32[8,128]{1,0:T(8,128)}, f32[8,128]{1,0:T(8,128)}, f32[8,128]{1,0:T(8,128)}) custom-call(f32[32,128]{1,0:T(8,128)} %get-tuple-element.58.own_ct, f32[32,128]{1,0:T(8,128)} %copy-done.4, f32[32,128]{1,0:T(8,128)} %copy-done.5, f32[32,128]{1,0:T(8,128)} %copy-done.6, f32[32,128]{1,0:T(8,128)} %copy-done.7, ...), custom_call_target="tpu_custom_call" | custom-call | tf_op jit(solution)/shard_map/push/pallas_call | solution.py:473
  99.6 0.0 collective-permute-start.12
  99.6 7.2 %collective-permute-start.13 = (f32[8,128]{1,0:T(8,128)}, f32[8,128]{1,0:T(8,128)S(1)}, u32[]{:S(2)}, u32[]{:S(2)}) collective-permute-start(f32[8,128]{1,0:T(8,128)} %get-tuple-element.67), channel_id=1, source_target_pairs={{0,252},{4,0},{8,4},{12,8},{16,12},{20,16},{24,20},{28,24},{32,28}... | collective-permute-start | bytes 12296 | tf_op jit(solution)/shard_map/ppermute | solution.py:357
  106.8 0.6 collective-permute-start.14
  107.4 0.0 collective-permute-start.15
  107.4 0.6 collective-permute-done.12.r0
  108.0 0.0 collective-permute-done.13.r1
  108.0 0.3 collective-permute-done.14.r2
  108.4 2.3 %collective-permute-done.15.r3 = f32[8,128]{1,0:T(8,128)S(1)} collective-permute-done((f32[8,128]{1,0:T(8,128)}, f32[8,128]{1,0:T(8,128)S(1)}, u32[]{:S(2)}, u32[]{:S(2)}) %collective-permute-start.15) | collective-permute-done | bytes 4128 | tf_op jit(solution)/shard_map/ppermute | solution.py:357
  110.6 0.0 copy-done.12
  110.6 0.0 copy-done.13
  110.6 0.0 copy-done.14
  110.7 0.6 copy-done.15
  111.2 1.6 %finish.1 = (f32[3,128]{1,0:T(4,128)}, f32[3,128]{1,0:T(4,128)}) custom-call(f32[8,128]{1,0:T(8,128)} %get-tuple-element.65.own_ct, f32[8,128]{1,0:T(8,128)} %copy-done.12, f32[8,128]{1,0:T(8,128)} %copy-done.13, f32[8,128]{1,0:T(8,128)} %copy-done.14, f32[8,128]{1,0:T(8,128)} %copy-done.15, s32[4,64]{1,0:T(4,128)} %send_ref.7, f32[3,128]{1,0:T(4,128)} %pos_ref.3, ...), custom_call_target="tpu_custom_call" | custom-call | tf_op jit(solution)/shard_map/finish/pallas_call | solution.py:482
  (6 shorter events, 0.0 us)
Async XLA Ops:
  2.2 20.4 %collective-permute-start = (f32[8,128]{1,0:T(8,128)}, f32[8,128]{1,0:T(8,128)S(1)}, u32[]{:S(2)}, u32[]{:S(2)}) collective-permute-start(f32[8,128]{1,0:T(8,128)} %get-tuple-element.37), channel_id=1, source_target_pairs={{0,4},{4,8},{8,12},{12,16},{16,20},{20,24},{24,28},{28,32},{32,36}... | collective-permute-start | bytes 12296 | tf_op jit(solution)/shard_map/ppermute | solution.py:357
  5.9 16.6 %collective-permute-start.1 = (f32[8,128]{1,0:T(8,128)}, f32[8,128]{1,0:T(8,128)S(1)}, u32[]{:S(2)}, u32[]{:S(2)}) collective-permute-start(f32[8,128]{1,0:T(8,128)} %get-tuple-element.38), channel_id=1, source_target_pairs={{0,252},{4,0},{8,4},{12,8},{16,12},{20,16},{24,20},{28,24},{32,28}... | collective-permute-start | bytes 12296 | tf_op jit(solution)/shard_map/ppermute | solution.py:357
  13.4 9.2 %collective-permute-start.2 = (f32[8,128]{1,0:T(8,128)}, f32[8,128]{1,0:T(8,128)S(1)}, u32[]{:S(2)}, u32[]{:S(2)}) collective-permute-start(f32[8,128]{1,0:T(8,128)} %get-tuple-element.39), channel_id=1, source_target_pairs={{0,1},{1,2},{2,3},{3,0},{4,5},{5,6},{6,7},{7,4},{8,9},{9,10},{10,1... | collective-permute-start | bytes 12296 | tf_op jit(solution)/shard_map/ppermute | solution.py:357
  14.6 8.0 %collective-permute-start.3 = (f32[8,128]{1,0:T(8,128)}, f32[8,128]{1,0:T(8,128)S(1)}, u32[]{:S(2)}, u32[]{:S(2)}) collective-permute-start(f32[8,128]{1,0:T(8,128)} %get-tuple-element.40), channel_id=1, source_target_pairs={{0,3},{1,0},{2,1},{3,2},{4,7},{5,4},{6,5},{7,6},{8,11},{9,8},{10,9... | collective-permute-start | bytes 12296 | tf_op jit(solution)/shard_map/ppermute | solution.py:357
  22.5 0.6 copy-start.8
  22.6 0.6 copy-start.9
  22.6 0.6 copy-start.10
  22.6 0.6 copy-start.11
  26.2 9.5 %collective-permute-start.4 = (f32[40,128]{1,0:T(8,128)}, f32[40,128]{1,0:T(8,128)S(1)}, u32[]{:S(2)}, u32[]{:S(2)}) collective-permute-start(f32[40,128]{1,0:T(8,128)} %get-tuple-element.44), channel_id=1, source_target_pairs={{0,4},{4,8},{8,12},{12,16},{16,20},{20,24},{24,28},{28,32},{32,36}... | collective-permute-start | bytes 61448 | tf_op jit(solution)/shard_map/ppermute | solution.py:357
  26.2 9.5 %collective-permute-start.5 = (f32[40,128]{1,0:T(8,128)}, f32[40,128]{1,0:T(8,128)S(1)}, u32[]{:S(2)}, u32[]{:S(2)}) collective-permute-start(f32[40,128]{1,0:T(8,128)} %get-tuple-element.45), channel_id=1, source_target_pairs={{0,252},{4,0},{8,4},{12,8},{16,12},{20,16},{24,20},{28,24},{32,28}... | collective-permute-start | bytes 61448 | tf_op jit(solution)/shard_map/ppermute | solution.py:357
  33.4 3.4 %collective-permute-start.6 = (f32[40,128]{1,0:T(8,128)}, f32[40,128]{1,0:T(8,128)S(1)}, u32[]{:S(2)}, u32[]{:S(2)}) collective-permute-start(f32[40,128]{1,0:T(8,128)} %get-tuple-element.46), channel_id=1, source_target_pairs={{0,1},{1,2},{2,3},{3,0},{4,5},{5,6},{6,7},{7,4},{8,9},{9,10},{10,1... | collective-permute-start | bytes 61448 | tf_op jit(solution)/shard_map/ppermute | solution.py:357
  35.7 3.4 %collective-permute-start.7 = (f32[40,128]{1,0:T(8,128)}, f32[40,128]{1,0:T(8,128)S(1)}, u32[]{:S(2)}, u32[]{:S(2)}) collective-permute-start(f32[40,128]{1,0:T(8,128)} %get-tuple-element.47), channel_id=1, source_target_pairs={{0,3},{1,0},{2,1},{3,2},{4,7},{5,4},{6,5},{7,6},{8,11},{9,8},{10,9... | collective-permute-start | bytes 61448 | tf_op jit(solution)/shard_map/ppermute | solution.py:357
  35.7 3.4 %copy-start = (f32[40,128]{1,0:T(8,128)}, f32[40,128]{1,0:T(8,128)S(1)}, u32[]{:S(2)}) copy-start(f32[40,128]{1,0:T(8,128)S(1)} %collective-permute-done.4.b1) | copy-start | bytes 61444
  35.7 3.4 %copy-start.1 = (f32[40,128]{1,0:T(8,128)}, f32[40,128]{1,0:T(8,128)S(1)}, u32[]{:S(2)}) copy-start(f32[40,128]{1,0:T(8,128)S(1)} %collective-permute-done.5.b2) | copy-start | bytes 61444
  36.8 2.3 %copy-start.2 = (f32[40,128]{1,0:T(8,128)}, f32[40,128]{1,0:T(8,128)S(1)}, u32[]{:S(2)}) copy-start(f32[40,128]{1,0:T(8,128)S(1)} %collective-permute-done.6.b3) | copy-start | bytes 61444
  39.1 0.6 copy-start.3
  84.7 8.5 %collective-permute-start.8 = (f32[32,128]{1,0:T(8,128)}, f32[32,128]{1,0:T(8,128)S(1)}, u32[]{:S(2)}, u32[]{:S(2)}) collective-permute-start(f32[32,128]{1,0:T(8,128)} %get-tuple-element.59), channel_id=1, source_target_pairs={{0,4},{4,8},{8,12},{12,16},{16,20},{20,24},{24,28},{28,32},{32,36}... | collective-permute-start | bytes 49160 | tf_op jit(solution)/shard_map/ppermute | solution.py:357
  84.7 8.5 %collective-permute-start.9 = (f32[32,128]{1,0:T(8,128)}, f32[32,128]{1,0:T(8,128)S(1)}, u32[]{:S(2)}, u32[]{:S(2)}) collective-permute-start(f32[32,128]{1,0:T(8,128)} %get-tuple-element.60), channel_id=1, source_target_pairs={{0,252},{4,0},{8,4},{12,8},{16,12},{20,16},{24,20},{28,24},{32,28}... | collective-permute-start | bytes 49160 | tf_op jit(solution)/shard_map/ppermute | solution.py:357
  91.9 1.7 %collective-permute-start.10 = (f32[32,128]{1,0:T(8,128)}, f32[32,128]{1,0:T(8,128)S(1)}, u32[]{:S(2)}, u32[]{:S(2)}) collective-permute-start(f32[32,128]{1,0:T(8,128)} %get-tuple-element.61), channel_id=1, source_target_pairs={{0,1},{1,2},{2,3},{3,0},{4,5},{5,6},{6,7},{7,4},{8,9},{9,10},{10,1... | collective-permute-start | bytes 49160 | tf_op jit(solution)/shard_map/ppermute | solution.py:357
  92.5 3.4 %collective-permute-start.11 = (f32[32,128]{1,0:T(8,128)}, f32[32,128]{1,0:T(8,128)S(1)}, u32[]{:S(2)}, u32[]{:S(2)}) collective-permute-start(f32[32,128]{1,0:T(8,128)} %get-tuple-element.62), channel_id=1, source_target_pairs={{0,3},{1,0},{2,1},{3,2},{4,7},{5,4},{6,5},{7,6},{8,11},{9,8},{10,9... | collective-permute-start | bytes 49160 | tf_op jit(solution)/shard_map/ppermute | solution.py:357
  93.2 2.6 %copy-start.4 = (f32[32,128]{1,0:T(8,128)}, f32[32,128]{1,0:T(8,128)S(1)}, u32[]{:S(2)}) copy-start(f32[32,128]{1,0:T(8,128)S(1)} %collective-permute-done.8.r0) | copy-start | bytes 49156
  93.2 2.6 %copy-start.5 = (f32[32,128]{1,0:T(8,128)}, f32[32,128]{1,0:T(8,128)S(1)}, u32[]{:S(2)}) copy-start(f32[32,128]{1,0:T(8,128)S(1)} %collective-permute-done.9.r1) | copy-start | bytes 49156
  93.6 2.3 %copy-start.6 = (f32[32,128]{1,0:T(8,128)}, f32[32,128]{1,0:T(8,128)S(1)}, u32[]{:S(2)}) copy-start(f32[32,128]{1,0:T(8,128)S(1)} %collective-permute-done.10.r2) | copy-start | bytes 49156
  95.9 0.6 copy-start.7
  99.6 8.4 %collective-permute-start.12 = (f32[8,128]{1,0:T(8,128)}, f32[8,128]{1,0:T(8,128)S(1)}, u32[]{:S(2)}, u32[]{:S(2)}) collective-permute-start(f32[8,128]{1,0:T(8,128)} %get-tuple-element.66), channel_id=1, source_target_pairs={{0,4},{4,8},{8,12},{12,16},{16,20},{20,24},{24,28},{28,32},{32,36}... | collective-permute-start | bytes 12296 | tf_op jit(solution)/shard_map/ppermute | solution.py:357
  99.6 8.4 %collective-permute-start.13 = (f32[8,128]{1,0:T(8,128)}, f32[8,128]{1,0:T(8,128)S(1)}, u32[]{:S(2)}, u32[]{:S(2)}) collective-permute-start(f32[8,128]{1,0:T(8,128)} %get-tuple-element.67), channel_id=1, source_target_pairs={{0,252},{4,0},{8,4},{12,8},{16,12},{20,16},{24,20},{28,24},{32,28}... | collective-permute-start | bytes 12296 | tf_op jit(solution)/shard_map/ppermute | solution.py:357
  106.8 1.6 %collective-permute-start.14 = (f32[8,128]{1,0:T(8,128)}, f32[8,128]{1,0:T(8,128)S(1)}, u32[]{:S(2)}, u32[]{:S(2)}) collective-permute-start(f32[8,128]{1,0:T(8,128)} %get-tuple-element.68), channel_id=1, source_target_pairs={{0,1},{1,2},{2,3},{3,0},{4,5},{5,6},{6,7},{7,4},{8,9},{9,10},{10,1... | collective-permute-start | bytes 12296 | tf_op jit(solution)/shard_map/ppermute | solution.py:357
  107.4 3.2 %collective-permute-start.15 = (f32[8,128]{1,0:T(8,128)}, f32[8,128]{1,0:T(8,128)S(1)}, u32[]{:S(2)}, u32[]{:S(2)}) collective-permute-start(f32[8,128]{1,0:T(8,128)} %get-tuple-element.69), channel_id=1, source_target_pairs={{0,3},{1,0},{2,1},{3,2},{4,7},{5,4},{6,5},{7,6},{8,11},{9,8},{10,9... | collective-permute-start | bytes 12296 | tf_op jit(solution)/shard_map/ppermute | solution.py:357
  108.0 2.6 %copy-start.12 = (f32[8,128]{1,0:T(8,128)}, f32[8,128]{1,0:T(8,128)S(1)}, u32[]{:S(2)}) copy-start(f32[8,128]{1,0:T(8,128)S(1)} %collective-permute-done.12.r0) | copy-start | bytes 12292
  108.0 2.6 %copy-start.13 = (f32[8,128]{1,0:T(8,128)}, f32[8,128]{1,0:T(8,128)S(1)}, u32[]{:S(2)}) copy-start(f32[8,128]{1,0:T(8,128)S(1)} %collective-permute-done.13.r1) | copy-start | bytes 12292
  108.4 2.3 %copy-start.14 = (f32[8,128]{1,0:T(8,128)}, f32[8,128]{1,0:T(8,128)S(1)}, u32[]{:S(2)}) copy-start(f32[8,128]{1,0:T(8,128)S(1)} %collective-permute-done.14.r2) | copy-start | bytes 12292
  110.6 0.6 copy-start.15

commit v2 on v1

v2 whole, which is shorter than its diff:
```python
import jax
import jax.numpy as jnp
from jax import lax
from jax.experimental import pallas as pl
from jax.experimental.pallas import tpu as pltpu
from jax.sharding import PartitionSpec as P

SPECIES = 4
RADIAL = 8
FEATS = 40
OWN = 128
SLOTS = 12
EXT = 640
EDGES = SLOTS * OWN
LATENT = 256
MEMBERS = 4
STEP = 256
LAG = 1

box_side = 4.0
soft_square = 0.25
centre_step = 0.75
basis_width = 0.75
pool_scale = 0.25
time_step = 0.25

f32 = jnp.float32
bf16 = jnp.bfloat16
NT = (((1,), (1,)), ((), ()))


def vmem(count):
    return [pl.BlockSpec(memory_space=pltpu.VMEM)] * count


def hbm(count):
    return [pl.BlockSpec(memory_space=pltpu.HBM)] * count


def params(mib):
    return pltpu.CompilerParams(vmem_limit_bytes=mib * 1024 * 1024)


def mm(a, b):
    return jnp.dot(a, b, preferred_element_type=f32)


def mm_nt(a, b):
    return lax.dot_general(a, b, NT, preferred_element_type=f32)


def split2(x):
    hi = x.astype(bf16)
    lo = (x - hi.astype(f32)).astype(bf16)
    return hi, lo


def split3(x):
    one = x.astype(bf16).astype(f32)
    rest = x - one
    two = rest.astype(bf16).astype(f32)
    return one, two, rest - two


def stacked3(x, rows):
    parts = list(split3(x))
    left = rows - 3 * x.shape[0]
    if left:
        parts.append(jnp.zeros((left, x.shape[1]), f32))
    return jnp.concatenate(parts, axis=0).astype(bf16)


def unstacked3(x, rows):
    return x[0:rows] + x[rows : 2 * rows] + x[2 * rows : 3 * rows]


def one_hot(rows, index_row, first=0):
    ids = lax.broadcasted_iota(jnp.int32, (rows, index_row.shape[1]), 0) + first
    return (ids == index_row).astype(f32).astype(bf16)


def lists_of(send_ref):
    pairs = ((2, 3), (0, 1), (1, 3), (0, 2))
    return [
        jnp.concatenate([send_ref[a : a + 1, :], send_ref[b : b + 1, :]], axis=1) for a, b in pairs
    ]


def odd_along(axis):
    return lax.rem(lax.axis_index(axis), 2) == 1


def by_partner(plus_x, minus_x, plus_y, minus_y):
    odd_x, odd_y = odd_along("gx"), odd_along("gy")
    return (
        jnp.where(odd_x, plus_x, minus_x),
        jnp.where(odd_x, minus_x, plus_x),
        jnp.where(odd_y, plus_y, minus_y),
        jnp.where(odd_y, minus_y, plus_y),
    )


def by_side(refs):
    s0, s1, s2, s3 = [ref[...] for ref in refs]
    odd_x, odd_y = odd_along("gx"), odd_along("gy")
    return (
        jnp.where(odd_x, s0, s1),
        jnp.where(odd_x, s1, s0),
        jnp.where(odd_y, s2, s3),
        jnp.where(odd_y, s3, s2),
    )


def fetched(given, kept, sems):
    copies = []
    for n, (source, target) in enumerate(zip(given, kept)):
        copies.append(pltpu.make_async_copy(source, target, sems.at[n]))
        copies[-1].start()
    return copies


def pack_kernel(pos_hbm, spec_hbm, send_hbm, own_ref, o0, o1, o2, o3, pos_ref, spec_ref, send_ref, sems):
    for copy in fetched((pos_hbm, spec_hbm, send_hbm), (pos_ref, spec_ref, send_ref), sems):
        copy.wait()
    own = jnp.concatenate(
        [pos_ref[...], spec_ref[...].astype(f32), jnp.zeros((4, OWN), f32)], axis=0
    )
    own_ref[...] = own
    stacked = stacked3(own, 32)
    for out, index in zip((o0, o1, o2, o3), by_partner(*lists_of(send_ref))):
        out[...] = unstacked3(mm(stacked, one_hot(OWN, index)), 8)


def halves(full):
    hi = full.astype(bf16).astype(f32)
    return hi, full - hi


def padded_rows(parts, rows):
    left = rows - sum(part.shape[0] for part in parts)
    return jnp.concatenate(parts + [jnp.zeros((left, parts[0].shape[1]), f32)], axis=0).astype(bf16)


def stack_rows(ref, m, full):
    hi, lo = split2(full)
    ref[m, 0:LATENT] = hi
    ref[m, LATENT : 2 * LATENT] = hi
    ref[m, 2 * LATENT : 3 * LATENT] = lo


def stack_columns(ref, m, full):
    hi, lo = split2(full)
    ref[m, :, 0:LATENT] = hi
    ref[m, :, LATENT : 2 * LATENT] = hi
    ref[m, :, 2 * LATENT :] = lo


def picks_kernel(nbr_hbm, counts_hbm, a_ref, at_ref, live_ref, alive_ref, nbr_ref, counts_ref, sems):
    for copy in fetched((nbr_hbm, counts_hbm), (nbr_ref, counts_ref), sems):
        copy.wait()
    slot_ids = lax.broadcasted_iota(jnp.int32, (SLOTS, OWN), 0)
    live = (slot_ids < counts_ref[...]).astype(f32)
    live_ref[...] = live
    nbr = nbr_ref[...]
    rest = OWN - SLOTS
    columns = jnp.transpose(jnp.concatenate([nbr, jnp.zeros((rest, OWN), jnp.int32)], axis=0))
    alive = jnp.transpose(jnp.concatenate([live, jnp.zeros((rest, OWN), f32)], axis=0))
    lanes = lax.broadcasted_iota(jnp.int32, (OWN, EXT), 1)
    for s in range(SLOTS):
        at = slice(s * OWN, (s + 1) * OWN)
        a_ref[at, :] = (lanes == columns[:, s : s + 1]).astype(f32).astype(bf16)
        at_ref[:, at] = one_hot(EXT, nbr[s : s + 1, :])
        alive_ref[at, :] = jnp.broadcast_to(alive[:, s : s + 1], (OWN, OWN))


def weights_kernel(
    after_hbm,
    wr1_hbm,
    nbr_emb_hbm,
    self_emb_hbm,
    wr2_hbm,
    wout_hbm,
    wone_hbm,
    wsrc_hbm,
    wdst_hbm,
    wedge_hbm,
    weff_ref,
    wback_ref,
    wr2b_ref,
    src_ref,
    dst_ref,
    edge_ref,
    srct_ref,
    dstt_ref,
    eout_ref,
    wr1_ref,
    nbr_emb_ref,
    self_emb_ref,
    wr2_ref,
    wout_ref,
    wone_ref,
    wsrc_ref,
    wdst_ref,
    wedge_ref,
    sems,
    large_sems,
):
    small = fetched(
        (wr1_hbm, nbr_emb_hbm, self_emb_hbm, wr2_hbm, wout_hbm),
        (wr1_ref, nbr_emb_ref, self_emb_ref, wr2_ref, wout_ref),
        sems,
    )
    large = fetched(
        (wone_hbm, wsrc_hbm, wdst_hbm, wedge_hbm), (wone_ref, wsrc_ref, wdst_ref, wedge_ref), large_sems
    )
    for copy in small:
        copy.wait()
    large[0].wait()
    for m in range(MEMBERS):
        mixed = jnp.concatenate(
            [wr1_ref[m] * nbr_emb_ref[m, sp : sp + 1, :] for sp in range(SPECIES)], axis=0
        )
        eff = pool_scale * jnp.dot(
            mixed, wone_ref[m], precision=lax.Precision.HIGHEST, preferred_element_type=f32
        )
        full = 0.5 * jnp.concatenate([eff, self_emb_ref[m], jnp.zeros((4, LATENT), f32)], axis=0)
        hi, lo = halves(full)
        weff_ref[m] = padded_rows([hi, hi, lo], 128)
        hi, lo = hi[0:32], lo[0:32]
        wback_ref[m, :, 0:LATENT] = padded_rows([hi, lo], 128)
        wback_ref[m, :, LATENT:] = padded_rows([hi], 128)
        hi, lo = halves(wr2_ref[m])
        dst_ref[m, 3 * LATENT :] = padded_rows([0.5 * hi, 0.5 * hi, 0.5 * lo], 128)
        wr2b_ref[m, :, 0:LATENT] = padded_rows([hi, lo], 128)
        wr2b_ref[m, :, LATENT:] = padded_rows([hi], 128)
    large[1].wait()
    for m in range(MEMBERS):
        stack_rows(src_ref, m, 0.5 * wsrc_ref[m])
        stack_columns(srct_ref, m, wsrc_ref[m])
    large[2].wait()
    for m in range(MEMBERS):
        stack_rows(dst_ref, m, 0.5 * wdst_ref[m])
        stack_columns(dstt_ref, m, wdst_ref[m])
    large[3].wait()
    for m in range(MEMBERS):
        readout = wout_ref[m : m + 1, :] * (0.25 / MEMBERS)
        stack_rows(edge_ref, m, 0.5 * wedge_ref[m])
        stack_columns(eout_ref, m, wedge_ref[m] * readout)


def geometry_kernel(own_ref, g0, g1, g2, g3, send_ref, at_ref, live_ref, b_ref, geo_ref, basis_ref, o0, o1, o2, o3):
    own = own_ref[...]
    rows = lax.broadcasted_iota(jnp.int32, (8, OWN), 0)
    pieces = [own]
    px, mx, py, my = by_side((g0, g1, g2, g3))
    for piece, row, by in ((mx, 0, -box_side), (px, 0, box_side), (my, 1, -box_side), (py, 1, box_side)):
        pieces.append(piece + jnp.where(rows == row, by, 0.0))
    ext = jnp.concatenate(pieces, axis=1)
    there = unstacked3(mm(stacked3(ext, 32), at_ref[...]), 8)
    centres = centre_step * lax.broadcasted_iota(jnp.int32, (RADIAL, OWN), 0).astype(f32)
    sums = [jnp.zeros((RADIAL, OWN), f32) for _ in range(SPECIES)]
    for s in range(SLOTS):
        other = there[:, s * OWN : (s + 1) * OWN]
        sep = other - own
        square = sep[0:1] * sep[0:1] + sep[1:2] * sep[1:2] + sep[2:3] * sep[2:3]
        distance = jnp.sqrt(square + soft_square)
        scaled = (distance - centres) / basis_width
        basis = jnp.exp(-scaled * scaled)
        basis_ref[:, s * OWN : (s + 1) * OWN] = basis
        geo_ref[:, s * OWN : (s + 1) * OWN] = jnp.where(
            rows == 4, distance, jnp.where(rows < 3, sep, other)
        )
        kind = other[3:4]
        alive = live_ref[s : s + 1, :]
        for sp in range(SPECIES):
            sums[sp] = sums[sp] + basis * jnp.where(kind == float(sp), alive, 0.0)
    flags = jnp.where(rows.astype(f32) == own[3:4], 1.0, 0.0)
    b_own = jnp.concatenate(sums + [flags], axis=0)
    b_ref[...] = b_own
    stacked = stacked3(b_own, OWN)
    for out, index in zip((o0, o1, o2, o3), by_partner(*lists_of(send_ref))):
        out[...] = unstacked3(mm(stacked, one_hot(OWN, index)), FEATS)


def silu_parts(half):
    above = 1.0 + jnp.tanh(half)
    value = half * above
    return value, above + value * (2.0 - above)


def tripled(x):
    hi, lo = split2(x)
    return jnp.concatenate([hi, lo, hi], axis=1)


def main_kernel(
    b0,
    b1,
    b2,
    b3,
    b4,
    basis_ref,
    a_ref,
    alive_ref,
    weff_ref,
    wback_ref,
    wr2b_ref,
    src_ref,
    dst_ref,
    edge_ref,
    srct_ref,
    dstt_ref,
    eout_ref,
    c0,
    c1,
    c2,
    c3,
    c4,
    ctb_out,
    xb,
    xe,
    bs,
    ctb,
    acc,
    acc_own,
):
    px, mx, py, my = by_side((b1, b2, b3, b4))
    for n, full in enumerate((b0[...], mx, px, my, py)):
        hi, lo = halves(full)
        tall = jnp.concatenate([hi, lo, hi, jnp.zeros((8, OWN), f32)], axis=0)
        xb[n * OWN : (n + 1) * OWN, :] = jnp.transpose(tall).astype(bf16)
    for s in range(SLOTS):
        hi, lo = halves(basis_ref[:, s * OWN : (s + 1) * OWN])
        tall = jnp.concatenate([hi, lo, hi, jnp.zeros((104, OWN), f32)], axis=0)
        bs[s * OWN : (s + 1) * OWN, :] = jnp.transpose(tall).astype(bf16)
    xe[...] = mm(a_ref[...], xb[...]).astype(bf16)
    ctb[...] = jnp.zeros_like(ctb)
    acc[...] = jnp.zeros_like(acc)
    acc_own[...] = jnp.zeros_like(acc_own)

    for m in range(MEMBERS):
        own_hid, own_slope = silu_parts(mm(xb[0:OWN, :], weff_ref[m]))
        centre = mm(tripled(own_hid), src_ref[m])
        many = jnp.concatenate([centre] * (STEP // OWN), axis=0)

        def rows_of(t):
            return slice(t * STEP, (t + 1) * STEP)

        def hidden(t, v):
            v["z"] = mm(xe[rows_of(t), :], weff_ref[m])

        def hidden_parts(t, v):
            hid, v["slope"] = silu_parts(v["z"])
            v["wide"] = tripled(hid)

        def pair(t, v):
            v["z"] = mm(v["wide"], dst_ref[m, 0 : 3 * LATENT]) + mm(bs[rows_of(t), :], dst_ref[m, 3 * LATENT :])

        def pair_parts(t, v):
            value, v["dx"] = silu_parts(v["z"] + many)
            v["wide"] = tripled(value)

        def update(t, v):
            v["z"] = mm(v["wide"], edge_ref[m])

        def update_parts(t, v):
            mask = alive_ref[rows_of(t), :]
            v["wide"] = tripled(silu_parts(v["z"])[1] * jnp.concatenate([mask, mask], axis=1))

        def pull_update(t, v):
            v["z"] = mm_nt(v["wide"], eout_ref[m])

        def pull_pair_parts(t, v):
            ct = v["z"] * v["dx"]
            v["sum"] = ct[0:OWN]
            for n in range(1, STEP // OWN):
                v["sum"] = v["sum"] + ct[n * OWN : (n + 1) * OWN]
            v["wide"] = tripled(ct)

        def pull_pair(t, v):
            ctb[rows_of(t), :] += mm_nt(v["wide"][:, 0 : 2 * LATENT], wr2b_ref[m])
            v["z"] = mm_nt(v["wide"], dstt_ref[m])

        def pull_hidden_parts(t, v):
            hi, lo = split2(v["z"] * v["slope"])
            v["wide"] = jnp.concatenate([hi, lo], axis=1)

        def pull_hidden(t, v):
            acc[rows_of(t), :] += mm_nt(v["wide"], wback_ref[m])

        stages = (
            hidden,
            hidden_parts,
            pair,
            pair_parts,
            update,
            update_parts,
            pull_update,
            pull_pair_parts,
            pull_pair,
            pull_hidden_parts,
            pull_hidden,
        )
        tiles = EDGES // STEP
        held = [{} for _ in range(tiles)]
        for tick in range((tiles - 1) * LAG + len(stages)):
            for t in range(tiles):
                stage = tick - t * LAG
                if 0 <= stage < len(stages):
                    stages[stage](t, held[t])
        total = held[0]["sum"]
        for t in range(1, tiles):
            total = total + held[t]["sum"]
        ct_own = mm_nt(tripled(total), srct_ref[m])
        hi, lo = split2(ct_own * own_slope)
        acc_own[...] += mm_nt(jnp.concatenate([hi, lo], axis=1), wback_ref[m])

    tall = []
    for s in range(SLOTS):
        at = slice(s * OWN, (s + 1) * OWN)
        wide = jnp.transpose(ctb[at, :])
        ctb_out[:, at] = wide[0:8] + wide[8:16]
        wide = jnp.transpose(acc[at, :])
        hi, lo = halves(wide[0:32] + wide[32:64])
        tall.append(jnp.concatenate([hi, lo], axis=0).astype(bf16))
    spread = mm(jnp.concatenate(tall, axis=1), a_ref[...])
    spread = spread[0:32] + spread[32:64]
    wide = jnp.transpose(acc_own[...])
    blocks = [spread[:, n * OWN : (n + 1) * OWN] for n in range(5)]
    c0[...] = blocks[0] + wide[0:32] + wide[32:64]
    for ref, block in zip((c1, c2, c3, c4), by_partner(blocks[2], blocks[1], blocks[4], blocks[3])):
        ref[...] = block


def collected(pieces, send_ref, rows):
    total = None
    for piece, index in zip(pieces, by_partner(*lists_of(send_ref))):
        got = unstacked3(
            mm_nt(stacked3(piece[...], -(-3 * rows // 16) * 16), one_hot(OWN, index)), rows
        )
        total = got if total is None else total + got
    return total


def push_kernel(own_ct, r0, r1, r2, r3, send_ref, basis_ref, geo_ref, live_ref, ctb_ref, a_ref, own_out, o0, o1, o2, o3):
    ct = own_ct[...] + collected((r0, r1, r2, r3), send_ref, 32)
    rows = lax.broadcasted_iota(jnp.int32, (8, OWN), 0)
    centres = centre_step * lax.broadcasted_iota(jnp.int32, (RADIAL, OWN), 0).astype(f32)
    pulled = jnp.zeros((8, OWN), f32)
    seps = []
    for s in range(SLOTS):
        at = slice(s * OWN, (s + 1) * OWN)
        geo = geo_ref[:, at]
        kind = geo[3:4]
        picked = ctb_ref[:, at]
        for sp in range(SPECIES):
            picked = picked + jnp.where(kind == float(sp), ct[sp * 8 : sp * 8 + 8], 0.0)
        distance = geo[4:5]
        slope = picked * basis_ref[:, at] * (distance - centres)
        ct_d = jnp.sum(slope, axis=0, keepdims=True) * (-2.0 / (basis_width * basis_width))
        ct_sep = jnp.where(rows < 3, geo * (ct_d * live_ref[s : s + 1, :] / distance), 0.0)
        pulled = pulled - ct_sep
        seps.append(ct_sep)
    all_sep = jnp.concatenate(seps, axis=1)
    spread = unstacked3(mm(stacked3(all_sep, 32), a_ref[...]), 8)
    own_out[...] = spread[:, 0:OWN] + pulled
    blocks = [spread[:, n * OWN : (n + 1) * OWN] for n in range(5)]
    for out, block in zip((o0, o1, o2, o3), by_partner(blocks[2], blocks[1], blocks[4], blocks[3])):
        out[...] = block


def finish_kernel(own_ct, r0, r1, r2, r3, send_ref, pos_ref, vel_ref, spec_ref, mass_ref, pos_out, vel_out):
    ct = own_ct[...] + collected((r0, r1, r2, r3), send_ref, 8)
    spec = spec_ref[...]
    scale = jnp.zeros(spec.shape, f32)
    for sp in range(SPECIES):
        scale = scale + jnp.where(spec == sp, mass_ref[sp], 0.0)
    vel = vel_ref[...] - time_step * scale * ct[0:3]
    vel_out[...] = vel
    pos_out[...] = pos_ref[...] + time_step * vel


def swapped(shard, axis, first):
    peers = lax.axis_size(axis)
    pairs = []
    for i in range(first, peers + first, 2):
        pairs += [(i % peers, (i + 1) % peers), ((i + 1) % peers, i % peers)]
    return lax.ppermute(shard, axis, pairs)


def exchanged(four):
    return (
        swapped(four[0], "gx", 1),
        swapped(four[1], "gx", 0),
        swapped(four[2], "gy", 1),
        swapped(four[3], "gy", 0),
    )


def like(*shape):
    return jax.ShapeDtypeStruct(shape, f32)


def like16(*shape):
    return jax.ShapeDtypeStruct(shape, bf16)


def run_picks(neighbours, counts):
    return pl.pallas_call(
        picks_kernel,
        out_shape=[
            like16(EDGES, EXT),
            like16(EXT, EDGES),
            like(SLOTS, OWN),
            like(EDGES, OWN),
        ],
        in_specs=hbm(2),
        out_specs=vmem(4),
        scratch_shapes=[
            pltpu.VMEM((SLOTS, OWN), jnp.int32),
            pltpu.VMEM((1, OWN), jnp.int32),
            pltpu.SemaphoreType.DMA((2,)),
        ],
        compiler_params=params(12),
        cost_estimate=pl.CostEstimate(flops=4_000_000_000, bytes_accessed=16_000_000, transcendentals=0),
        name="picks",
    )(neighbours, counts[None, :])


def run_weights(after, *given):
    return pl.pallas_call(
        weights_kernel,
        out_shape=[
            like16(MEMBERS, 128, LATENT),
            like16(MEMBERS, 128, 2 * LATENT),
            like16(MEMBERS, 128, 2 * LATENT),
            like16(MEMBERS, 3 * LATENT, LATENT),
            like16(MEMBERS, 3 * LATENT + 128, LATENT),
            like16(MEMBERS, 3 * LATENT, LATENT),
        ]
        + [like16(MEMBERS, LATENT, 3 * LATENT)] * 3,
        in_specs=hbm(10),
        out_specs=vmem(9),
        scratch_shapes=[
            pltpu.VMEM((MEMBERS, RADIAL, LATENT), f32),
            pltpu.VMEM((MEMBERS, SPECIES, LATENT), f32),
            pltpu.VMEM((MEMBERS, SPECIES, LATENT), f32),
            pltpu.VMEM((MEMBERS, RADIAL, LATENT), f32),
            pltpu.VMEM((MEMBERS, LATENT), f32),
        ]
        + [pltpu.VMEM((MEMBERS, LATENT, LATENT), f32)] * 4
        + [pltpu.SemaphoreType.DMA((5,)), pltpu.SemaphoreType.DMA((4,))],
        compiler_params=params(20),
        cost_estimate=pl.CostEstimate(flops=4_000_000_000, bytes_accessed=16_000_000, transcendentals=0),
        name="weights",
    )(after, *given)


def run_members(sums, basis, a, alive, weights):
    return pl.pallas_call(
        main_kernel,
        out_shape=[like(32, OWN)] * 5 + [like(8, EDGES)],
        in_specs=vmem(17),
        out_specs=vmem(6),
        scratch_shapes=[
            pltpu.VMEM((EXT, 128), bf16),
            pltpu.VMEM((EDGES, 128), bf16),
            pltpu.VMEM((EDGES, 128), bf16),
            pltpu.VMEM((EDGES, 128), f32),
            pltpu.VMEM((EDGES, 128), f32),
            pltpu.VMEM((OWN, 128), f32),
        ],
        compiler_params=params(40),
        name="members",
    )(*sums, basis, a, alive, *weights)


def shards(
    positions,
    velocities,
    species,
    counts,
    neighbours,
    send_lists,
    inv_mass,
    w_rad_one,
    emb_nbr,
    emb_self,
    w_one,
    w_src,
    w_dst,
    w_rad_two,
    w_edge,
    w_out,
):
    spec = species[None, :]
    own, *packed = pl.pallas_call(
        pack_kernel,
        out_shape=[like(8, OWN)] * 5,
        in_specs=hbm(3),
        out_specs=vmem(5),
        scratch_shapes=[
            pltpu.VMEM((3, OWN), f32),
            pltpu.VMEM((1, OWN), jnp.int32),
            pltpu.VMEM((4, OWN // 2), jnp.int32),
            pltpu.SemaphoreType.DMA((3,)),
        ],
        compiler_params=params(4),
        name="pack",
    )(positions, spec, send_lists)
    ghosts = exchanged(packed)
    a, at, live, alive = run_picks(neighbours, counts)
    b_own, geo, basis, *b_packed = pl.pallas_call(
        geometry_kernel,
        out_shape=[like(FEATS, OWN), like(8, EDGES), like(8, EDGES)] + [like(FEATS, OWN)] * 4,
        in_specs=vmem(8),
        out_specs=vmem(7),
        compiler_params=params(12),
        name="geometry",
    )(own, *ghosts, send_lists, at, live)
    b_ghosts = exchanged(b_packed)
    weights = run_weights(
        b_own, w_rad_one, emb_nbr, emb_self, w_rad_two, w_out, w_one, w_src, w_dst, w_edge
    )
    *cts, ctb = run_members([b_own, *b_ghosts], basis, a, alive, weights)
    back = exchanged(cts[1:])
    own_ct, *outgoing = pl.pallas_call(
        push_kernel,
        out_shape=[like(8, OWN)] * 5,
        in_specs=vmem(11),
        out_specs=vmem(5),
        compiler_params=params(12),
        name="push",
    )(cts[0], *back, send_lists, basis, geo, live, ctb, a)
    last = exchanged(outgoing)
    new_positions, new_velocities = pl.pallas_call(
        finish_kernel,
        out_shape=[like(3, OWN), like(3, OWN)],
        in_specs=vmem(9) + [pl.BlockSpec(memory_space=pltpu.SMEM)],
        out_specs=vmem(2),
        compiler_params=params(4),
        name="finish",
    )(own_ct, *last, send_lists, positions, velocities, spec, inv_mass)
    return (new_positions, new_velocities)


def solution(mesh):
    split = P(None, ("gx", "gy"))
    row = P(("gx", "gy"))
    placed = (split, split, row, row, split, split) + (P(),) * 10
    return jax.shard_map(
        shards, mesh=mesh, in_specs=placed, out_specs=(split, split), check_vma=False
    )
```

time: 113 us -> 70.4 us (0.62)
  the two profiles are of different devices: /device:TPU:1 before, /device:TPU:0 now
where the time goes in v2:
time: 70.4 us; the launch traced here: 69.1 us
  Pallas kernels  27.3 us (39%)
  starting transfers between devices  24.7 us (35%)
  waiting for transfers between devices  12.8 us (18%)
  local copies, waits for them, and re-layouts  3.44 us (5%)
  between operations  0.88 us (1%)
    ppermute x16, starting transfers between devices, swapped(): return lax.ppermute(shard, axis, pairs)  24.7 us
    pallas_call x1, Pallas kernels, run_members(): pl.pallas_call(main_kernel, out_shape=[like(32, OWN)] * 5 + [like(8, EDGE...  20.1 us
    ppermute x16, waiting for transfers between devices, swapped(): return lax.ppermute(shard, axis, pairs)  12.8 us
    unnamed x38, local copies, waits for them, and re-layouts  3.44 us
    pallas_call x1, Pallas kernels, run_weights(): pl.pallas_call(weights_kernel, out_shape=[like16(MEMBERS, 128, LATENT), l...  2.69 us
  transfers between devices with their start and end apart: 16, of which 5 were waited for; matrix products, arithmetic and copies ran while one was open for 0% of the time, Pallas kernels for 6%

profile of v2, /device:TPU:0, one launch (start us, length us, event | category | flops | bytes accessed | tf_op | source)
XLA Modules:
  0.0 69.1 jit_solution(13018116082127309670)
XLA Ops:
  0.6 0.0 copy-start
  0.6 0.7 copy-done
  1.3 0.7 copy-done.2
  2.0 0.7 copy-done.4
  2.7 0.3 pack.1
  2.9 9.0 %collective-permute-start = (f32[8,128]{1,0:T(8,128)S(1)}, f32[8,128]{1,0:T(8,128)S(1)}, u32[]{:S(2)}, u32[]{:S(2)}) collective-permute-start(f32[8,128]{1,0:T(8,128)S(1)} %get-tuple-element.39), channel_id=1, source_target_pairs={{4,8},{8,4},{12,16},{16,12},{20,24},{24,20},{28,32},{32,28},{36,40... | collective-permute-start | bytes 12296 | tf_op jit(solution)/shard_map/ppermute | solution.py:488
  12.0 0.0 collective-permute-start.1
  12.0 0.0 collective-permute-start.2
  12.0 0.8 %collective-permute-start.3 = (f32[8,128]{1,0:T(8,128)S(1)}, f32[8,128]{1,0:T(8,128)S(1)}, u32[]{:S(2)}, u32[]{:S(2)}) collective-permute-start(f32[8,128]{1,0:T(8,128)S(1)} %get-tuple-element.42), channel_id=1, source_target_pairs={{0,1},{1,0},{2,3},{3,2},{4,5},{5,4},{6,7},{7,6},{8,9},{9,8},{10,11... | collective-permute-start | bytes 12296 | tf_op jit(solution)/shard_map/ppermute | solution.py:488
  12.8 0.7 %copy-done.16 = s32[12,128]{1,0:T(8,128)S(1)} copy-done((s32[12,128]{1,0:T(8,128)S(1)}, s32[12,128]{1,0:T(8,128)}, u32[]{:S(2)}) %copy-start.16) | copy-done | bytes 6168
  13.4 0.7 copy-done.18
  14.1 1.4 %picks.1 = (bf16[1536,640]{1,0:T(8,128)(2,1)S(1)}, bf16[640,1536]{1,0:T(8,128)(2,1)S(1)}, f32[12,128]{1,0:T(8,128)S(1)}, f32[1536,128]{1,0:T(8,128)S(1)}) custom-call(s32[12,128]{1,0:T(8,128)S(1)} %copy-done.16, s32[1,128]{1,0:T(1,128)S(1)} %bitcast.4), custom_call_target="tpu_custom_call" | custom-call | flops 4000000000 | bytes 16000000 | tf_op jit(solution)/shard_map/picks/pallas_call | solution.py:509
  15.5 0.0 copy-start.8
  15.5 0.0 copy-start.12
  15.5 0.0 copy-start.13
  15.5 0.0 copy-start.14
  15.5 0.0 copy-start.15
  15.5 0.0 copy-start.17
  15.5 0.0 collective-permute-done.g0
  15.6 1.5 %collective-permute-done.1.g1 = f32[8,128]{1,0:T(8,128)S(1)} collective-permute-done((f32[8,128]{1,0:T(8,128)S(1)}, f32[8,128]{1,0:T(8,128)S(1)}, u32[]{:S(2)}, u32[]{:S(2)}) %collective-permute-start.1) | collective-permute-done | bytes 4128 | tf_op jit(solution)/shard_map/ppermute | solution.py:488
  17.1 0.0 collective-permute-done.2.g2
  17.1 0.0 collective-permute-done.3.g3
  17.1 0.0 copy-done.1
  17.1 0.6 geometry.1
  17.7 4.3 %collective-permute-start.4 = (f32[40,128]{1,0:T(8,128)S(1)}, f32[40,128]{1,0:T(8,128)S(1)}, u32[]{:S(2)}, u32[]{:S(2)}) collective-permute-start(f32[40,128]{1,0:T(8,128)S(1)} %get-tuple-element.46), channel_id=1, source_target_pairs={{4,8},{8,4},{12,16},{16,12},{20,24},{24,20},{28,32},{32,28},{36,40... | collective-permute-start | bytes 61448 | tf_op jit(solution)/shard_map/ppermute | solution.py:488
  22.0 0.0 collective-permute-start.5
  22.0 0.0 collective-permute-start.6
  22.0 0.8 %collective-permute-start.7 = (f32[40,128]{1,0:T(8,128)S(1)}, f32[40,128]{1,0:T(8,128)S(1)}, u32[]{:S(2)}, u32[]{:S(2)}) collective-permute-start(f32[40,128]{1,0:T(8,128)S(1)} %get-tuple-element.49), channel_id=1, source_target_pairs={{0,1},{1,0},{2,3},{3,2},{4,5},{5,4},{6,7},{7,6},{8,9},{9,8},{10,11... | collective-permute-start | bytes 61448 | tf_op jit(solution)/shard_map/ppermute | solution.py:488
  22.8 0.0 copy-done.9
  22.8 0.0 copy-done.10
  22.8 0.0 copy-done.11
  22.8 0.0 copy-done.8
  22.9 0.0 copy-done.12
  22.9 0.0 copy-done.13
  22.9 0.0 copy-done.14
  22.9 0.0 copy-done.15
  22.9 2.7 %weights.1 = (bf16[4,128,256]{2,1,0:T(8,128)(2,1)S(1)}, bf16[4,128,512]{2,1,0:T(8,128)(2,1)S(1)}, bf16[4,128,512]{2,1,0:T(8,128)(2,1)S(1)}, bf16[4,768,256]{2,1,...) custom-call(f32[40,128]{1,0:T(8,128)S(1)} %get-tuple-element.45.afte, ...), custom_call_target="tpu_custom_call" | custom-call | flops 4000000000 | bytes 16000000 | tf_op jit(solution)/shard_map/weights/pallas_call | solution.py:531
  25.6 1.7 %collective-permute-done.4.b1 = f32[40,128]{1,0:T(8,128)S(1)} collective-permute-done((f32[40,128]{1,0:T(8,128)S(1)}, f32[40,128]{1,0:T(8,128)S(1)}, u32[]{:S(2)}, u32[]{:S(2)}) %collective-permute-start.4) | collective-permute-done | bytes 20512 | tf_op jit(solution)/shard_map/ppermute | solution.py:488
  27.3 0.2 collective-permute-done.5.b2
  27.5 0.0 collective-permute-done.6.b3
  27.5 0.0 collective-permute-done.7.b4
  27.5 20.1 %members.1 = (f32[32,128]{1,0:T(8,128)S(1)}, f32[32,128]{1,0:T(8,128)S(1)}, f32[32,128]{1,0:T(8,128)S(1)}, f32[32,128]{1,0:T(8,128)S(1)}, f32[32,128]{1,0:T(8,128)S(1)}, /*index=5*/f32[8,1536]{1,0:T(8,128)S(1)}) custom-call(f32[40,128]{1,0:T(8,128)S(1)} %get-tuple-element.45.after_hbm.b0, f32[40,128]{1,0:T(8,128)S(1)} %collective-permute-done.4.b1, ...), custom_call_target="tpu_custom_call" | custom-call | tf_op jit(solution)/shard_map/members/pallas_call | solution.py:560
  47.7 0.0 copy-start.3
  47.7 0.0 copy-start.5
  47.7 0.0 copy-start.6
  47.7 0.0 copy-start.7
  47.7 4.1 %collective-permute-start.8 = (f32[32,128]{1,0:T(8,128)S(1)}, f32[32,128]{1,0:T(8,128)S(1)}, u32[]{:S(2)}, u32[]{:S(2)}) collective-permute-start(f32[32,128]{1,0:T(8,128)S(1)} %get-tuple-element.63), channel_id=1, source_target_pairs={{4,8},{8,4},{12,16},{16,12},{20,24},{24,20},{28,32},{32,28},{36,40... | collective-permute-start | bytes 49160 | tf_op jit(solution)/shard_map/ppermute | solution.py:488
  51.9 0.0 collective-permute-start.9
  51.9 0.0 collective-permute-start.10
  51.9 0.8 %collective-permute-start.11 = (f32[32,128]{1,0:T(8,128)S(1)}, f32[32,128]{1,0:T(8,128)S(1)}, u32[]{:S(2)}, u32[]{:S(2)}) collective-permute-start(f32[32,128]{1,0:T(8,128)S(1)} %get-tuple-element.66), channel_id=1, source_target_pairs={{0,1},{1,0},{2,3},{3,2},{4,5},{5,4},{6,7},{7,6},{8,9},{9,8},{10,11... | collective-permute-start | bytes 49160 | tf_op jit(solution)/shard_map/ppermute | solution.py:488
  52.7 4.7 %collective-permute-done.8.r0 = f32[32,128]{1,0:T(8,128)S(1)} collective-permute-done((f32[32,128]{1,0:T(8,128)S(1)}, f32[32,128]{1,0:T(8,128)S(1)}, u32[]{:S(2)}, u32[]{:S(2)}) %collective-permute-start.8) | collective-permute-done | bytes 16416 | tf_op jit(solution)/shard_map/ppermute | solution.py:488
  57.4 0.0 collective-permute-done.9.r1
  57.4 0.0 collective-permute-done.10.r2
  57.4 0.0 collective-permute-done.11.r3
  57.4 0.8 %push.1 = (f32[8,128]{1,0:T(8,128)S(1)}, f32[8,128]{1,0:T(8,128)S(1)}, f32[8,128]{1,0:T(8,128)S(1)}, f32[8,128]{1,0:T(8,128)S(1)}, f32[8,128]{1,0:T(8,128)S(1)}) custom-call(f32[32,128]{1,0:T(8,128)S(1)} %get-tuple-element.62.own_ct, f32[32,128]{1,0:T(8,128)S(1)} %collective-permute-done.8.r0, f32[32,128]{1,0:T(8,128)S(1)} %collective-permute-done.9.r1, ...), custom_call_target="tpu_custom_call" | custom-call | tf_op jit(solution)/shard_map/push/pallas_call | solution.py:627
  58.2 4.0 %collective-permute-start.12 = (f32[8,128]{1,0:T(8,128)S(1)}, f32[8,128]{1,0:T(8,128)S(1)}, u32[]{:S(2)}, u32[]{:S(2)}) collective-permute-start(f32[8,128]{1,0:T(8,128)S(1)} %get-tuple-element.70), channel_id=1, source_target_pairs={{4,8},{8,4},{12,16},{16,12},{20,24},{24,20},{28,32},{32,28},{36,40... | collective-permute-start | bytes 12296 | tf_op jit(solution)/shard_map/ppermute | solution.py:488
  62.3 0.0 collective-permute-start.13
  62.3 0.0 collective-permute-start.14
  62.3 0.8 %collective-permute-start.15 = (f32[8,128]{1,0:T(8,128)S(1)}, f32[8,128]{1,0:T(8,128)S(1)}, u32[]{:S(2)}, u32[]{:S(2)}) collective-permute-start(f32[8,128]{1,0:T(8,128)S(1)} %get-tuple-element.73), channel_id=1, source_target_pairs={{0,1},{1,0},{2,3},{3,2},{4,5},{5,4},{6,7},{7,6},{8,9},{9,8},{10,11... | collective-permute-start | bytes 12296 | tf_op jit(solution)/shard_map/ppermute | solution.py:488
  63.1 4.5 %collective-permute-done.12.r0 = f32[8,128]{1,0:T(8,128)S(1)} collective-permute-done((f32[8,128]{1,0:T(8,128)S(1)}, f32[8,128]{1,0:T(8,128)S(1)}, u32[]{:S(2)}, u32[]{:S(2)}) %collective-permute-start.12) | collective-permute-done | bytes 4128 | tf_op jit(solution)/shard_map/ppermute | solution.py:488
  67.7 0.0 collective-permute-done.13.r1
  67.7 0.0 collective-permute-done.14.r2
  67.7 0.0 collective-permute-done.15.r3
  67.7 1.4 %finish.1 = (f32[3,128]{1,0:T(4,128)}, f32[3,128]{1,0:T(4,128)}) custom-call(f32[8,128]{1,0:T(8,128)S(1)} %get-tuple-element.69.own_ct, f32[8,128]{1,0:T(8,128)S(1)} %collective-permute-done.12.r0, f32[8,128]{1,0:T(8,128)S(1)} %collective-permute-done.13.r1, f32[8,128]{1,0:T(8,128)S(1)} %collective-permute-done.14.r2, ...), custom_call_target="tpu_custom_call" | custom-call | tf_op jit(solution)/shard_map/finish/pallas_call | solution.py:636
  (13 shorter events, 0.0 us)
Async XLA Ops:
  0.6 0.7 copy-start
  1.3 0.7 copy-start.2
  2.0 0.7 copy-start.4
  2.9 12.6 %collective-permute-start = (f32[8,128]{1,0:T(8,128)S(1)}, f32[8,128]{1,0:T(8,128)S(1)}, u32[]{:S(2)}, u32[]{:S(2)}) collective-permute-start(f32[8,128]{1,0:T(8,128)S(1)} %get-tuple-element.39), channel_id=1, source_target_pairs={{4,8},{8,4},{12,16},{16,12},{20,24},{24,20},{28,32},{32,28},{36,40... | collective-permute-start | bytes 12296 | tf_op jit(solution)/shard_map/ppermute | solution.py:488
  12.0 5.1 %collective-permute-start.1 = (f32[8,128]{1,0:T(8,128)S(1)}, f32[8,128]{1,0:T(8,128)S(1)}, u32[]{:S(2)}, u32[]{:S(2)}) collective-permute-start(f32[8,128]{1,0:T(8,128)S(1)} %get-tuple-element.40), channel_id=1, source_target_pairs={{0,4},{4,0},{8,12},{12,8},{16,20},{20,16},{24,28},{28,24},{32,36},... | collective-permute-start | bytes 12296 | tf_op jit(solution)/shard_map/ppermute | solution.py:488
  12.0 5.1 %collective-permute-start.2 = (f32[8,128]{1,0:T(8,128)S(1)}, f32[8,128]{1,0:T(8,128)S(1)}, u32[]{:S(2)}, u32[]{:S(2)}) collective-permute-start(f32[8,128]{1,0:T(8,128)S(1)} %get-tuple-element.41), channel_id=1, source_target_pairs={{1,2},{2,1},{3,0},{0,3},{5,6},{6,5},{7,4},{4,7},{9,10},{10,9},{11,... | collective-permute-start | bytes 12296 | tf_op jit(solution)/shard_map/ppermute | solution.py:488
  12.0 5.1 %collective-permute-start.3 = (f32[8,128]{1,0:T(8,128)S(1)}, f32[8,128]{1,0:T(8,128)S(1)}, u32[]{:S(2)}, u32[]{:S(2)}) collective-permute-start(f32[8,128]{1,0:T(8,128)S(1)} %get-tuple-element.42), channel_id=1, source_target_pairs={{0,1},{1,0},{2,3},{3,2},{4,5},{5,4},{6,7},{7,6},{8,9},{9,8},{10,11... | collective-permute-start | bytes 12296 | tf_op jit(solution)/shard_map/ppermute | solution.py:488
  12.7 0.7 %copy-start.16 = (s32[12,128]{1,0:T(8,128)S(1)}, s32[12,128]{1,0:T(8,128)}, u32[]{:S(2)}) copy-start(s32[12,128]{1,0:T(8,128)} %nbr_hbm.1) | copy-start | bytes 18436
  13.4 0.7 copy-start.18
  14.1 3.0 %copy-start.1 = (s32[4,64]{1,0:T(4,128)S(1)}, s32[4,64]{1,0:T(4,128)}, u32[]{:S(2)}) copy-start(s32[4,64]{1,0:T(4,128)} %send_ref.5) | copy-start | bytes 3076
  14.1 8.7 %copy-start.9 = (f32[4,256,256]{2,1,0:T(8,128)S(1)}, f32[4,256,256]{2,1,0:T(8,128)}, u32[]{:S(2)}) copy-start(f32[4,256,256]{2,1,0:T(8,128)} %wsrc_hbm.1) | copy-start | bytes 3145732
  14.1 8.7 %copy-start.10 = (f32[4,256,256]{2,1,0:T(8,128)S(1)}, f32[4,256,256]{2,1,0:T(8,128)}, u32[]{:S(2)}) copy-start(f32[4,256,256]{2,1,0:T(8,128)} %wdst_hbm.1) | copy-start | bytes 3145732
  14.1 8.7 %copy-start.11 = (f32[4,256,256]{2,1,0:T(8,128)S(1)}, f32[4,256,256]{2,1,0:T(8,128)}, u32[]{:S(2)}) copy-start(f32[4,256,256]{2,1,0:T(8,128)} %wedge_hbm.1) | copy-start | bytes 3145732
  15.5 7.4 %copy-start.8 = (f32[4,256,256]{2,1,0:T(8,128)S(1)}, f32[4,256,256]{2,1,0:T(8,128)}, u32[]{:S(2)}) copy-start(f32[4,256,256]{2,1,0:T(8,128)} %wone_hbm.1) | copy-start | bytes 3145732
  15.5 7.4 %copy-start.12 = (f32[4,8,256]{2,1,0:T(8,128)S(1)}, f32[4,8,256]{2,1,0:T(8,128)}, u32[]{:S(2)}) copy-start(f32[4,8,256]{2,1,0:T(8,128)} %wr1_hbm.1) | copy-start | bytes 98308
  15.5 7.4 %copy-start.13 = (f32[4,8,256]{2,1,0:T(8,128)S(1)}, f32[4,8,256]{2,1,0:T(8,128)}, u32[]{:S(2)}) copy-start(f32[4,8,256]{2,1,0:T(8,128)} %wr2_hbm.1) | copy-start | bytes 98308
  15.5 7.4 %copy-start.14 = (f32[4,4,256]{2,1,0:T(4,128)S(1)}, f32[4,4,256]{2,1,0:T(4,128)}, u32[]{:S(2)}) copy-start(f32[4,4,256]{2,1,0:T(4,128)} %nbr_emb_hbm.1) | copy-start | bytes 49156
  15.5 7.4 %copy-start.15 = (f32[4,4,256]{2,1,0:T(4,128)S(1)}, f32[4,4,256]{2,1,0:T(4,128)}, u32[]{:S(2)}) copy-start(f32[4,4,256]{2,1,0:T(4,128)} %self_emb_hbm.1) | copy-start | bytes 49156
  15.5 7.4 %copy-start.17 = (f32[4,256]{1,0:T(4,128)S(1)}, f32[4,256]{1,0:T(4,128)}, u32[]{:S(2)}) copy-start(f32[4,256]{1,0:T(4,128)} %wout_hbm.1) | copy-start | bytes 12292
  17.7 9.6 %collective-permute-start.4 = (f32[40,128]{1,0:T(8,128)S(1)}, f32[40,128]{1,0:T(8,128)S(1)}, u32[]{:S(2)}, u32[]{:S(2)}) collective-permute-start(f32[40,128]{1,0:T(8,128)S(1)} %get-tuple-element.46), channel_id=1, source_target_pairs={{4,8},{8,4},{12,16},{16,12},{20,24},{24,20},{28,32},{32,28},{36,40... | collective-permute-start | bytes 61448 | tf_op jit(solution)/shard_map/ppermute | solution.py:488
  22.0 5.5 %collective-permute-start.5 = (f32[40,128]{1,0:T(8,128)S(1)}, f32[40,128]{1,0:T(8,128)S(1)}, u32[]{:S(2)}, u32[]{:S(2)}) collective-permute-start(f32[40,128]{1,0:T(8,128)S(1)} %get-tuple-element.47), channel_id=1, source_target_pairs={{0,4},{4,0},{8,12},{12,8},{16,20},{20,16},{24,28},{28,24},{32,36},... | collective-permute-start | bytes 61448 | tf_op jit(solution)/shard_map/ppermute | solution.py:488
  22.0 5.5 %collective-permute-start.6 = (f32[40,128]{1,0:T(8,128)S(1)}, f32[40,128]{1,0:T(8,128)S(1)}, u32[]{:S(2)}, u32[]{:S(2)}) collective-permute-start(f32[40,128]{1,0:T(8,128)S(1)} %get-tuple-element.48), channel_id=1, source_target_pairs={{1,2},{2,1},{3,0},{0,3},{5,6},{6,5},{7,4},{4,7},{9,10},{10,9},{11,... | collective-permute-start | bytes 61448 | tf_op jit(solution)/shard_map/ppermute | solution.py:488
  22.0 5.5 %collective-permute-start.7 = (f32[40,128]{1,0:T(8,128)S(1)}, f32[40,128]{1,0:T(8,128)S(1)}, u32[]{:S(2)}, u32[]{:S(2)}) collective-permute-start(f32[40,128]{1,0:T(8,128)S(1)} %get-tuple-element.49), channel_id=1, source_target_pairs={{0,1},{1,0},{2,3},{3,2},{4,5},{5,4},{6,7},{7,6},{8,9},{9,8},{10,11... | collective-permute-start | bytes 61448 | tf_op jit(solution)/shard_map/ppermute | solution.py:488
  47.7 20.0 %copy-start.3 = (f32[3,128]{1,0:T(4,128)S(1)}, f32[3,128]{1,0:T(4,128)}, u32[]{:S(2)}) copy-start(f32[3,128]{1,0:T(4,128)} %pos_ref.1) | copy-start | bytes 4612
  47.7 20.0 %copy-start.5 = (s32[128]{0:T(128)S(1)}, s32[128]{0:T(128)}, u32[]{:S(2)}) copy-start(s32[128]{0:T(128)} %param.18) | copy-start | bytes 1540
  47.7 20.0 %copy-start.6 = (f32[3,128]{1,0:T(4,128)S(1)}, f32[3,128]{1,0:T(4,128)}, u32[]{:S(2)}) copy-start(f32[3,128]{1,0:T(4,128)} %vel_ref.1) | copy-start | bytes 4612
  47.7 20.0 %copy-start.7 = (f32[4]{0:T(128)S(1)}, f32[4]{0:T(128)}, u32[]{:S(2)}) copy-start(f32[4]{0:T(128)} %mass_ref.1) | copy-start | bytes 52
  47.7 9.7 %collective-permute-start.8 = (f32[32,128]{1,0:T(8,128)S(1)}, f32[32,128]{1,0:T(8,128)S(1)}, u32[]{:S(2)}, u32[]{:S(2)}) collective-permute-start(f32[32,128]{1,0:T(8,128)S(1)} %get-tuple-element.63), channel_id=1, source_target_pairs={{4,8},{8,4},{12,16},{16,12},{20,24},{24,20},{28,32},{32,28},{36,40... | collective-permute-start | bytes 49160 | tf_op jit(solution)/shard_map/ppermute | solution.py:488
  51.9 5.5 %collective-permute-start.9 = (f32[32,128]{1,0:T(8,128)S(1)}, f32[32,128]{1,0:T(8,128)S(1)}, u32[]{:S(2)}, u32[]{:S(2)}) collective-permute-start(f32[32,128]{1,0:T(8,128)S(1)} %get-tuple-element.64), channel_id=1, source_target_pairs={{0,4},{4,0},{8,12},{12,8},{16,20},{20,16},{24,28},{28,24},{32,36},... | collective-permute-start | bytes 49160 | tf_op jit(solution)/shard_map/ppermute | solution.py:488
  51.9 5.5 %collective-permute-start.10 = (f32[32,128]{1,0:T(8,128)S(1)}, f32[32,128]{1,0:T(8,128)S(1)}, u32[]{:S(2)}, u32[]{:S(2)}) collective-permute-start(f32[32,128]{1,0:T(8,128)S(1)} %get-tuple-element.65), channel_id=1, source_target_pairs={{1,2},{2,1},{3,0},{0,3},{5,6},{6,5},{7,4},{4,7},{9,10},{10,9},{11,... | collective-permute-start | bytes 49160 | tf_op jit(solution)/shard_map/ppermute | solution.py:488
  51.9 5.5 %collective-permute-start.11 = (f32[32,128]{1,0:T(8,128)S(1)}, f32[32,128]{1,0:T(8,128)S(1)}, u32[]{:S(2)}, u32[]{:S(2)}) collective-permute-start(f32[32,128]{1,0:T(8,128)S(1)} %get-tuple-element.66), channel_id=1, source_target_pairs={{0,1},{1,0},{2,3},{3,2},{4,5},{5,4},{6,7},{7,6},{8,9},{9,8},{10,11... | collective-permute-start | bytes 49160 | tf_op jit(solution)/shard_map/ppermute | solution.py:488
  58.2 9.4 %collective-permute-start.12 = (f32[8,128]{1,0:T(8,128)S(1)}, f32[8,128]{1,0:T(8,128)S(1)}, u32[]{:S(2)}, u32[]{:S(2)}) collective-permute-start(f32[8,128]{1,0:T(8,128)S(1)} %get-tuple-element.70), channel_id=1, source_target_pairs={{4,8},{8,4},{12,16},{16,12},{20,24},{24,20},{28,32},{32,28},{36,40... | collective-permute-start | bytes 12296 | tf_op jit(solution)/shard_map/ppermute | solution.py:488
  62.3 5.4 %collective-permute-start.13 = (f32[8,128]{1,0:T(8,128)S(1)}, f32[8,128]{1,0:T(8,128)S(1)}, u32[]{:S(2)}, u32[]{:S(2)}) collective-permute-start(f32[8,128]{1,0:T(8,128)S(1)} %get-tuple-element.71), channel_id=1, source_target_pairs={{0,4},{4,0},{8,12},{12,8},{16,20},{20,16},{24,28},{28,24},{32,36},... | collective-permute-start | bytes 12296 | tf_op jit(solution)/shard_map/ppermute | solution.py:488
  62.3 5.4 %collective-permute-start.14 = (f32[8,128]{1,0:T(8,128)S(1)}, f32[8,128]{1,0:T(8,128)S(1)}, u32[]{:S(2)}, u32[]{:S(2)}) collective-permute-start(f32[8,128]{1,0:T(8,128)S(1)} %get-tuple-element.72), channel_id=1, source_target_pairs={{1,2},{2,1},{3,0},{0,3},{5,6},{6,5},{7,4},{4,7},{9,10},{10,9},{11,... | collective-permute-start | bytes 12296 | tf_op jit(solution)/shard_map/ppermute | solution.py:488
  62.3 5.4 %collective-permute-start.15 = (f32[8,128]{1,0:T(8,128)S(1)}, f32[8,128]{1,0:T(8,128)S(1)}, u32[]{:S(2)}, u32[]{:S(2)}) collective-permute-start(f32[8,128]{1,0:T(8,128)S(1)} %get-tuple-element.73), channel_id=1, source_target_pairs={{0,1},{1,0},{2,3},{3,2},{4,5},{5,4},{6,7},{7,6},{8,9},{9,8},{10,11... | collective-permute-start | bytes 12296 | tf_op jit(solution)/shard_map/ppermute | solution.py:488

commit v3 on v2

--- a/solution.py
+++ b/solution.py
@@ -16,6 +16,7 @@
 MEMBERS = 4
 STEP = 256
 LAG = 1
+MEMBERS_MIB = 32
 
 box_side = 4.0
 soft_square = 0.25
@@ -31,10 +32,6 @@
 
 def vmem(count):
     return [pl.BlockSpec(memory_space=pltpu.VMEM)] * count
-
-
-def hbm(count):
-    return [pl.BlockSpec(memory_space=pltpu.HBM)] * count
 
 
 def params(mib):
@@ -111,16 +108,14 @@
     )
 
 
-def fetched(given, kept, sems):
+def pack_kernel(pos_hbm, spec_hbm, send_hbm, own_ref, o0, o1, o2, o3, pos_ref, spec_ref, send_ref, sems):
     copies = []
-    for n, (source, target) in enumerate(zip(given, kept)):
-        copies.append(pltpu.make_async_copy(source, target, sems.at[n]))
+    for n, (given, kept) in enumerate(
+        ((pos_hbm, pos_ref), (spec_hbm, spec_ref), (send_hbm, send_ref))
+    ):
+        copies.append(pltpu.make_async_copy(given, kept, sems.at[n]))
         copies[-1].start()
-    return copies
-
-
-def pack_kernel(pos_hbm, spec_hbm, send_hbm, own_ref, o0, o1, o2, o3, pos_ref, spec_ref, send_ref, sems):
-    for copy in fetched((pos_hbm, spec_hbm, send_hbm), (pos_ref, spec_ref, send_ref), sems):
+    for copy in copies:
         copy.wait()
     own = jnp.concatenate(
         [pos_ref[...], spec_ref[...].astype(f32), jnp.zeros((4, OWN), f32)], axis=0
@@ -155,9 +150,18 @@
     ref[m, :, 2 * LATENT :] = lo
 
 
-def picks_kernel(nbr_hbm, counts_hbm, a_ref, at_ref, live_ref, alive_ref, nbr_ref, counts_ref, sems):
-    for copy in fetched((nbr_hbm, counts_hbm), (nbr_ref, counts_ref), sems):
-        copy.wait()
+def silu_parts(half):
+    above = 1.0 + jnp.tanh(half)
+    value = half * above
+    return value, above + value * (2.0 - above)
+
+
+def tripled(x):
+    hi, lo = split2(x)
+    return jnp.concatenate([hi, lo, hi], axis=1)
+
+
+def picks_kernel(nbr_ref, counts_ref, a_ref, at_ref, live_ref, alive_ref):
     slot_ids = lax.broadcasted_iota(jnp.int32, (SLOTS, OWN), 0)
     live = (slot_ids < counts_ref[...]).astype(f32)
     live_ref[...] = live
@@ -174,25 +178,8 @@
 
 
 def weights_kernel(
-    after_hbm,
-    wr1_hbm,
-    nbr_emb_hbm,
-    self_emb_hbm,
-    wr2_hbm,
-    wout_hbm,
-    wone_hbm,
-    wsrc_hbm,
-    wdst_hbm,
-    wedge_hbm,
-    weff_ref,
-    wback_ref,
-    wr2b_ref,
-    src_ref,
-    dst_ref,
-    edge_ref,
-    srct_ref,
-    dstt_ref,
-    eout_ref,
+    b_ref,
+    basis_ref,
     wr1_ref,
     nbr_emb_ref,
     self_emb_ref,
@@ -202,20 +189,27 @@
     wsrc_ref,
     wdst_ref,
     wedge_ref,
-    sems,
-    large_sems,
+    xb_ref,
+    bs_ref,
+    slope_ref,
+    centre_ref,
+    weff_ref,
+    dst_ref,
+    edge_ref,
+    dstt_ref,
+    eout_ref,
+    wback_ref,
+    wr2b_ref,
+    srct_ref,
 ):
-    small = fetched(
-        (wr1_hbm, nbr_emb_hbm, self_emb_hbm, wr2_hbm, wout_hbm),
-        (wr1_ref, nbr_emb_ref, self_emb_ref, wr2_ref, wout_ref),
-        sems,
-    )
-    large = fetched(
-        (wone_hbm, wsrc_hbm, wdst_hbm, wedge_hbm), (wone_ref, wsrc_ref, wdst_ref, wedge_ref), large_sems
-    )
-    for copy in small:
-        copy.wait()
-    large[0].wait()
+    hi, lo = halves(b_ref[...])
+    tall = jnp.concatenate([hi, lo, hi, jnp.zeros((8, OWN), f32)], axis=0)
+    xb = jnp.transpose(tall).astype(bf16)
+    xb_ref[...] = xb
+    for s in range(SLOTS):
+        hi, lo = halves(basis_ref[:, s * OWN : (s + 1) * OWN])
+        tall = jnp.concatenate([hi, lo, hi, jnp.zeros((104, OWN), f32)], axis=0)
+        bs_ref[s * OWN : (s + 1) * OWN, :] = jnp.transpose(tall).astype(bf16)
     for m in range(MEMBERS):
         mixed = jnp.concatenate(
             [wr1_ref[m] * nbr_emb_ref[m, sp : sp + 1, :] for sp in range(SPECIES)], axis=0
@@ -225,24 +219,21 @@
         )
         full = 0.5 * jnp.concatenate([eff, self_emb_ref[m], jnp.zeros((4, LATENT), f32)], axis=0)
         hi, lo = halves(full)
-        weff_ref[m] = padded_rows([hi, hi, lo], 128)
+        weff = padded_rows([hi, hi, lo], 128)
+        weff_ref[m] = weff
         hi, lo = hi[0:32], lo[0:32]
         wback_ref[m, :, 0:LATENT] = padded_rows([hi, lo], 128)
         wback_ref[m, :, LATENT:] = padded_rows([hi], 128)
         hi, lo = halves(wr2_ref[m])
         dst_ref[m, 3 * LATENT :] = padded_rows([0.5 * hi, 0.5 * hi, 0.5 * lo], 128)
-        wr2b_ref[m, :, 0:LATENT] = padded_rows([hi, lo], 128)
-        wr2b_ref[m, :, LATENT:] = padded_rows([hi], 128)
-    large[1].wait()
-    for m in range(MEMBERS):
-        stack_rows(src_ref, m, 0.5 * wsrc_ref[m])
+        wr2b_ref[:, 2 * m * LATENT : (2 * m + 1) * LATENT] = padded_rows([hi, lo], 128)
+        wr2b_ref[:, (2 * m + 1) * LATENT : (2 * m + 2) * LATENT] = padded_rows([hi], 128)
+        hid, slope_ref[m] = silu_parts(mm(xb, weff))
+        hi, lo = split2(0.5 * wsrc_ref[m])
+        centre_ref[m] = mm(tripled(hid), jnp.concatenate([hi, hi, lo], axis=0))
         stack_columns(srct_ref, m, wsrc_ref[m])
-    large[2].wait()
-    for m in range(MEMBERS):
         stack_rows(dst_ref, m, 0.5 * wdst_ref[m])
         stack_columns(dstt_ref, m, wdst_ref[m])
-    large[3].wait()
-    for m in range(MEMBERS):
         readout = wout_ref[m : m + 1, :] * (0.25 / MEMBERS)
         stack_rows(edge_ref, m, 0.5 * wedge_ref[m])
         stack_columns(eout_ref, m, wedge_ref[m] * readout)
@@ -282,154 +273,138 @@
         out[...] = unstacked3(mm(stacked, one_hot(OWN, index)), FEATS)
 
 
-def silu_parts(half):
-    above = 1.0 + jnp.tanh(half)
-    value = half * above
-    return value, above + value * (2.0 - above)
-
-
-def tripled(x):
-    hi, lo = split2(x)
-    return jnp.concatenate([hi, lo, hi], axis=1)
-
-
 def main_kernel(
-    b0,
     b1,
     b2,
     b3,
     b4,
-    basis_ref,
     a_ref,
     alive_ref,
+    xb_own,
+    bs,
+    centre_ref,
     weff_ref,
-    wback_ref,
-    wr2b_ref,
-    src_ref,
     dst_ref,
     edge_ref,
-    srct_ref,
     dstt_ref,
     eout_ref,
+    wback_ref,
     c0,
     c1,
     c2,
     c3,
     c4,
-    ctb_out,
+    cx_ref,
+    sum_ref,
     xb,
     xe,
-    bs,
-    ctb,
     acc,
-    acc_own,
 ):
     px, mx, py, my = by_side((b1, b2, b3, b4))
-    for n, full in enumerate((b0[...], mx, px, my, py)):
+    xb[0:OWN, :] = xb_own[...]
+    for n, full in enumerate((mx, px, my, py)):
         hi, lo = halves(full)
         tall = jnp.concatenate([hi, lo, hi, jnp.zeros((8, OWN), f32)], axis=0)
-        xb[n * OWN : (n + 1) * OWN, :] = jnp.transpose(tall).astype(bf16)
+        xb[(n + 1) * OWN : (n + 2) * OWN, :] = jnp.transpose(tall).astype(bf16)
+    xe[...] = mm(a_ref[...], xb[...]).astype(bf16)
+    acc[...] = jnp.zeros_like(acc)
+
+    def rows_of(t):
+        return slice(t * STEP, (t + 1) * STEP)
+
+    def hidden(m, t, v):
+        v["z"] = mm(xe[rows_of(t), :], weff_ref[m])
+
+    def hidden_parts(m, t, v):
+        hid, v["slope"] = silu_parts(v["z"])
+        v["wide"] = tripled(hid)
+
+    def pair(m, t, v):
+        v["z"] = mm(v["wide"], dst_ref[m, 0 : 3 * LATENT]) + mm(bs[rows_of(t), :], dst_ref[m, 3 * LATENT :])
+
+    def pair_parts(m, t, v):
+        value, v["dx"] = silu_parts(v["z"] + jnp.concatenate([centre_ref[m]] * (STEP // OWN), axis=0))
+        v["wide"] = tripled(value)
+
+    def update(m, t, v):
+        v["z"] = mm(v["wide"], edge_ref[m])
+
+    def update_parts(m, t, v):
+        mask = alive_ref[rows_of(t), :]
+        v["wide"] = tripled(silu_parts(v["z"])[1] * jnp.concatenate([mask, mask], axis=1))
+
+    def pull_update(m, t, v):
+        v["z"] = mm_nt(v["wide"], eout_ref[m])
+
+    def pull_pair_parts(m, t, v):
+        ct = v["z"] * v["dx"]
+        v["sum"] = ct[0:OWN]
+        for n in range(1, STEP // OWN):
+            v["sum"] = v["sum"] + ct[n * OWN : (n + 1) * OWN]
+        v["wide"] = tripled(ct)
+
+    def pull_pair(m, t, v):
+        cx_ref[rows_of(t), 2 * m * LATENT : (2 * m + 2) * LATENT] = v["wide"][:, 0 : 2 * LATENT]
+        v["z"] = mm_nt(v["wide"], dstt_ref[m])
+
+    def pull_hidden_parts(m, t, v):
+        hi, lo = split2(v["z"] * v["slope"])
+        v["wide"] = jnp.concatenate([hi, lo], axis=1)
+
+    def pull_hidden(m, t, v):
+        acc[rows_of(t), :] += mm_nt(v["wide"], wback_ref[m])
+
+    stages = (
+        hidden,
+        hidden_parts,
+        pair,
+        pair_parts,
+        update,
+        update_parts,
+        pull_update,
+        pull_pair_parts,
+        pull_pair,
+        pull_hidden_parts,
+        pull_hidden,
+    )
+    tiles = EDGES // STEP
+    chains = [(m, t, {}) for m in range(MEMBERS) for t in range(tiles)]
+    for tick in range((len(chains) - 1) * LAG + len(stages)):
+        for number, chain in enumerate(chains):
+            stage = tick - number * LAG
+            if 0 <= stage < len(stages):
+                stages[stage](*chain)
+    for m in range(MEMBERS):
+        total = chains[m * tiles][2]["sum"]
+        for t in range(1, tiles):
+            total = total + chains[m * tiles + t][2]["sum"]
+        sum_ref[m] = total
+
+    tall = []
     for s in range(SLOTS):
-        hi, lo = halves(basis_ref[:, s * OWN : (s + 1) * OWN])
-        tall = jnp.concatenate([hi, lo, hi, jnp.zeros((104, OWN), f32)], axis=0)
-        bs[s * OWN : (s + 1) * OWN, :] = jnp.transpose(tall).astype(bf16)
-    xe[...] = mm(a_ref[...], xb[...]).astype(bf16)
-    ctb[...] = jnp.zeros_like(ctb)
-    acc[...] = jnp.zeros_like(acc)
-    acc_own[...] = jnp.zeros_like(acc_own)
-
+        wide = jnp.transpose(acc[s * OWN : (s + 1) * OWN, :])
+        hi, lo = halves(wide[0:32] + wide[32:64])
+        tall.append(jnp.concatenate([hi, lo], axis=0).astype(bf16))
+    spread = mm(jnp.concatenate(tall, axis=1), a_ref[...])
+    spread = spread[0:32] + spread[32:64]
+    blocks = [spread[:, n * OWN : (n + 1) * OWN] for n in range(5)]
+    c0[...] = blocks[0]
+    for ref, block in zip((c1, c2, c3, c4), by_partner(blocks[2], blocks[1], blocks[4], blocks[3])):
+        ref[...] = block
+
+
+def centre_kernel(c0, cx_ref, sum_ref, slope_ref, srct_ref, wback_ref, wr2b_ref, own_out, ctb_out):
+    total = jnp.zeros((OWN, 128), f32)
     for m in range(MEMBERS):
-        own_hid, own_slope = silu_parts(mm(xb[0:OWN, :], weff_ref[m]))
-        centre = mm(tripled(own_hid), src_ref[m])
-        many = jnp.concatenate([centre] * (STEP // OWN), axis=0)
-
-        def rows_of(t):
-            return slice(t * STEP, (t + 1) * STEP)
-
-        def hidden(t, v):
-            v["z"] = mm(xe[rows_of(t), :], weff_ref[m])
-
-        def hidden_parts(t, v):
-            hid, v["slope"] = silu_parts(v["z"])
-            v["wide"] = tripled(hid)
-
-        def pair(t, v):
-            v["z"] = mm(v["wide"], dst_ref[m, 0 : 3 * LATENT]) + mm(bs[rows_of(t), :], dst_ref[m, 3 * LATENT :])
-
-        def pair_parts(t, v):
-            value, v["dx"] = silu_parts(v["z"] + many)
-            v["wide"] = tripled(value)
-
-        def update(t, v):
-            v["z"] = mm(v["wide"], edge_ref[m])
-
-        def update_parts(t, v):
-            mask = alive_ref[rows_of(t), :]
-            v["wide"] = tripled(silu_parts(v["z"])[1] * jnp.concatenate([mask, mask], axis=1))
-
-        def pull_update(t, v):
-            v["z"] = mm_nt(v["wide"], eout_ref[m])
-
-        def pull_pair_parts(t, v):
-            ct = v["z"] * v["dx"]
-            v["sum"] = ct[0:OWN]
-            for n in range(1, STEP // OWN):
-                v["sum"] = v["sum"] + ct[n * OWN : (n + 1) * OWN]
-            v["wide"] = tripled(ct)
-
-        def pull_pair(t, v):
-            ctb[rows_of(t), :] += mm_nt(v["wide"][:, 0 : 2 * LATENT], wr2b_ref[m])
-            v["z"] = mm_nt(v["wide"], dstt_ref[m])
-
-        def pull_hidden_parts(t, v):
-            hi, lo = split2(v["z"] * v["slope"])
-            v["wide"] = jnp.concatenate([hi, lo], axis=1)
-
-        def pull_hidden(t, v):
-            acc[rows_of(t), :] += mm_nt(v["wide"], wback_ref[m])
-
-        stages = (
-            hidden,
-            hidden_parts,
-            pair,
-            pair_parts,
-            update,
-            update_parts,
-            pull_update,
-            pull_pair_parts,
-            pull_pair,
-            pull_hidden_parts,
-            pull_hidden,
-        )
-        tiles = EDGES // STEP
-        held = [{} for _ in range(tiles)]
-        for tick in range((tiles - 1) * LAG + len(stages)):
-            for t in range(tiles):
-                stage = tick - t * LAG
-                if 0 <= stage < len(stages):
-                    stages[stage](t, held[t])
-        total = held[0]["sum"]
-        for t in range(1, tiles):
-            total = total + held[t]["sum"]
-        ct_own = mm_nt(tripled(total), srct_ref[m])
-        hi, lo = split2(ct_own * own_slope)
-        acc_own[...] += mm_nt(jnp.concatenate([hi, lo], axis=1), wback_ref[m])
-
-    tall = []
+        hi, lo = split2(mm_nt(tripled(sum_ref[m]), srct_ref[m]) * slope_ref[m])
+        total = total + mm_nt(jnp.concatenate([hi, lo], axis=1), wback_ref[m])
+    wide = jnp.transpose(total)
+    own_out[...] = c0[...] + wide[0:32] + wide[32:64]
+    ctb = mm_nt(cx_ref[...], wr2b_ref[...])
     for s in range(SLOTS):
         at = slice(s * OWN, (s + 1) * OWN)
         wide = jnp.transpose(ctb[at, :])
         ctb_out[:, at] = wide[0:8] + wide[8:16]
-        wide = jnp.transpose(acc[at, :])
-        hi, lo = halves(wide[0:32] + wide[32:64])
-        tall.append(jnp.concatenate([hi, lo], axis=0).astype(bf16))
-    spread = mm(jnp.concatenate(tall, axis=1), a_ref[...])
-    spread = spread[0:32] + spread[32:64]
-    wide = jnp.transpose(acc_own[...])
-    blocks = [spread[:, n * OWN : (n + 1) * OWN] for n in range(5)]
-    c0[...] = blocks[0] + wide[0:32] + wide[32:64]
-    for ref, block in zip((c1, c2, c3, c4), by_partner(blocks[2], blocks[1], blocks[4], blocks[3])):
-        ref[...] = block
 
 
 def collected(pieces, send_ref, rows):
@@ -514,65 +489,66 @@
             like(SLOTS, OWN),
             like(EDGES, OWN),
         ],
-        in_specs=hbm(2),
+        in_specs=vmem(2),
         out_specs=vmem(4),
-        scratch_shapes=[
-            pltpu.VMEM((SLOTS, OWN), jnp.int32),
-            pltpu.VMEM((1, OWN), jnp.int32),
-            pltpu.SemaphoreType.DMA((2,)),
-        ],
         compiler_params=params(12),
         cost_estimate=pl.CostEstimate(flops=4_000_000_000, bytes_accessed=16_000_000, transcendentals=0),
         name="picks",
     )(neighbours, counts[None, :])
 
 
-def run_weights(after, *given):
+def run_weights(*given):
     return pl.pallas_call(
         weights_kernel,
         out_shape=[
+            like16(OWN, 128),
+            like16(EDGES, 128),
+            like(MEMBERS, OWN, LATENT),
+            like(MEMBERS, OWN, LATENT),
             like16(MEMBERS, 128, LATENT),
-            like16(MEMBERS, 128, 2 * LATENT),
-            like16(MEMBERS, 128, 2 * LATENT),
-            like16(MEMBERS, 3 * LATENT, LATENT),
             like16(MEMBERS, 3 * LATENT + 128, LATENT),
             like16(MEMBERS, 3 * LATENT, LATENT),
-        ]
-        + [like16(MEMBERS, LATENT, 3 * LATENT)] * 3,
-        in_specs=hbm(10),
-        out_specs=vmem(9),
-        scratch_shapes=[
-            pltpu.VMEM((MEMBERS, RADIAL, LATENT), f32),
-            pltpu.VMEM((MEMBERS, SPECIES, LATENT), f32),
-            pltpu.VMEM((MEMBERS, SPECIES, LATENT), f32),
-            pltpu.VMEM((MEMBERS, RADIAL, LATENT), f32),
-            pltpu.VMEM((MEMBERS, LATENT), f32),
-        ]
-        + [pltpu.VMEM((MEMBERS, LATENT, LATENT), f32)] * 4
-        + [pltpu.SemaphoreType.DMA((5,)), pltpu.SemaphoreType.DMA((4,))],
-        compiler_params=params(20),
+            like16(MEMBERS, LATENT, 3 * LATENT),
+            like16(MEMBERS, LATENT, 3 * LATENT),
+            like16(MEMBERS, 128, 2 * LATENT),
+            like16(128, 2 * MEMBERS * LATENT),
+            like16(MEMBERS, LATENT, 3 * LATENT),
+        ],
+        in_specs=vmem(11),
+        out_specs=vmem(12),
+        compiler_params=params(12),
         cost_estimate=pl.CostEstimate(flops=4_000_000_000, bytes_accessed=16_000_000, transcendentals=0),
         name="weights",
-    )(after, *given)
-
-
-def run_members(sums, basis, a, alive, weights):
+    )(*given)
+
+
+def run_members(*given):
     return pl.pallas_call(
         main_kernel,
-        out_shape=[like(32, OWN)] * 5 + [like(8, EDGES)],
-        in_specs=vmem(17),
-        out_specs=vmem(6),
+        out_shape=[like(32, OWN)] * 5
+        + [like16(EDGES, 2 * MEMBERS * LATENT), like(MEMBERS, OWN, LATENT)],
+        in_specs=vmem(15),
+        out_specs=vmem(7),
         scratch_shapes=[
             pltpu.VMEM((EXT, 128), bf16),
             pltpu.VMEM((EDGES, 128), bf16),
-            pltpu.VMEM((EDGES, 128), bf16),
             pltpu.VMEM((EDGES, 128), f32),
-            pltpu.VMEM((EDGES, 128), f32),
-            pltpu.VMEM((OWN, 128), f32),
         ],
-        compiler_params=params(40),
+        compiler_params=params(MEMBERS_MIB),
         name="members",
-    )(*sums, basis, a, alive, *weights)
+    )(*given)
+
+
+def run_centre(*given):
+    return pl.pallas_call(
+        centre_kernel,
+        out_shape=[like(32, OWN), like(8, EDGES)],
+        in_specs=vmem(7),
+        out_specs=vmem(2),
+        compiler_params=params(16),
+        cost_estimate=pl.CostEstimate(flops=3_000_000_000, bytes_accessed=16_000_000, transcendentals=0),
+        name="centre",
+    )(*given)
 
 
 def shards(
@@ -597,7 +573,7 @@
     own, *packed = pl.pallas_call(
         pack_kernel,
         out_shape=[like(8, OWN)] * 5,
-        in_specs=hbm(3),
+        in_specs=[pl.BlockSpec(memory_space=pl.ANY)] * 3,
         out_specs=vmem(5),
         scratch_shapes=[
             pltpu.VMEM((3, OWN), f32),
@@ -605,7 +581,7 @@
             pltpu.VMEM((4, OWN // 2), jnp.int32),
             pltpu.SemaphoreType.DMA((3,)),
         ],
-        compiler_params=params(4),
+        compiler_params=params(60),
         name="pack",
     )(positions, spec, send_lists)
     ghosts = exchanged(packed)
@@ -619,11 +595,12 @@
         name="geometry",
     )(own, *ghosts, send_lists, at, live)
     b_ghosts = exchanged(b_packed)
-    weights = run_weights(
-        b_own, w_rad_one, emb_nbr, emb_self, w_rad_two, w_out, w_one, w_src, w_dst, w_edge
+    xb, bs, slope, centre, *maps, wback, wr2b, srct = run_weights(
+        b_own, basis, w_rad_one, emb_nbr, emb_self, w_rad_two, w_out, w_one, w_src, w_dst, w_edge
     )
-    *cts, ctb = run_members([b_own, *b_ghosts], basis, a, alive, weights)
+    *cts, cx, sums = run_members(*b_ghosts, a, alive, xb, bs, centre, *maps, wback)
     back = exchanged(cts[1:])
+    own_sums, ctb = run_centre(cts[0], cx, sums, slope, srct, wback, wr2b)
     own_ct, *outgoing = pl.pallas_call(
         push_kernel,
         out_shape=[like(8, OWN)] * 5,
@@ -631,7 +608,7 @@
         out_specs=vmem(5),
         compiler_params=params(12),
         name="push",
-    )(cts[0], *back, send_lists, basis, geo, live, ctb, a)
+    )(own_sums, *back, send_lists, basis, geo, live, ctb, a)
     last = exchanged(outgoing)
     new_positions, new_velocities = pl.pallas_call(
         finish_kernel,

time: 70.4 us -> 66.2 us (0.940)
  waiting for transfers between devices: 12.8 us -> 9.27 us
  local copies, waits for them, and re-layouts: 3.44 us -> 1.43 us
  Pallas kernels: 27.3 us -> 28.7 us
    ppermute x16, waiting for transfers between devices: 12.8 us -> 9.27 us  [swapped(): return lax.ppermute(shard, axis, pairs)]
    unnamed x38 -> x34, local copies, waits for them, and re-layouts: 3.44 us -> 1.43 us
    pallas_call x3 -> x4, Pallas kernels: 23.1 us -> 24.5 us  [the longest x1 16.5 us: run_members(): pl.pallas_call(main_kernel, out_shape=[like(32, OWN)] * 5 + [like16(EDGES...]
  transfers between devices with their start and end apart: 16 -> 16, of which waited for: 5 -> 5; matrix products, arithmetic and copies ran while one was open for 0% -> 0% of each run, Pallas kernels for 6% -> 12%
where the time goes in v3:
time: 66.2 us; the launch traced here: 64.9 us
  Pallas kernels  28.7 us (43%)
  starting transfers between devices  24.7 us (37%)
  waiting for transfers between devices  9.27 us (14%)
  local copies, waits for them, and re-layouts  1.43 us (2%)
  between operations  0.88 us (1%)
    ppermute x16, starting transfers between devices, swapped(): return lax.ppermute(shard, axis, pairs)  24.7 us
    pallas_call x1, Pallas kernels, run_members(): pl.pallas_call(main_kernel, out_shape=[like(32, OWN)] * 5 + [like16(EDGES...  16.5 us
    ppermute x16, waiting for transfers between devices, swapped(): return lax.ppermute(shard, axis, pairs)  9.27 us
    pallas_call x1, Pallas kernels, run_weights(): pl.pallas_call(weights_kernel, out_shape=[like16(OWN, 128), like16(EDGES,...  3.69 us
    pallas_call x1, Pallas kernels, run_centre(): pl.pallas_call(centre_kernel, out_shape=[like(32, OWN), like(8, EDGES)],...  2.69 us
    pallas_call x1, Pallas kernels, shards(): pl.pallas_call(pack_kernel, out_shape=[like(8, OWN)] * 5, in_specs=[pl.Bl...  1.56 us
    unnamed x34, local copies, waits for them, and re-layouts  1.43 us
    pallas_call x1, Pallas kernels, shards(): pl.pallas_call(finish_kernel, out_shape=[like(3, OWN), like(3, OWN)], in_...  1.39 us
  transfers between devices with their start and end apart: 16, of which 5 were waited for; matrix products, arithmetic and copies ran while one was open for 0% of the time, Pallas kernels for 12%

profile of v3, /device:TPU:0, one launch (start us, length us, event | category | flops | bytes accessed | tf_op | source)
XLA Modules:
  0.0 64.9 jit_solution(17740676442012957234)
XLA Ops:
  0.6 1.6 %pack.1 = (f32[8,128]{1,0:T(8,128)}, f32[8,128]{1,0:T(8,128)}, f32[8,128]{1,0:T(8,128)}, f32[8,128]{1,0:T(8,128)}, f32[8,128]{1,0:T(8,128)}) custom-call(f32[3,128]{1,0:T(4,128)} %pos_ref.1, s32[1,128]{1,0:T(1,128)} %bitcast.2, s32[4,64]{1,0:T(4,128)} %send_ref.5), custom_call_target="tpu_custom_call" | custom-call | tf_op jit(solution)/shard_map/pack/pallas_call | solution.py:573
  2.2 9.0 %collective-permute-start = (f32[8,128]{1,0:T(8,128)}, f32[8,128]{1,0:T(8,128)S(1)}, u32[]{:S(2)}, u32[]{:S(2)}) collective-permute-start(f32[8,128]{1,0:T(8,128)} %get-tuple-element.45), channel_id=1, source_target_pairs={{4,8},{8,4},{12,16},{16,12},{20,24},{24,20},{28,32},{32,28},{36,40... | collective-permute-start | bytes 12296 | tf_op jit(solution)/shard_map/ppermute | solution.py:463
  11.2 0.0 collective-permute-start.1
  11.2 0.0 collective-permute-start.2
  11.2 0.8 %collective-permute-start.3 = (f32[8,128]{1,0:T(8,128)}, f32[8,128]{1,0:T(8,128)S(1)}, u32[]{:S(2)}, u32[]{:S(2)}) collective-permute-start(f32[8,128]{1,0:T(8,128)} %get-tuple-element.48), channel_id=1, source_target_pairs={{0,1},{1,0},{2,3},{3,2},{4,5},{5,4},{6,7},{7,6},{8,9},{9,8},{10,11... | collective-permute-start | bytes 12296 | tf_op jit(solution)/shard_map/ppermute | solution.py:463
  12.0 0.7 %copy-done.14 = s32[12,128]{1,0:T(8,128)S(1)} copy-done((s32[12,128]{1,0:T(8,128)S(1)}, s32[12,128]{1,0:T(8,128)}, u32[]{:S(2)}) %copy-start.14) | copy-done | bytes 6168
  12.7 0.7 %copy-done.16 = s32[128]{0:T(128)S(1)} copy-done((s32[128]{0:T(128)S(1)}, s32[128]{0:T(128)}, u32[]{:S(2)}) %copy-start.16) | copy-done | bytes 536
  13.4 0.0 copy-start.9
  13.4 1.3 %picks.1 = (bf16[1536,640]{1,0:T(8,128)(2,1)S(1)}, bf16[640,1536]{1,0:T(8,128)(2,1)S(1)}, f32[12,128]{1,0:T(8,128)S(1)}, f32[1536,128]{1,0:T(8,128)S(1)}) custom-call(s32[12,128]{1,0:T(8,128)S(1)} %copy-done.14, s32[1,128]{1,0:T(1,128)S(1)} %bitcast.4), custom_call_target="tpu_custom_call" | custom-call | flops 4000000000 | bytes 16000000 | tf_op jit(solution)/shard_map/picks/pallas_call | solution.py:484
  14.7 0.0 copy-start.6
  14.7 0.0 copy-start.10
  14.8 0.0 copy-start.11
  14.8 0.0 copy-start.12
  14.8 0.0 copy-start.13
  14.8 0.0 copy-start.15
  14.8 0.0 collective-permute-done.g0
  14.8 1.7 %collective-permute-done.1.g1 = f32[8,128]{1,0:T(8,128)S(1)} collective-permute-done((f32[8,128]{1,0:T(8,128)}, f32[8,128]{1,0:T(8,128)S(1)}, u32[]{:S(2)}, u32[]{:S(2)}) %collective-permute-start.1) | collective-permute-done | bytes 4128 | tf_op jit(solution)/shard_map/ppermute | solution.py:463
  16.6 0.0 collective-permute-done.2.g2
  16.6 0.0 collective-permute-done.3.g3
  16.6 0.0 copy-done
  16.6 0.0 copy-done.2
  16.6 0.6 geometry.1
  17.2 4.3 %collective-permute-start.4 = (f32[40,128]{1,0:T(8,128)S(1)}, f32[40,128]{1,0:T(8,128)S(1)}, u32[]{:S(2)}, u32[]{:S(2)}) collective-permute-start(f32[40,128]{1,0:T(8,128)S(1)} %get-tuple-element.51), channel_id=1, source_target_pairs={{4,8},{8,4},{12,16},{16,12},{20,24},{24,20},{28,32},{32,28},{36,40... | collective-permute-start | bytes 61448 | tf_op jit(solution)/shard_map/ppermute | solution.py:463
  21.5 0.0 collective-permute-start.5
  21.5 0.0 collective-permute-start.6
  21.5 0.8 %collective-permute-start.7 = (f32[40,128]{1,0:T(8,128)S(1)}, f32[40,128]{1,0:T(8,128)S(1)}, u32[]{:S(2)}, u32[]{:S(2)}) collective-permute-start(f32[40,128]{1,0:T(8,128)S(1)} %get-tuple-element.54), channel_id=1, source_target_pairs={{0,1},{1,0},{2,3},{3,2},{4,5},{5,4},{6,7},{7,6},{8,9},{9,8},{10,11... | collective-permute-start | bytes 61448 | tf_op jit(solution)/shard_map/ppermute | solution.py:463
  22.3 0.0 copy-done.7
  22.3 0.0 copy-done.8
  22.3 0.0 copy-done.9
  22.3 0.0 copy-done.6
  22.4 0.0 copy-done.10
  22.4 0.0 copy-done.11
  22.4 0.0 copy-done.12
  22.4 3.7 %weights.1 = (bf16[128,128]{1,0:T(8,128)(2,1)S(1)}, bf16[1536,128]{1,0:T(8,128)(2,1)S(1)}, f32[4,128,256]{2,1,0:T(8,128)S(1)}, f32[4,128,256]{2,1,0:T(8,128)S(1)...) custom-call(f32[40,128]{1,0:T(8,128)S(1)} %get-tuple-element.57.b_re, ...), custom_call_target="tpu_custom_call" | custom-call | flops 4000000000 | bytes 16000000 | tf_op jit(solution)/shard_map/weights/pallas_call | solution.py:501
  26.1 0.7 %collective-permute-done.4.b1 = f32[40,128]{1,0:T(8,128)S(1)} collective-permute-done((f32[40,128]{1,0:T(8,128)S(1)}, f32[40,128]{1,0:T(8,128)S(1)}, u32[]{:S(2)}, u32[]{:S(2)}) %collective-permute-start.4) | collective-permute-done | bytes 20512 | tf_op jit(solution)/shard_map/ppermute | solution.py:463
  26.8 0.2 collective-permute-done.5.b2
  27.0 0.0 collective-permute-done.6.b3
  27.0 0.0 collective-permute-done.7.b4
  27.0 16.5 %members.1 = (f32[32,128]{1,0:T(8,128)S(1)}, f32[32,128]{1,0:T(8,128)S(1)}, f32[32,128]{1,0:T(8,128)S(1)}, f32[32,128]{1,0:T(8,128)S(1)}, f32[32,128]{1,0:T(8,12...) custom-call(f32[40,128]{1,0:T(8,128)S(1)} %collective-permute-done.4.b1, ...), custom_call_target="tpu_custom_call" | custom-call | tf_op jit(solution)/shard_map/members/pallas_call | solution.py:526
  43.6 4.1 %collective-permute-start.8 = (f32[32,128]{1,0:T(8,128)S(1)}, f32[32,128]{1,0:T(8,128)S(1)}, u32[]{:S(2)}, u32[]{:S(2)}) collective-permute-start(f32[32,128]{1,0:T(8,128)S(1)} %get-tuple-element.75), channel_id=1, source_target_pairs={{4,8},{8,4},{12,16},{16,12},{20,24},{24,20},{28,32},{32,28},{36,40... | collective-permute-start | bytes 49160 | tf_op jit(solution)/shard_map/ppermute | solution.py:463
  47.7 0.0 collective-permute-start.9
  47.7 0.0 collective-permute-start.10
  47.7 0.8 %collective-permute-start.11 = (f32[32,128]{1,0:T(8,128)S(1)}, f32[32,128]{1,0:T(8,128)S(1)}, u32[]{:S(2)}, u32[]{:S(2)}) collective-permute-start(f32[32,128]{1,0:T(8,128)S(1)} %get-tuple-element.78), channel_id=1, source_target_pairs={{0,1},{1,0},{2,3},{3,2},{4,5},{5,4},{6,7},{7,6},{8,9},{9,8},{10,11... | collective-permute-start | bytes 49160 | tf_op jit(solution)/shard_map/ppermute | solution.py:463
  48.5 2.7 %centre.1 = (f32[32,128]{1,0:T(8,128)S(1)}, f32[8,1536]{1,0:T(8,128)S(1)}) custom-call(f32[32,128]{1,0:T(8,128)S(1)} %get-tuple-element.68.c0, bf16[1536,2048]{1,0:T(8,128)(2,1)S(1)} %get-tuple-element.69.cx_ref, f32[4,128,256]{2,1,0:T(8,128)S(1)} %get-tuple-element.70.sum_ref, f32[4,128,256]{2,1,0:T(8,128)S(1)} %get-tuple-element.71.slope_ref, ...), custom_call_target="tpu_custom_call" | custom-call | flops 3000000000 | bytes 16000000 | tf_op jit(solution)/shard_map/centre/pallas_call | solution.py:543
  51.2 0.0 copy-start.4
  51.2 0.0 copy-start.5
  51.2 2.0 %collective-permute-done.8.r0 = f32[32,128]{1,0:T(8,128)S(1)} collective-permute-done((f32[32,128]{1,0:T(8,128)S(1)}, f32[32,128]{1,0:T(8,128)S(1)}, u32[]{:S(2)}, u32[]{:S(2)}) %collective-permute-start.8) | collective-permute-done | bytes 16416 | tf_op jit(solution)/shard_map/ppermute | solution.py:463
  53.2 0.0 collective-permute-done.9.r1
  53.3 0.0 collective-permute-done.10.r2
  53.3 0.0 collective-permute-done.11.r3
  53.3 0.8 %push.1 = (f32[8,128]{1,0:T(8,128)S(1)}, f32[8,128]{1,0:T(8,128)S(1)}, f32[8,128]{1,0:T(8,128)S(1)}, f32[8,128]{1,0:T(8,128)S(1)}, f32[8,128]{1,0:T(8,128)S(1)}) custom-call(f32[32,128]{1,0:T(8,128)S(1)} %get-tuple-element.74.own_ct, f32[32,128]{1,0:T(8,128)S(1)} %collective-permute-done.8.r0, f32[32,128]{1,0:T(8,128)S(1)} %collective-permute-done.9.r1, ...), custom_call_target="tpu_custom_call" | custom-call | tf_op jit(solution)/shard_map/push/pallas_call | solution.py:604
  54.1 4.0 %collective-permute-start.12 = (f32[8,128]{1,0:T(8,128)S(1)}, f32[8,128]{1,0:T(8,128)S(1)}, u32[]{:S(2)}, u32[]{:S(2)}) collective-permute-start(f32[8,128]{1,0:T(8,128)S(1)} %get-tuple-element.82), channel_id=1, source_target_pairs={{4,8},{8,4},{12,16},{16,12},{20,24},{24,20},{28,32},{32,28},{36,40... | collective-permute-start | bytes 12296 | tf_op jit(solution)/shard_map/ppermute | solution.py:463
  58.1 0.0 collective-permute-start.13
  58.1 0.0 collective-permute-start.14
  58.1 0.8 %collective-permute-start.15 = (f32[8,128]{1,0:T(8,128)S(1)}, f32[8,128]{1,0:T(8,128)S(1)}, u32[]{:S(2)}, u32[]{:S(2)}) collective-permute-start(f32[8,128]{1,0:T(8,128)S(1)} %get-tuple-element.85), channel_id=1, source_target_pairs={{0,1},{1,0},{2,3},{3,2},{4,5},{5,4},{6,7},{7,6},{8,9},{9,8},{10,11... | collective-permute-start | bytes 12296 | tf_op jit(solution)/shard_map/ppermute | solution.py:463
  58.9 4.6 %collective-permute-done.12.r0 = f32[8,128]{1,0:T(8,128)S(1)} collective-permute-done((f32[8,128]{1,0:T(8,128)S(1)}, f32[8,128]{1,0:T(8,128)S(1)}, u32[]{:S(2)}, u32[]{:S(2)}) %collective-permute-start.12) | collective-permute-done | bytes 4128 | tf_op jit(solution)/shard_map/ppermute | solution.py:463
  63.5 0.0 collective-permute-done.13.r1
  63.5 0.0 collective-permute-done.14.r2
  63.5 0.0 collective-permute-done.15.r3
  63.5 0.0 copy-done.1
  63.5 0.0 copy-done.3
  63.5 0.0 copy-done.4
  63.5 0.0 copy-done.5
  63.6 1.4 %finish.1 = (f32[3,128]{1,0:T(4,128)}, f32[3,128]{1,0:T(4,128)}) custom-call(f32[8,128]{1,0:T(8,128)S(1)} %get-tuple-element.81.own_ct, f32[8,128]{1,0:T(8,128)S(1)} %collective-permute-done.12.r0, f32[8,128]{1,0:T(8,128)S(1)} %collective-permute-done.13.r1, f32[8,128]{1,0:T(8,128)S(1)} %collective-permute-done.14.r2, ...), custom_call_target="tpu_custom_call" | custom-call | tf_op jit(solution)/shard_map/finish/pallas_call | solution.py:613
  (10 shorter events, 0.0 us)
Async XLA Ops:
  2.2 12.6 %collective-permute-start = (f32[8,128]{1,0:T(8,128)}, f32[8,128]{1,0:T(8,128)S(1)}, u32[]{:S(2)}, u32[]{:S(2)}) collective-permute-start(f32[8,128]{1,0:T(8,128)} %get-tuple-element.45), channel_id=1, source_target_pairs={{4,8},{8,4},{12,16},{16,12},{20,24},{24,20},{28,32},{32,28},{36,40... | collective-permute-start | bytes 12296 | tf_op jit(solution)/shard_map/ppermute | solution.py:463
  11.2 5.3 %collective-permute-start.1 = (f32[8,128]{1,0:T(8,128)}, f32[8,128]{1,0:T(8,128)S(1)}, u32[]{:S(2)}, u32[]{:S(2)}) collective-permute-start(f32[8,128]{1,0:T(8,128)} %get-tuple-element.46), channel_id=1, source_target_pairs={{0,4},{4,0},{8,12},{12,8},{16,20},{20,16},{24,28},{28,24},{32,36},... | collective-permute-start | bytes 12296 | tf_op jit(solution)/shard_map/ppermute | solution.py:463
  11.2 5.3 %collective-permute-start.2 = (f32[8,128]{1,0:T(8,128)}, f32[8,128]{1,0:T(8,128)S(1)}, u32[]{:S(2)}, u32[]{:S(2)}) collective-permute-start(f32[8,128]{1,0:T(8,128)} %get-tuple-element.47), channel_id=1, source_target_pairs={{1,2},{2,1},{3,0},{0,3},{5,6},{6,5},{7,4},{4,7},{9,10},{10,9},{11,... | collective-permute-start | bytes 12296 | tf_op jit(solution)/shard_map/ppermute | solution.py:463
  11.2 5.3 %collective-permute-start.3 = (f32[8,128]{1,0:T(8,128)}, f32[8,128]{1,0:T(8,128)S(1)}, u32[]{:S(2)}, u32[]{:S(2)}) collective-permute-start(f32[8,128]{1,0:T(8,128)} %get-tuple-element.48), channel_id=1, source_target_pairs={{0,1},{1,0},{2,3},{3,2},{4,5},{5,4},{6,7},{7,6},{8,9},{9,8},{10,11... | collective-permute-start | bytes 12296 | tf_op jit(solution)/shard_map/ppermute | solution.py:463
  12.0 0.7 %copy-start.14 = (s32[12,128]{1,0:T(8,128)S(1)}, s32[12,128]{1,0:T(8,128)}, u32[]{:S(2)}) copy-start(s32[12,128]{1,0:T(8,128)} %nbr_ref.1) | copy-start | bytes 18436
  12.7 0.7 %copy-start.16 = (s32[128]{0:T(128)S(1)}, s32[128]{0:T(128)}, u32[]{:S(2)}) copy-start(s32[128]{0:T(128)} %param.19) | copy-start | bytes 1540
  13.4 3.2 %copy-start = (s32[4,64]{1,0:T(4,128)S(1)}, s32[4,64]{1,0:T(4,128)}, u32[]{:S(2)}) copy-start(s32[4,64]{1,0:T(4,128)} %send_ref.5) | copy-start | bytes 3076
  13.4 3.2 %copy-start.2 = (f32[8,128]{1,0:T(8,128)S(1)}, f32[8,128]{1,0:T(8,128)}, u32[]{:S(2)}) copy-start(f32[8,128]{1,0:T(8,128)} %get-tuple-element.44.own_ref) | copy-start | bytes 12292
  13.4 9.0 %copy-start.7 = (f32[4,256,256]{2,1,0:T(8,128)S(1)}, f32[4,256,256]{2,1,0:T(8,128)}, u32[]{:S(2)}) copy-start(f32[4,256,256]{2,1,0:T(8,128)} %wsrc_ref.1) | copy-start | bytes 3145732
  13.4 9.0 %copy-start.8 = (f32[4,256,256]{2,1,0:T(8,128)S(1)}, f32[4,256,256]{2,1,0:T(8,128)}, u32[]{:S(2)}) copy-start(f32[4,256,256]{2,1,0:T(8,128)} %wdst_ref.1) | copy-start | bytes 3145732
  13.4 9.0 %copy-start.9 = (f32[4,256,256]{2,1,0:T(8,128)S(1)}, f32[4,256,256]{2,1,0:T(8,128)}, u32[]{:S(2)}) copy-start(f32[4,256,256]{2,1,0:T(8,128)} %wedge_ref.1) | copy-start | bytes 3145732
  14.7 7.6 %copy-start.6 = (f32[4,256,256]{2,1,0:T(8,128)S(1)}, f32[4,256,256]{2,1,0:T(8,128)}, u32[]{:S(2)}) copy-start(f32[4,256,256]{2,1,0:T(8,128)} %wone_ref.1) | copy-start | bytes 3145732
  14.7 7.6 %copy-start.10 = (f32[4,8,256]{2,1,0:T(8,128)S(1)}, f32[4,8,256]{2,1,0:T(8,128)}, u32[]{:S(2)}) copy-start(f32[4,8,256]{2,1,0:T(8,128)} %wr1_ref.1) | copy-start | bytes 98308
  14.8 7.6 %copy-start.11 = (f32[4,8,256]{2,1,0:T(8,128)S(1)}, f32[4,8,256]{2,1,0:T(8,128)}, u32[]{:S(2)}) copy-start(f32[4,8,256]{2,1,0:T(8,128)} %wr2_ref.1) | copy-start | bytes 98308
  14.8 7.6 %copy-start.12 = (f32[4,4,256]{2,1,0:T(4,128)S(1)}, f32[4,4,256]{2,1,0:T(4,128)}, u32[]{:S(2)}) copy-start(f32[4,4,256]{2,1,0:T(4,128)} %nbr_emb_ref.1) | copy-start | bytes 49156
  14.8 7.6 %copy-start.13 = (f32[4,4,256]{2,1,0:T(4,128)S(1)}, f32[4,4,256]{2,1,0:T(4,128)}, u32[]{:S(2)}) copy-start(f32[4,4,256]{2,1,0:T(4,128)} %self_emb_ref.1) | copy-start | bytes 49156
  14.8 7.6 %copy-start.15 = (f32[4,256]{1,0:T(4,128)S(1)}, f32[4,256]{1,0:T(4,128)}, u32[]{:S(2)}) copy-start(f32[4,256]{1,0:T(4,128)} %wout_ref.1) | copy-start | bytes 12292
  17.2 9.6 %collective-permute-start.4 = (f32[40,128]{1,0:T(8,128)S(1)}, f32[40,128]{1,0:T(8,128)S(1)}, u32[]{:S(2)}, u32[]{:S(2)}) collective-permute-start(f32[40,128]{1,0:T(8,128)S(1)} %get-tuple-element.51), channel_id=1, source_target_pairs={{4,8},{8,4},{12,16},{16,12},{20,24},{24,20},{28,32},{32,28},{36,40... | collective-permute-start | bytes 61448 | tf_op jit(solution)/shard_map/ppermute | solution.py:463
  21.5 5.5 %collective-permute-start.5 = (f32[40,128]{1,0:T(8,128)S(1)}, f32[40,128]{1,0:T(8,128)S(1)}, u32[]{:S(2)}, u32[]{:S(2)}) collective-permute-start(f32[40,128]{1,0:T(8,128)S(1)} %get-tuple-element.52), channel_id=1, source_target_pairs={{0,4},{4,0},{8,12},{12,8},{16,20},{20,16},{24,28},{28,24},{32,36},... | collective-permute-start | bytes 61448 | tf_op jit(solution)/shard_map/ppermute | solution.py:463
  21.5 5.5 %collective-permute-start.6 = (f32[40,128]{1,0:T(8,128)S(1)}, f32[40,128]{1,0:T(8,128)S(1)}, u32[]{:S(2)}, u32[]{:S(2)}) collective-permute-start(f32[40,128]{1,0:T(8,128)S(1)} %get-tuple-element.53), channel_id=1, source_target_pairs={{1,2},{2,1},{3,0},{0,3},{5,6},{6,5},{7,4},{4,7},{9,10},{10,9},{11,... | collective-permute-start | bytes 61448 | tf_op jit(solution)/shard_map/ppermute | solution.py:463
  21.5 5.5 %collective-permute-start.7 = (f32[40,128]{1,0:T(8,128)S(1)}, f32[40,128]{1,0:T(8,128)S(1)}, u32[]{:S(2)}, u32[]{:S(2)}) collective-permute-start(f32[40,128]{1,0:T(8,128)S(1)} %get-tuple-element.54), channel_id=1, source_target_pairs={{0,1},{1,0},{2,3},{3,2},{4,5},{5,4},{6,7},{7,6},{8,9},{9,8},{10,11... | collective-permute-start | bytes 61448 | tf_op jit(solution)/shard_map/ppermute | solution.py:463
  43.6 9.7 %collective-permute-start.8 = (f32[32,128]{1,0:T(8,128)S(1)}, f32[32,128]{1,0:T(8,128)S(1)}, u32[]{:S(2)}, u32[]{:S(2)}) collective-permute-start(f32[32,128]{1,0:T(8,128)S(1)} %get-tuple-element.75), channel_id=1, source_target_pairs={{4,8},{8,4},{12,16},{16,12},{20,24},{24,20},{28,32},{32,28},{36,40... | collective-permute-start | bytes 49160 | tf_op jit(solution)/shard_map/ppermute | solution.py:463
  47.7 5.5 %collective-permute-start.9 = (f32[32,128]{1,0:T(8,128)S(1)}, f32[32,128]{1,0:T(8,128)S(1)}, u32[]{:S(2)}, u32[]{:S(2)}) collective-permute-start(f32[32,128]{1,0:T(8,128)S(1)} %get-tuple-element.76), channel_id=1, source_target_pairs={{0,4},{4,0},{8,12},{12,8},{16,20},{20,16},{24,28},{28,24},{32,36},... | collective-permute-start | bytes 49160 | tf_op jit(solution)/shard_map/ppermute | solution.py:463
  47.7 5.5 %collective-permute-start.10 = (f32[32,128]{1,0:T(8,128)S(1)}, f32[32,128]{1,0:T(8,128)S(1)}, u32[]{:S(2)}, u32[]{:S(2)}) collective-permute-start(f32[32,128]{1,0:T(8,128)S(1)} %get-tuple-element.77), channel_id=1, source_target_pairs={{1,2},{2,1},{3,0},{0,3},{5,6},{6,5},{7,4},{4,7},{9,10},{10,9},{11,... | collective-permute-start | bytes 49160 | tf_op jit(solution)/shard_map/ppermute | solution.py:463
  47.7 5.5 %collective-permute-start.11 = (f32[32,128]{1,0:T(8,128)S(1)}, f32[32,128]{1,0:T(8,128)S(1)}, u32[]{:S(2)}, u32[]{:S(2)}) collective-permute-start(f32[32,128]{1,0:T(8,128)S(1)} %get-tuple-element.78), channel_id=1, source_target_pairs={{0,1},{1,0},{2,3},{3,2},{4,5},{5,4},{6,7},{7,6},{8,9},{9,8},{10,11... | collective-permute-start | bytes 49160 | tf_op jit(solution)/shard_map/ppermute | solution.py:463
  51.2 12.3 %copy-start.1 = (f32[3,128]{1,0:T(4,128)S(1)}, f32[3,128]{1,0:T(4,128)}, u32[]{:S(2)}) copy-start(f32[3,128]{1,0:T(4,128)} %pos_ref.1) | copy-start | bytes 4612
  51.2 12.3 %copy-start.3 = (s32[128]{0:T(128)S(1)}, s32[128]{0:T(128)}, u32[]{:S(2)}) copy-start(s32[128]{0:T(128)} %param.18) | copy-start | bytes 1540
  51.2 12.3 %copy-start.4 = (f32[3,128]{1,0:T(4,128)S(1)}, f32[3,128]{1,0:T(4,128)}, u32[]{:S(2)}) copy-start(f32[3,128]{1,0:T(4,128)} %vel_ref.1) | copy-start | bytes 4612
  51.2 12.3 %copy-start.5 = (f32[4]{0:T(128)S(1)}, f32[4]{0:T(128)}, u32[]{:S(2)}) copy-start(f32[4]{0:T(128)} %mass_ref.1) | copy-start | bytes 52
  54.1 9.4 %collective-permute-start.12 = (f32[8,128]{1,0:T(8,128)S(1)}, f32[8,128]{1,0:T(8,128)S(1)}, u32[]{:S(2)}, u32[]{:S(2)}) collective-permute-start(f32[8,128]{1,0:T(8,128)S(1)} %get-tuple-element.82), channel_id=1, source_target_pairs={{4,8},{8,4},{12,16},{16,12},{20,24},{24,20},{28,32},{32,28},{36,40... | collective-permute-start | bytes 12296 | tf_op jit(solution)/shard_map/ppermute | solution.py:463
  58.1 5.4 %collective-permute-start.13 = (f32[8,128]{1,0:T(8,128)S(1)}, f32[8,128]{1,0:T(8,128)S(1)}, u32[]{:S(2)}, u32[]{:S(2)}) collective-permute-start(f32[8,128]{1,0:T(8,128)S(1)} %get-tuple-element.83), channel_id=1, source_target_pairs={{0,4},{4,0},{8,12},{12,8},{16,20},{20,16},{24,28},{28,24},{32,36},... | collective-permute-start | bytes 12296 | tf_op jit(solution)/shard_map/ppermute | solution.py:463
  58.1 5.4 %collective-permute-start.14 = (f32[8,128]{1,0:T(8,128)S(1)}, f32[8,128]{1,0:T(8,128)S(1)}, u32[]{:S(2)}, u32[]{:S(2)}) collective-permute-start(f32[8,128]{1,0:T(8,128)S(1)} %get-tuple-element.84), channel_id=1, source_target_pairs={{1,2},{2,1},{3,0},{0,3},{5,6},{6,5},{7,4},{4,7},{9,10},{10,9},{11,... | collective-permute-start | bytes 12296 | tf_op jit(solution)/shard_map/ppermute | solution.py:463
  58.1 5.4 %collective-permute-start.15 = (f32[8,128]{1,0:T(8,128)S(1)}, f32[8,128]{1,0:T(8,128)S(1)}, u32[]{:S(2)}, u32[]{:S(2)}) collective-permute-start(f32[8,128]{1,0:T(8,128)S(1)} %get-tuple-element.85), channel_id=1, source_target_pairs={{0,1},{1,0},{2,3},{3,2},{4,5},{5,4},{6,7},{7,6},{8,9},{9,8},{10,11... | collective-permute-start | bytes 12296 | tf_op jit(solution)/shard_map/ppermute | solution.py:463

commit v4 on v3

--- a/solution.py
+++ b/solution.py
@@ -108,6 +108,10 @@
     )
 
 
+def all_lists(send_ref):
+    return jnp.concatenate(by_partner(*lists_of(send_ref)), axis=1)
+
+
 def pack_kernel(pos_hbm, spec_hbm, send_hbm, own_ref, o0, o1, o2, o3, pos_ref, spec_ref, send_ref, sems):
     copies = []
     for n, (given, kept) in enumerate(
@@ -122,8 +126,9 @@
     )
     own_ref[...] = own
     stacked = stacked3(own, 32)
-    for out, index in zip((o0, o1, o2, o3), by_partner(*lists_of(send_ref))):
-        out[...] = unstacked3(mm(stacked, one_hot(OWN, index)), 8)
+    picked = unstacked3(mm(stacked, one_hot(OWN, all_lists(send_ref))), 8)
+    for n, out in enumerate((o0, o1, o2, o3)):
+        out[...] = picked[:, n * OWN : (n + 1) * OWN]
 
 
 def halves(full):
@@ -269,8 +274,9 @@
     b_own = jnp.concatenate(sums + [flags], axis=0)
     b_ref[...] = b_own
     stacked = stacked3(b_own, OWN)
-    for out, index in zip((o0, o1, o2, o3), by_partner(*lists_of(send_ref))):
-        out[...] = unstacked3(mm(stacked, one_hot(OWN, index)), FEATS)
+    picked = unstacked3(mm(stacked, one_hot(OWN, all_lists(send_ref))), FEATS)
+    for n, out in enumerate((o0, o1, o2, o3)):
+        out[...] = picked[:, n * OWN : (n + 1) * OWN]
 
 
 def main_kernel(
@@ -393,7 +399,25 @@
         ref[...] = block
 
 
-def centre_kernel(c0, cx_ref, sum_ref, slope_ref, srct_ref, wback_ref, wr2b_ref, own_out, ctb_out):
+def centre_kernel(
+    c0,
+    cx_ref,
+    sum_ref,
+    slope_ref,
+    srct_ref,
+    wback_ref,
+    wr2b_ref,
+    spec_ref,
+    mass_ref,
+    own_out,
+    ctb_out,
+    step_out,
+):
+    spec = spec_ref[...]
+    scale = jnp.zeros(spec.shape, f32)
+    for sp in range(SPECIES):
+        scale = scale + jnp.where(spec == sp, mass_ref[sp], 0.0)
+    step_out[...] = time_step * scale
     total = jnp.zeros((OWN, 128), f32)
     for m in range(MEMBERS):
         hi, lo = split2(mm_nt(tripled(sum_ref[m]), srct_ref[m]) * slope_ref[m])
@@ -408,13 +432,9 @@
 
 
 def collected(pieces, send_ref, rows):
-    total = None
-    for piece, index in zip(pieces, by_partner(*lists_of(send_ref))):
-        got = unstacked3(
-            mm_nt(stacked3(piece[...], -(-3 * rows // 16) * 16), one_hot(OWN, index)), rows
-        )
-        total = got if total is None else total + got
-    return total
+    wide = jnp.concatenate([piece[...] for piece in pieces], axis=1)
+    stacked = stacked3(wide, -(-3 * rows // 16) * 16)
+    return unstacked3(mm_nt(stacked, one_hot(OWN, all_lists(send_ref))), rows)
 
 
 def push_kernel(own_ct, r0, r1, r2, r3, send_ref, basis_ref, geo_ref, live_ref, ctb_ref, a_ref, own_out, o0, o1, o2, o3):
@@ -444,13 +464,9 @@
         out[...] = block
 
 
-def finish_kernel(own_ct, r0, r1, r2, r3, send_ref, pos_ref, vel_ref, spec_ref, mass_ref, pos_out, vel_out):
+def finish_kernel(own_ct, r0, r1, r2, r3, send_ref, pos_ref, vel_ref, step_ref, pos_out, vel_out):
     ct = own_ct[...] + collected((r0, r1, r2, r3), send_ref, 8)
-    spec = spec_ref[...]
-    scale = jnp.zeros(spec.shape, f32)
-    for sp in range(SPECIES):
-        scale = scale + jnp.where(spec == sp, mass_ref[sp], 0.0)
-    vel = vel_ref[...] - time_step * scale * ct[0:3]
+    vel = vel_ref[...] - step_ref[...] * ct[0:3]
     vel_out[...] = vel
     pos_out[...] = pos_ref[...] + time_step * vel
 
@@ -542,9 +558,9 @@
 def run_centre(*given):
     return pl.pallas_call(
         centre_kernel,
-        out_shape=[like(32, OWN), like(8, EDGES)],
-        in_specs=vmem(7),
-        out_specs=vmem(2),
+        out_shape=[like(32, OWN), like(8, EDGES), like(1, OWN)],
+        in_specs=vmem(8) + [pl.BlockSpec(memory_space=pltpu.SMEM)],
+        out_specs=vmem(3),
         compiler_params=params(16),
         cost_estimate=pl.CostEstimate(flops=3_000_000_000, bytes_accessed=16_000_000, transcendentals=0),
         name="centre",
@@ -600,7 +616,9 @@
     )
     *cts, cx, sums = run_members(*b_ghosts, a, alive, xb, bs, centre, *maps, wback)
     back = exchanged(cts[1:])
-    own_sums, ctb = run_centre(cts[0], cx, sums, slope, srct, wback, wr2b)
+    own_sums, ctb, step = run_centre(
+        cts[0], cx, sums, slope, srct, wback, wr2b, spec, inv_mass
+    )
     own_ct, *outgoing = pl.pallas_call(
         push_kernel,
         out_shape=[like(8, OWN)] * 5,
@@ -613,11 +631,11 @@
     new_positions, new_velocities = pl.pallas_call(
         finish_kernel,
         out_shape=[like(3, OWN), like(3, OWN)],
-        in_specs=vmem(9) + [pl.BlockSpec(memory_space=pltpu.SMEM)],
+        in_specs=vmem(9),
         out_specs=vmem(2),
         compiler_params=params(4),
         name="finish",
-    )(own_ct, *last, send_lists, positions, velocities, spec, inv_mass)
+    )(own_ct, *last, send_lists, positions, velocities, step)
     return (new_positions, new_velocities)
 
 

time: 66.2 us -> 65.5 us (0.989)
  transfers between devices with their start and end apart: 16 -> 16, of which waited for: 5 -> 5; matrix products, arithmetic and copies ran while one was open for 0% -> 0% of each run, Pallas kernels for 12% -> 13%
where the time goes in v4:
time: 65.5 us; the launch traced here: 64.3 us
  Pallas kernels  28.5 us (44%)
  starting transfers between devices  24.7 us (38%)
  waiting for transfers between devices  8.75 us (13%)
  local copies, waits for them, and re-layouts  1.43 us (2%)
  between operations  0.86 us (1%)
    ppermute x16, starting transfers between devices, swapped(): return lax.ppermute(shard, axis, pairs)  24.7 us
    pallas_call x1, Pallas kernels, run_members(): pl.pallas_call(main_kernel, out_shape=[like(32, OWN)] * 5 + [like16(EDGES...  16.6 us
    ppermute x16, waiting for transfers between devices, swapped(): return lax.ppermute(shard, axis, pairs)  8.75 us
    pallas_call x1, Pallas kernels, run_weights(): pl.pallas_call(weights_kernel, out_shape=[like16(OWN, 128), like16(EDGES,...  3.69 us
    pallas_call x1, Pallas kernels, run_centre(): pl.pallas_call(centre_kernel, out_shape=[like(32, OWN), like(8, EDGES), l...  3.23 us
    pallas_call x1, Pallas kernels, shards(): pl.pallas_call(pack_kernel, out_shape=[like(8, OWN)] * 5, in_specs=[pl.Bl...  1.56 us
    unnamed x34, local copies, waits for them, and re-layouts  1.43 us
    pallas_call x1, Pallas kernels, run_picks(): pl.pallas_call(picks_kernel, out_shape=[like16(EDGES, EXT), like16(EXT, E...  1.32 us
  transfers between devices with their start and end apart: 16, of which 5 were waited for; matrix products, arithmetic and copies ran while one was open for 0% of the time, Pallas kernels for 13%

profile of v4, /device:TPU:0, one launch (start us, length us, event | category | flops | bytes accessed | tf_op | source)
XLA Modules:
  0.0 64.3 jit_solution(4026429190132404335)
XLA Ops:
  0.6 1.6 %pack.1 = (f32[8,128]{1,0:T(8,128)}, f32[8,128]{1,0:T(8,128)}, f32[8,128]{1,0:T(8,128)}, f32[8,128]{1,0:T(8,128)}, f32[8,128]{1,0:T(8,128)}) custom-call(f32[3,128]{1,0:T(4,128)} %pos_ref.1, s32[1,128]{1,0:T(1,128)} %bitcast.2, s32[4,64]{1,0:T(4,128)} %send_ref.5), custom_call_target="tpu_custom_call" | custom-call | tf_op jit(solution)/shard_map/pack/pallas_call | solution.py:589
  2.2 9.0 %collective-permute-start = (f32[8,128]{1,0:T(8,128)}, f32[8,128]{1,0:T(8,128)S(1)}, u32[]{:S(2)}, u32[]{:S(2)}) collective-permute-start(f32[8,128]{1,0:T(8,128)} %get-tuple-element.46), channel_id=1, source_target_pairs={{4,8},{8,4},{12,16},{16,12},{20,24},{24,20},{28,32},{32,28},{36,40... | collective-permute-start | bytes 12296 | tf_op jit(solution)/shard_map/ppermute | solution.py:479
  11.2 0.0 collective-permute-start.1
  11.2 0.0 collective-permute-start.2
  11.2 0.8 %collective-permute-start.3 = (f32[8,128]{1,0:T(8,128)}, f32[8,128]{1,0:T(8,128)S(1)}, u32[]{:S(2)}, u32[]{:S(2)}) collective-permute-start(f32[8,128]{1,0:T(8,128)} %get-tuple-element.49), channel_id=1, source_target_pairs={{0,1},{1,0},{2,3},{3,2},{4,5},{5,4},{6,7},{7,6},{8,9},{9,8},{10,11... | collective-permute-start | bytes 12296 | tf_op jit(solution)/shard_map/ppermute | solution.py:479
  12.0 0.7 %copy-done.13 = s32[12,128]{1,0:T(8,128)S(1)} copy-done((s32[12,128]{1,0:T(8,128)S(1)}, s32[12,128]{1,0:T(8,128)}, u32[]{:S(2)}) %copy-start.13) | copy-done | bytes 6168
  12.7 0.7 %copy-done.15 = s32[128]{0:T(128)S(1)} copy-done((s32[128]{0:T(128)S(1)}, s32[128]{0:T(128)}, u32[]{:S(2)}) %copy-start.15) | copy-done | bytes 536
  13.4 0.0 copy-start.8
  13.4 1.3 %picks.1 = (bf16[1536,640]{1,0:T(8,128)(2,1)S(1)}, bf16[640,1536]{1,0:T(8,128)(2,1)S(1)}, f32[12,128]{1,0:T(8,128)S(1)}, f32[1536,128]{1,0:T(8,128)S(1)}) custom-call(s32[12,128]{1,0:T(8,128)S(1)} %copy-done.13, s32[1,128]{1,0:T(1,128)S(1)} %bitcast.4), custom_call_target="tpu_custom_call" | custom-call | flops 4000000000 | bytes 16000000 | tf_op jit(solution)/shard_map/picks/pallas_call | solution.py:500
  14.7 0.0 copy-start.5
  14.7 0.0 copy-start.9
  14.8 0.0 copy-start.10
  14.8 0.0 copy-start.11
  14.8 0.0 copy-start.12
  14.8 0.0 copy-start.14
  14.8 0.0 collective-permute-done.g0
  14.8 1.7 %collective-permute-done.1.g1 = f32[8,128]{1,0:T(8,128)S(1)} collective-permute-done((f32[8,128]{1,0:T(8,128)}, f32[8,128]{1,0:T(8,128)S(1)}, u32[]{:S(2)}, u32[]{:S(2)}) %collective-permute-start.1) | collective-permute-done | bytes 4128 | tf_op jit(solution)/shard_map/ppermute | solution.py:479
  16.6 0.0 collective-permute-done.2.g2
  16.6 0.0 collective-permute-done.3.g3
  16.6 0.0 copy-done
  16.6 0.0 copy-done.2
  16.6 0.6 geometry.1
  17.2 4.3 %collective-permute-start.4 = (f32[40,128]{1,0:T(8,128)S(1)}, f32[40,128]{1,0:T(8,128)S(1)}, u32[]{:S(2)}, u32[]{:S(2)}) collective-permute-start(f32[40,128]{1,0:T(8,128)S(1)} %get-tuple-element.52), channel_id=1, source_target_pairs={{4,8},{8,4},{12,16},{16,12},{20,24},{24,20},{28,32},{32,28},{36,40... | collective-permute-start | bytes 61448 | tf_op jit(solution)/shard_map/ppermute | solution.py:479
  21.5 0.0 collective-permute-start.5
  21.5 0.0 collective-permute-start.6
  21.5 0.8 %collective-permute-start.7 = (f32[40,128]{1,0:T(8,128)S(1)}, f32[40,128]{1,0:T(8,128)S(1)}, u32[]{:S(2)}, u32[]{:S(2)}) collective-permute-start(f32[40,128]{1,0:T(8,128)S(1)} %get-tuple-element.55), channel_id=1, source_target_pairs={{0,1},{1,0},{2,3},{3,2},{4,5},{5,4},{6,7},{7,6},{8,9},{9,8},{10,11... | collective-permute-start | bytes 61448 | tf_op jit(solution)/shard_map/ppermute | solution.py:479
  22.3 0.0 copy-done.6
  22.3 0.0 copy-done.7
  22.3 0.0 copy-done.8
  22.3 0.0 copy-done.5
  22.3 0.0 copy-done.9
  22.4 0.0 copy-done.10
  22.4 0.0 copy-done.11
  22.4 0.0 copy-done.12
  22.4 0.0 copy-done.14
  22.4 3.7 %weights.1 = (bf16[128,128]{1,0:T(8,128)(2,1)S(1)}, bf16[1536,128]{1,0:T(8,128)(2,1)S(1)}, f32[4,128,256]{2,1,0:T(8,128)S(1)}, f32[4,128,256]{2,1,0:T(8,128)S(1)...) custom-call(f32[40,128]{1,0:T(8,128)S(1)} %get-tuple-element.58.b_re, ...), custom_call_target="tpu_custom_call" | custom-call | flops 4000000000 | bytes 16000000 | tf_op jit(solution)/shard_map/weights/pallas_call | solution.py:517
  26.1 0.7 %collective-permute-done.4.b1 = f32[40,128]{1,0:T(8,128)S(1)} collective-permute-done((f32[40,128]{1,0:T(8,128)S(1)}, f32[40,128]{1,0:T(8,128)S(1)}, u32[]{:S(2)}, u32[]{:S(2)}) %collective-permute-start.4) | collective-permute-done | bytes 20512 | tf_op jit(solution)/shard_map/ppermute | solution.py:479
  26.8 0.2 collective-permute-done.5.b2
  27.0 0.0 collective-permute-done.6.b3
  27.0 0.0 collective-permute-done.7.b4
  27.0 0.0 copy-start.16
  27.1 16.6 %members.1 = (f32[32,128]{1,0:T(8,128)S(1)}, f32[32,128]{1,0:T(8,128)S(1)}, f32[32,128]{1,0:T(8,128)S(1)}, f32[32,128]{1,0:T(8,128)S(1)}, f32[32,128]{1,0:T(8,12...) custom-call(f32[40,128]{1,0:T(8,128)S(1)} %collective-permute-done.4.b1, ...), custom_call_target="tpu_custom_call" | custom-call | tf_op jit(solution)/shard_map/members/pallas_call | solution.py:542
  43.6 4.1 %collective-permute-start.8 = (f32[32,128]{1,0:T(8,128)S(1)}, f32[32,128]{1,0:T(8,128)S(1)}, u32[]{:S(2)}, u32[]{:S(2)}) collective-permute-start(f32[32,128]{1,0:T(8,128)S(1)} %get-tuple-element.76), channel_id=1, source_target_pairs={{4,8},{8,4},{12,16},{16,12},{20,24},{24,20},{28,32},{32,28},{36,40... | collective-permute-start | bytes 49160 | tf_op jit(solution)/shard_map/ppermute | solution.py:479
  47.7 0.0 collective-permute-start.9
  47.7 0.0 collective-permute-start.10
  47.7 0.8 %collective-permute-start.11 = (f32[32,128]{1,0:T(8,128)S(1)}, f32[32,128]{1,0:T(8,128)S(1)}, u32[]{:S(2)}, u32[]{:S(2)}) collective-permute-start(f32[32,128]{1,0:T(8,128)S(1)} %get-tuple-element.79), channel_id=1, source_target_pairs={{0,1},{1,0},{2,3},{3,2},{4,5},{5,4},{6,7},{7,6},{8,9},{9,8},{10,11... | collective-permute-start | bytes 49160 | tf_op jit(solution)/shard_map/ppermute | solution.py:479
  48.5 0.0 copy-done.4
  48.5 0.0 copy-done.16
  48.5 3.2 %centre.1 = (f32[32,128]{1,0:T(8,128)S(1)}, f32[8,1536]{1,0:T(8,128)S(1)}, f32[1,128]{1,0:T(1,128)S(1)}) custom-call(f32[32,128]{1,0:T(8,128)S(1)} %get-tuple-element.69.c0, bf16[1536,2048]{1,0:T(8,128)(2,1)S(1)} %get-tuple-element.70.cx_ref, f32[4,128,256]{2,1,0:T(8,128)S(1)} %get-tuple-element.71.sum_ref, f32[4,128,256]{2,1,0:T(8,128)S(1)} %get-tuple-element.72.slope_ref, ...), custom_call_target="tpu_custom_call" | custom-call | flops 3000000000 | bytes 16000000 | tf_op jit(solution)/shard_map/centre/pallas_call | solution.py:559
  51.8 1.5 %collective-permute-done.8.r0 = f32[32,128]{1,0:T(8,128)S(1)} collective-permute-done((f32[32,128]{1,0:T(8,128)S(1)}, f32[32,128]{1,0:T(8,128)S(1)}, u32[]{:S(2)}, u32[]{:S(2)}) %collective-permute-start.8) | collective-permute-done | bytes 16416 | tf_op jit(solution)/shard_map/ppermute | solution.py:479
  53.3 0.0 collective-permute-done.9.r1
  53.3 0.0 collective-permute-done.10.r2
  53.3 0.0 collective-permute-done.11.r3
  53.3 0.7 %push.1 = (f32[8,128]{1,0:T(8,128)S(1)}, f32[8,128]{1,0:T(8,128)S(1)}, f32[8,128]{1,0:T(8,128)S(1)}, f32[8,128]{1,0:T(8,128)S(1)}, f32[8,128]{1,0:T(8,128)S(1)}) custom-call(f32[32,128]{1,0:T(8,128)S(1)} %get-tuple-element.75.own_ct, f32[32,128]{1,0:T(8,128)S(1)} %collective-permute-done.8.r0, f32[32,128]{1,0:T(8,128)S(1)} %collective-permute-done.9.r1, ...), custom_call_target="tpu_custom_call" | custom-call | tf_op jit(solution)/shard_map/push/pallas_call | solution.py:622
  54.0 4.0 %collective-permute-start.12 = (f32[8,128]{1,0:T(8,128)S(1)}, f32[8,128]{1,0:T(8,128)S(1)}, u32[]{:S(2)}, u32[]{:S(2)}) collective-permute-start(f32[8,128]{1,0:T(8,128)S(1)} %get-tuple-element.83), channel_id=1, source_target_pairs={{4,8},{8,4},{12,16},{16,12},{20,24},{24,20},{28,32},{32,28},{36,40... | collective-permute-start | bytes 12296 | tf_op jit(solution)/shard_map/ppermute | solution.py:479
  58.0 0.0 collective-permute-start.13
  58.0 0.0 collective-permute-start.14
  58.0 0.8 %collective-permute-start.15 = (f32[8,128]{1,0:T(8,128)S(1)}, f32[8,128]{1,0:T(8,128)S(1)}, u32[]{:S(2)}, u32[]{:S(2)}) collective-permute-start(f32[8,128]{1,0:T(8,128)S(1)} %get-tuple-element.86), channel_id=1, source_target_pairs={{0,1},{1,0},{2,3},{3,2},{4,5},{5,4},{6,7},{7,6},{8,9},{9,8},{10,11... | collective-permute-start | bytes 12296 | tf_op jit(solution)/shard_map/ppermute | solution.py:479
  58.9 4.6 %collective-permute-done.12.r0 = f32[8,128]{1,0:T(8,128)S(1)} collective-permute-done((f32[8,128]{1,0:T(8,128)S(1)}, f32[8,128]{1,0:T(8,128)S(1)}, u32[]{:S(2)}, u32[]{:S(2)}) %collective-permute-start.12) | collective-permute-done | bytes 4128 | tf_op jit(solution)/shard_map/ppermute | solution.py:479
  63.4 0.0 collective-permute-done.13.r1
  63.4 0.0 collective-permute-done.14.r2
  63.4 0.0 collective-permute-done.15.r3
  63.4 0.0 copy-done.1
  63.4 0.8 %finish.1 = (f32[3,128]{1,0:T(4,128)}, f32[3,128]{1,0:T(4,128)}) custom-call(f32[8,128]{1,0:T(8,128)S(1)} %get-tuple-element.82.own_ct, f32[8,128]{1,0:T(8,128)S(1)} %collective-permute-done.12.r0, f32[8,128]{1,0:T(8,128)S(1)} %collective-permute-done.13.r1, f32[8,128]{1,0:T(8,128)S(1)} %collective-permute-done.14.r2, ...), custom_call_target="tpu_custom_call" | custom-call | tf_op jit(solution)/shard_map/finish/pallas_call | solution.py:631
  (10 shorter events, 0.0 us)
Async XLA Ops:
  2.2 12.6 %collective-permute-start = (f32[8,128]{1,0:T(8,128)}, f32[8,128]{1,0:T(8,128)S(1)}, u32[]{:S(2)}, u32[]{:S(2)}) collective-permute-start(f32[8,128]{1,0:T(8,128)} %get-tuple-element.46), channel_id=1, source_target_pairs={{4,8},{8,4},{12,16},{16,12},{20,24},{24,20},{28,32},{32,28},{36,40... | collective-permute-start | bytes 12296 | tf_op jit(solution)/shard_map/ppermute | solution.py:479
  11.2 5.3 %collective-permute-start.1 = (f32[8,128]{1,0:T(8,128)}, f32[8,128]{1,0:T(8,128)S(1)}, u32[]{:S(2)}, u32[]{:S(2)}) collective-permute-start(f32[8,128]{1,0:T(8,128)} %get-tuple-element.47), channel_id=1, source_target_pairs={{0,4},{4,0},{8,12},{12,8},{16,20},{20,16},{24,28},{28,24},{32,36},... | collective-permute-start | bytes 12296 | tf_op jit(solution)/shard_map/ppermute | solution.py:479
  11.2 5.3 %collective-permute-start.2 = (f32[8,128]{1,0:T(8,128)}, f32[8,128]{1,0:T(8,128)S(1)}, u32[]{:S(2)}, u32[]{:S(2)}) collective-permute-start(f32[8,128]{1,0:T(8,128)} %get-tuple-element.48), channel_id=1, source_target_pairs={{1,2},{2,1},{3,0},{0,3},{5,6},{6,5},{7,4},{4,7},{9,10},{10,9},{11,... | collective-permute-start | bytes 12296 | tf_op jit(solution)/shard_map/ppermute | solution.py:479
  11.2 5.3 %collective-permute-start.3 = (f32[8,128]{1,0:T(8,128)}, f32[8,128]{1,0:T(8,128)S(1)}, u32[]{:S(2)}, u32[]{:S(2)}) collective-permute-start(f32[8,128]{1,0:T(8,128)} %get-tuple-element.49), channel_id=1, source_target_pairs={{0,1},{1,0},{2,3},{3,2},{4,5},{5,4},{6,7},{7,6},{8,9},{9,8},{10,11... | collective-permute-start | bytes 12296 | tf_op jit(solution)/shard_map/ppermute | solution.py:479
  12.0 0.7 %copy-start.13 = (s32[12,128]{1,0:T(8,128)S(1)}, s32[12,128]{1,0:T(8,128)}, u32[]{:S(2)}) copy-start(s32[12,128]{1,0:T(8,128)} %nbr_ref.1) | copy-start | bytes 18436
  12.7 0.7 %copy-start.15 = (s32[128]{0:T(128)S(1)}, s32[128]{0:T(128)}, u32[]{:S(2)}) copy-start(s32[128]{0:T(128)} %param.19) | copy-start | bytes 1540
  13.4 3.2 %copy-start = (s32[4,64]{1,0:T(4,128)S(1)}, s32[4,64]{1,0:T(4,128)}, u32[]{:S(2)}) copy-start(s32[4,64]{1,0:T(4,128)} %send_ref.5) | copy-start | bytes 3076
  13.4 3.2 %copy-start.2 = (f32[8,128]{1,0:T(8,128)S(1)}, f32[8,128]{1,0:T(8,128)}, u32[]{:S(2)}) copy-start(f32[8,128]{1,0:T(8,128)} %get-tuple-element.45.own_ref) | copy-start | bytes 12292
  13.4 9.0 %copy-start.6 = (f32[4,256,256]{2,1,0:T(8,128)S(1)}, f32[4,256,256]{2,1,0:T(8,128)}, u32[]{:S(2)}) copy-start(f32[4,256,256]{2,1,0:T(8,128)} %wsrc_ref.1) | copy-start | bytes 3145732
  13.4 9.0 %copy-start.7 = (f32[4,256,256]{2,1,0:T(8,128)S(1)}, f32[4,256,256]{2,1,0:T(8,128)}, u32[]{:S(2)}) copy-start(f32[4,256,256]{2,1,0:T(8,128)} %wdst_ref.1) | copy-start | bytes 3145732
  13.4 9.0 %copy-start.8 = (f32[4,256,256]{2,1,0:T(8,128)S(1)}, f32[4,256,256]{2,1,0:T(8,128)}, u32[]{:S(2)}) copy-start(f32[4,256,256]{2,1,0:T(8,128)} %wedge_ref.1) | copy-start | bytes 3145732
  14.7 7.6 %copy-start.5 = (f32[4,256,256]{2,1,0:T(8,128)S(1)}, f32[4,256,256]{2,1,0:T(8,128)}, u32[]{:S(2)}) copy-start(f32[4,256,256]{2,1,0:T(8,128)} %wone_ref.1) | copy-start | bytes 3145732
  14.7 7.6 %copy-start.9 = (f32[4,8,256]{2,1,0:T(8,128)S(1)}, f32[4,8,256]{2,1,0:T(8,128)}, u32[]{:S(2)}) copy-start(f32[4,8,256]{2,1,0:T(8,128)} %wr1_ref.1) | copy-start | bytes 98308
  14.8 7.6 %copy-start.10 = (f32[4,8,256]{2,1,0:T(8,128)S(1)}, f32[4,8,256]{2,1,0:T(8,128)}, u32[]{:S(2)}) copy-start(f32[4,8,256]{2,1,0:T(8,128)} %wr2_ref.1) | copy-start | bytes 98308
  14.8 7.6 %copy-start.11 = (f32[4,4,256]{2,1,0:T(4,128)S(1)}, f32[4,4,256]{2,1,0:T(4,128)}, u32[]{:S(2)}) copy-start(f32[4,4,256]{2,1,0:T(4,128)} %nbr_emb_ref.1) | copy-start | bytes 49156
  14.8 7.6 %copy-start.12 = (f32[4,4,256]{2,1,0:T(4,128)S(1)}, f32[4,4,256]{2,1,0:T(4,128)}, u32[]{:S(2)}) copy-start(f32[4,4,256]{2,1,0:T(4,128)} %self_emb_ref.1) | copy-start | bytes 49156
  14.8 7.6 %copy-start.14 = (f32[4,256]{1,0:T(4,128)S(1)}, f32[4,256]{1,0:T(4,128)}, u32[]{:S(2)}) copy-start(f32[4,256]{1,0:T(4,128)} %wout_ref.1) | copy-start | bytes 12292
  17.2 9.6 %collective-permute-start.4 = (f32[40,128]{1,0:T(8,128)S(1)}, f32[40,128]{1,0:T(8,128)S(1)}, u32[]{:S(2)}, u32[]{:S(2)}) collective-permute-start(f32[40,128]{1,0:T(8,128)S(1)} %get-tuple-element.52), channel_id=1, source_target_pairs={{4,8},{8,4},{12,16},{16,12},{20,24},{24,20},{28,32},{32,28},{36,40... | collective-permute-start | bytes 61448 | tf_op jit(solution)/shard_map/ppermute | solution.py:479
  21.5 5.5 %collective-permute-start.5 = (f32[40,128]{1,0:T(8,128)S(1)}, f32[40,128]{1,0:T(8,128)S(1)}, u32[]{:S(2)}, u32[]{:S(2)}) collective-permute-start(f32[40,128]{1,0:T(8,128)S(1)} %get-tuple-element.53), channel_id=1, source_target_pairs={{0,4},{4,0},{8,12},{12,8},{16,20},{20,16},{24,28},{28,24},{32,36},... | collective-permute-start | bytes 61448 | tf_op jit(solution)/shard_map/ppermute | solution.py:479
  21.5 5.5 %collective-permute-start.6 = (f32[40,128]{1,0:T(8,128)S(1)}, f32[40,128]{1,0:T(8,128)S(1)}, u32[]{:S(2)}, u32[]{:S(2)}) collective-permute-start(f32[40,128]{1,0:T(8,128)S(1)} %get-tuple-element.54), channel_id=1, source_target_pairs={{1,2},{2,1},{3,0},{0,3},{5,6},{6,5},{7,4},{4,7},{9,10},{10,9},{11,... | collective-permute-start | bytes 61448 | tf_op jit(solution)/shard_map/ppermute | solution.py:479
  21.5 5.5 %collective-permute-start.7 = (f32[40,128]{1,0:T(8,128)S(1)}, f32[40,128]{1,0:T(8,128)S(1)}, u32[]{:S(2)}, u32[]{:S(2)}) collective-permute-start(f32[40,128]{1,0:T(8,128)S(1)} %get-tuple-element.55), channel_id=1, source_target_pairs={{0,1},{1,0},{2,3},{3,2},{4,5},{5,4},{6,7},{7,6},{8,9},{9,8},{10,11... | collective-permute-start | bytes 61448 | tf_op jit(solution)/shard_map/ppermute | solution.py:479
  27.0 21.5 %copy-start.4 = (s32[128]{0:T(128)S(1)}, s32[128]{0:T(128)}, u32[]{:S(2)}) copy-start(s32[128]{0:T(128)} %param.18) | copy-start | bytes 1540
  27.0 21.5 %copy-start.16 = (f32[4]{0:T(128)S(1)}, f32[4]{0:T(128)}, u32[]{:S(2)}) copy-start(f32[4]{0:T(128)} %mass_ref.1) | copy-start | bytes 52
  43.6 9.7 %collective-permute-start.8 = (f32[32,128]{1,0:T(8,128)S(1)}, f32[32,128]{1,0:T(8,128)S(1)}, u32[]{:S(2)}, u32[]{:S(2)}) collective-permute-start(f32[32,128]{1,0:T(8,128)S(1)} %get-tuple-element.76), channel_id=1, source_target_pairs={{4,8},{8,4},{12,16},{16,12},{20,24},{24,20},{28,32},{32,28},{36,40... | collective-permute-start | bytes 49160 | tf_op jit(solution)/shard_map/ppermute | solution.py:479
  47.7 5.5 %collective-permute-start.9 = (f32[32,128]{1,0:T(8,128)S(1)}, f32[32,128]{1,0:T(8,128)S(1)}, u32[]{:S(2)}, u32[]{:S(2)}) collective-permute-start(f32[32,128]{1,0:T(8,128)S(1)} %get-tuple-element.77), channel_id=1, source_target_pairs={{0,4},{4,0},{8,12},{12,8},{16,20},{20,16},{24,28},{28,24},{32,36},... | collective-permute-start | bytes 49160 | tf_op jit(solution)/shard_map/ppermute | solution.py:479
  47.7 5.5 %collective-permute-start.10 = (f32[32,128]{1,0:T(8,128)S(1)}, f32[32,128]{1,0:T(8,128)S(1)}, u32[]{:S(2)}, u32[]{:S(2)}) collective-permute-start(f32[32,128]{1,0:T(8,128)S(1)} %get-tuple-element.78), channel_id=1, source_target_pairs={{1,2},{2,1},{3,0},{0,3},{5,6},{6,5},{7,4},{4,7},{9,10},{10,9},{11,... | collective-permute-start | bytes 49160 | tf_op jit(solution)/shard_map/ppermute | solution.py:479
  47.7 5.5 %collective-permute-start.11 = (f32[32,128]{1,0:T(8,128)S(1)}, f32[32,128]{1,0:T(8,128)S(1)}, u32[]{:S(2)}, u32[]{:S(2)}) collective-permute-start(f32[32,128]{1,0:T(8,128)S(1)} %get-tuple-element.79), channel_id=1, source_target_pairs={{0,1},{1,0},{2,3},{3,2},{4,5},{5,4},{6,7},{7,6},{8,9},{9,8},{10,11... | collective-permute-start | bytes 49160 | tf_op jit(solution)/shard_map/ppermute | solution.py:479
  51.8 11.7 %copy-start.1 = (f32[3,128]{1,0:T(4,128)S(1)}, f32[3,128]{1,0:T(4,128)}, u32[]{:S(2)}) copy-start(f32[3,128]{1,0:T(4,128)} %pos_ref.1) | copy-start | bytes 4612
  51.8 11.7 %copy-start.3 = (f32[3,128]{1,0:T(4,128)S(1)}, f32[3,128]{1,0:T(4,128)}, u32[]{:S(2)}) copy-start(f32[3,128]{1,0:T(4,128)} %vel_ref.1) | copy-start | bytes 4612
  54.0 9.4 %collective-permute-start.12 = (f32[8,128]{1,0:T(8,128)S(1)}, f32[8,128]{1,0:T(8,128)S(1)}, u32[]{:S(2)}, u32[]{:S(2)}) collective-permute-start(f32[8,128]{1,0:T(8,128)S(1)} %get-tuple-element.83), channel_id=1, source_target_pairs={{4,8},{8,4},{12,16},{16,12},{20,24},{24,20},{28,32},{32,28},{36,40... | collective-permute-start | bytes 12296 | tf_op jit(solution)/shard_map/ppermute | solution.py:479
  58.0 5.4 %collective-permute-start.13 = (f32[8,128]{1,0:T(8,128)S(1)}, f32[8,128]{1,0:T(8,128)S(1)}, u32[]{:S(2)}, u32[]{:S(2)}) collective-permute-start(f32[8,128]{1,0:T(8,128)S(1)} %get-tuple-element.84), channel_id=1, source_target_pairs={{0,4},{4,0},{8,12},{12,8},{16,20},{20,16},{24,28},{28,24},{32,36},... | collective-permute-start | bytes 12296 | tf_op jit(solution)/shard_map/ppermute | solution.py:479
  58.0 5.4 %collective-permute-start.14 = (f32[8,128]{1,0:T(8,128)S(1)}, f32[8,128]{1,0:T(8,128)S(1)}, u32[]{:S(2)}, u32[]{:S(2)}) collective-permute-start(f32[8,128]{1,0:T(8,128)S(1)} %get-tuple-element.85), channel_id=1, source_target_pairs={{1,2},{2,1},{3,0},{0,3},{5,6},{6,5},{7,4},{4,7},{9,10},{10,9},{11,... | collective-permute-start | bytes 12296 | tf_op jit(solution)/shard_map/ppermute | solution.py:479
  58.0 5.4 %collective-permute-start.15 = (f32[8,128]{1,0:T(8,128)S(1)}, f32[8,128]{1,0:T(8,128)S(1)}, u32[]{:S(2)}, u32[]{:S(2)}) collective-permute-start(f32[8,128]{1,0:T(8,128)S(1)} %get-tuple-element.86), channel_id=1, source_target_pairs={{0,1},{1,0},{2,3},{3,2},{4,5},{5,4},{6,7},{7,6},{8,9},{9,8},{10,11... | collective-permute-start | bytes 12296 | tf_op jit(solution)/shard_map/ppermute | solution.py:479
